TPU v7x, 32 devices: a whole 2x2x4 slice. The times are simulated.
32 devices in a mesh: row: 4 (over y, x), col: 4 (over z), layer: 2 (over core).
Axes of the slice: x: 2, y: 2, z: 4, core: 2. Of those that a mesh axis runs over, the one named last changes fastest.
Arguments:
- similarity: bfloat16 [6144, 6144], P('row', ('col', 'layer')), may hold values from 0.049804688 to 1
- block_mask: int32 [48, 48], P('row', ('col', 'layer')), may hold values from 0 to 1, as said below
Outputs:
- normalized: float32 [6144, 6144], P('row', ('col', 'layer'))
Inputs may be any that keep to these rules, and one draw needn't show every extreme that they name: Entries are 0 or 1; every diagonal block is 1; each device's share of block_mask holds at most 18 ones, and some device's share holds exactly 18.
All inputs are finite; a program needn't handle non-finite values.
Results may differ from a plain program's by a relative error of at most 0.0003.
Values may be sent and summed in bfloat16 or wider, within the bound.
No kernel may reach another device: no remote copies, remote signals or barrier semaphores. Data moves between devices by JAX's collectives and lax.ppermute only.
A program may use at most 256 MiB of HBM per device.

v0:
```python
import jax
import jax.numpy as jnp
from jax import lax
from jax.sharding import PartitionSpec as P

BLK = 128


def body(similarity, block_mask):
    expanded = jnp.repeat(jnp.repeat(block_mask, BLK, 0), BLK, 1).astype(similarity.dtype)
    masked = similarity * expanded
    tile_rows, tile_cols = masked.shape
    full_tile = lax.all_gather(masked, "layer", axis=1, tiled=True)
    half_rows = tile_rows // lax.axis_size("layer")
    own_half = lax.dynamic_slice_in_dim(
        full_tile, lax.axis_index("layer") * half_rows, half_rows, 0
    )
    inner_panel = lax.all_gather(own_half, "row", axis=0, tiled=True)
    partial_value = jnp.dot(
        lax.all_gather(masked, "col", axis=1, tiled=True),
        inner_panel,
        preferred_element_type=jnp.float32,
    )
    product = lax.psum_scatter(partial_value, "layer", scatter_dimension=1, tiled=True)
    inflated = product * product
    totals = lax.psum(jnp.sum(inflated, axis=0), "row")
    scaling = tile_rows * lax.axis_size("row")
    return scaling * inflated / totals


def solution(mesh):
    return jax.shard_map(
        body,
        mesh=mesh,
        in_specs=(P("row", ("col", "layer")), P("row", ("col", "layer"))),
        out_specs=P("row", ("col", "layer")),
        check_vma=False,
    )
```

profile of v0, /device:TPU:0, one launch (start us, length us, event | category | flops | bytes accessed | tf_op | source)
XLA Modules:
  0.0 359.4 jit_solution(13780762947482760483)
XLA Ops:
  6.5 0.0 all-gather.6.cloned.1.call-start
  6.5 0.7 convert_element_type.11
  7.2 0.1 broadcast_bitcast_fusion
  7.3 2.8 copy.4
  10.2 1.6 bitcast_multiply_fusion
  11.7 0.0 all-gather.6.cloned.1.call-update
  11.8 0.0 all-gather.4.cloned.1.call-start
  11.8 0.7 all-gather.4.cloned.1.call-update
  12.5 0.0 all-gather.8.cloned.1.call-start
  12.6 16.5 %all-gather.6.cloned.1.call-done = bf16[1536,1536]{0,1:T(8,128)(2,1)} async-done(((bf16[1536,768]{0,1:T(8,128)(2,1)}), bf16[1536,1536]{0,1:T(8,128)(2,1)}) %all-gather.6.cloned.1.call-update) | async-done | bytes 4718608 | tf_op jit(solution)/shard_map/all_gather | solution.py:13
  29.1 3.2 constant_dynamic-slice_fusion
  32.3 0.0 all-gather.8.cloned.1.call-update
  32.3 0.0 reduce-scatter.2.cloned.1.call-start
  32.3 166.3 %all-gather.4.cloned.1.call-done = bf16[1536,3072]{0,1:T(8,128)(2,1)} async-done(((bf16[1536,768]{0,1:T(8,128)(2,1)}), bf16[1536,3072]{0,1:T(8,128)(2,1)}) %all-gather.4.cloned.1.call-update) | async-done | bytes 9437200 | tf_op jit(solution)/shard_map/all_gather | solution.py:20
  198.6 96.4 %all-gather.8.cloned.1.call-done = bf16[3072,1536]{0,1:T(8,128)(2,1)} async-done(((bf16[768,1536]{0,1:T(8,128)(2,1)}), bf16[3072,1536]{0,1:T(8,128)(2,1)}) %all-gather.8.cloned.1.call-update) | async-done | bytes 9437200 | tf_op jit(solution)/shard_map/all_gather | solution.py:18
  295.0 21.9 %fusion = f32[1536,1536]{1,0:T(8,128)} fusion(bf16[1536,3072]{0,1:T(8,128)(2,1)} %all-gather.4.cloned.1.call-done, bf16[3072,1536]{0,1:T(8,128)(2,1)} %all-gather.8.cloned.1.call-done), kind=kOutput, calls=%fused_computation.6 | convolution fusion | flops 14495514624 | bytes 28311552 | tf_op jit(solution)/shard_map/dot_general | solution.py:19
  316.9 0.0 reduce-scatter.2.cloned.1.call-update
  317.0 17.9 %reduce-scatter.2.cloned.1.call-done = f32[1536,768]{1,0:T(8,128)} async-done(((f32[1536,1536]{1,0:T(8,128)}), f32[1536,768]{1,0:T(8,128)}) %reduce-scatter.2.cloned.1.call-update) | async-done | bytes 4718608 | tf_op jit(solution)/shard_map/reduce_scatter | solution.py:24
  334.9 2.7 multiply_reduce_fusion
  337.6 10.2 %psum.7 = f32[768]{0:T(1024)S(1)} all-reduce(f32[768]{0:T(1024)S(1)} %multiply_reduce_fusion), channel_id=1, replica_groups=mesh['row'=4,'col'=4,'layer'=2] {'row'}, use_global_device_ids=true, to_apply=%region_2.0 | all-reduce | flops 768 | bytes 6144 | tf_op jit(solution)/shard_map/psum | solution.py:26
  347.9 5.0 %multiply_divide_fusion = f32[1536,768]{1,0:T(8,128)} fusion(f32[1536,768]{1,0:T(8,128)} %reduce-scatter.2.cloned.1.call-done, f32[768]{0:T(1024)S(1)} %psum.7), kind=kLoop, calls=%fused_computation | loop fusion | flops 3538944 | bytes 9440256 | tf_op jit(solution)/shard_map/div | solution.py:28
  (1 shorter events, 0.0 us)
Async XLA Ops:
  6.5 22.5 %all-gather.6.cloned.1.call-start = ((), (), s32[]{:S(2)}) async-start(), calls=%async_computation.2 | async-start | bytes 7077888 | tf_op jit(solution)/shard_map/all_gather | solution.py:13
  11.8 186.8 %all-gather.4.cloned.1.call-start = ((), (), s32[]{:S(2)}) async-start(), calls=%async_computation.1 | async-start | bytes 11796480 | tf_op jit(solution)/shard_map/all_gather | solution.py:20
  12.5 282.5 %all-gather.8.cloned.1.call-start = ((), (), s32[]{:S(2)}) async-start(), calls=%async_computation.3 | async-start | bytes 11796480 | tf_op jit(solution)/shard_map/all_gather | solution.py:18
  32.3 302.6 %reduce-scatter.2.cloned.1.call-start = ((), (), s32[]{:S(2)}) async-start(), calls=%async_computation.4 | async-start | bytes 14155776 | tf_op jit(solution)/shard_map/reduce_scatter | solution.py:24
Sparse Core Ops, SparseCore 0:
  11.9 17.1 all-gather.5
  30.6 167.9 all-gather.3
  200.5 94.5 all-gather.7
  317.1 17.7 reduce-scatter.1
where the time goes:
time: 360 us; the launch traced here: 359 us
  waiting for transfers between devices  298 us (83%)
  matrix products  21.9 us (6%)
  between operations  13.1 us (4%)
  blocking collectives  10.2 us (3%)
  other arithmetic  10 us (3%)
  local copies, waits for them, and re-layouts  6.14 us (2%)
    all_gather x1, waiting for transfers between devices, body(): lax.all_gather(masked, 'col', axis=1, tiled=True)  166 us
    all_gather x1, waiting for transfers between devices, body(): inner_panel = lax.all_gather(own_half, 'row', axis=0, tiled=True)  96.4 us
    dot_general x1, matrix products, body(): jnp.dot(lax.all_gather(masked, 'col', axis=1, tiled=True), inner_panel, p...  21.9 us
    reduce_scatter x1, waiting for transfers between devices, body(): lax.psum_scatter(partial_value, 'layer', scatter_dimension=1, tiled=True)  17.9 us
    all_gather x1, waiting for transfers between devices, body(): full_tile = lax.all_gather(masked, 'layer', axis=1, tiled=True)  16.5 us
    psum x1, blocking collectives, body(): totals = lax.psum(jnp.sum(inflated, axis=0), 'row')  10.2 us
  transfers between devices with their start and end apart: 4, of which 4 were waited for; matrix products, arithmetic and copies ran while one was open for 1% of the time, Pallas kernels for 0%

commit v1 on v0

v1 whole, which is shorter than its diff:
```python
import functools

import jax
import jax.numpy as jnp
from jax import lax
from jax.experimental import pallas as pl
from jax.experimental.pallas import tpu as pltpu
from jax.sharding import PartitionSpec as P

BLK = 128
SLOTS = 18
SHARE = SLOTS * BLK
HEAD = 16
ROWS = HEAD + SHARE
UNROLL = 4
MIB = 1024 * 1024

SMEM = pl.BlockSpec(memory_space=pltpu.SMEM)
VMEM = pl.BlockSpec(memory_space=pltpu.VMEM)
ANY = pl.BlockSpec(memory_space=pl.ANY)
SMALL = pl.CostEstimate(flops=10**8, bytes_accessed=10**6, transcendentals=0)


def compact_kernel(mask_ref, sim_ref, out_ref, places, sems):
    nb_cols, nb_rows = mask_ref.shape

    def block_copy(slot, i, k):
        return pltpu.make_async_copy(
            sim_ref.at[pl.ds(pl.multiple_of(i * BLK, BLK), BLK), pl.ds(k * BLK, BLK)],
            out_ref.at[pl.ds(pl.multiple_of(HEAD + slot * BLK, HEAD), BLK), :],
            sems.at[slot],
        )

    def scan(i, count):
        for k in range(nb_cols):
            here = mask_ref[k, i]

            @pl.when(here != 0)
            def _():
                block_copy(count, i, k).start()
                places[count] = i * 8 + k

            count = count + here
        return count

    for slot in range(SLOTS):
        places[slot] = 0
    count = lax.fori_loop(0, nb_rows, scan, jnp.int32(0))
    lane = lax.broadcasted_iota(jnp.int32, (HEAD, BLK), 1)
    header = jnp.where(lane == SLOTS, count, 0)
    for slot in range(SLOTS):
        header = jnp.where(lane == slot, places[slot], header)
    out_ref[0:HEAD, :] = header.astype(jnp.float32).astype(out_ref.dtype)

    def wait(slot, carry):
        block_copy(slot, 0, 0).wait()
        return carry

    lax.fori_loop(0, count, wait, 0)


def compact(mask, similarity):
    return pl.pallas_call(
        compact_kernel,
        out_shape=jax.ShapeDtypeStruct((ROWS, BLK), similarity.dtype),
        in_specs=[SMEM, ANY],
        out_specs=VMEM,
        scratch_shapes=[pltpu.SMEM((SLOTS,), jnp.int32), pltpu.SemaphoreType.DMA((SLOTS,))],
        cost_estimate=pl.CostEstimate(flops=0, bytes_accessed=2 * SHARE * BLK * 2, transcendentals=0),
        name="compact",
    )(mask, similarity)


def multiply_pairs(todo, share, x_ref, y_blocks, acc, sums, x_base=0):
    def multiply(step, carry):
        terms = []
        for u in range(UNROLL):
            packed = todo[share, 1 + step * UNROLL + u]
            x = x_base + HEAD + lax.shift_right_logical(packed, 22) * BLK
            y = jnp.bitwise_and(lax.shift_right_logical(packed, 7), 4095) * HEAD
            x_block = x_ref[pl.ds(pl.multiple_of(x, HEAD), BLK), :]
            y_block = y_blocks[pl.ds(pl.multiple_of(y, HEAD), BLK), :]
            terms.append((packed, jnp.dot(x_block, y_block, preferred_element_type=jnp.float32)))
        for packed, term in terms:
            at = jnp.bitwise_and(packed, 127)
            j = jnp.bitwise_and(lax.shift_right_logical(packed, 19), 7)
            old = acc[at]
            new = old + term
            acc[at] = new
            sums[j] += jnp.sum((term * (old + new)).reshape(BLK // 8, 8, BLK), axis=0)
        return carry

    n_steps = lax.shift_right_logical(todo[share, 0] + UNROLL - 1, UNROLL.bit_length() - 1)
    lax.fori_loop(0, n_steps, multiply, 0)


def list_pairs(todo, share, places, at, n_slots, first_inner, slots_of, n_of, nb_rows, nb_cols):
    def slot_pairs(slot, count):
        place = places[at, slot]
        k = first_inner + jnp.bitwise_and(place, 7)
        packed = (slot << 22) + lax.shift_right_logical(place, 3) * nb_cols

        def pair(n, count):
            todo[share, 1 + count] = packed + slots_of[k * 8 + n]
            return count + 1

        return lax.fori_loop(0, n_of[k], pair, count)

    count = lax.fori_loop(0, n_slots, slot_pairs, jnp.int32(0))
    for u in range(UNROLL):
        todo[share, 1 + count + u] = (nb_cols << 19) + nb_rows * nb_cols
    todo[share, 0] = count


def clear_blocks(ref):
    def clear(at, carry):
        ref[at] = jnp.zeros(ref.shape[1:], ref.dtype)
        return carry

    lax.fori_loop(0, ref.shape[0], clear, 0)


def read_headers(headers, heads, places, sem):
    for at, header in enumerate(headers):
        heads[at : at + 1, :] = header.astype(jnp.float32)[0:1, :].astype(jnp.int32)
    copy = pltpu.make_async_copy(heads, places, sem)
    copy.start()
    return copy


def inner_of(n_col, nb_rows, nb_cols, tile, layer):
    valid = jnp.logical_and(tile >= 0, tile < n_col)
    return valid, jnp.where(valid, tile, 0) * nb_rows + layer * nb_cols


def tile_rows(y_blocks, tile, rows=ROWS):
    return y_blocks.at[pl.ds(pl.multiple_of(tile * ROWS, HEAD), rows), :]


def column_headers(y_blocks, r, n_row):
    return [tile_rows(y_blocks, jnp.bitwise_xor(r, m), HEAD)[...] for m in range(n_row)]


def list_column(slots_of, n_of, places, sources, r, nb_rows):
    def no_slots(k, carry):
        n_of[k] = 0
        return carry

    lax.fori_loop(0, n_of.shape[0], no_slots, 0)
    for at, m in sources:
        tile = jnp.bitwise_xor(r, m)
        first = tile * (ROWS // HEAD) + 1

        def put(slot, carry):
            place = places[at, slot]
            k = tile * nb_rows + lax.shift_right_logical(place, 3)
            n = n_of[k]
            j = jnp.bitwise_and(place, 7)
            slots_of[k * 8 + n] = (j << 19) + ((first + slot * (BLK // HEAD)) << 7) + j
            n_of[k] = n + 1
            return carry

        lax.fori_loop(0, places[at, SLOTS], put, 0)


def chain_tile(c, step, odd):
    forward = 1 - 2 * jnp.bitwise_and(c, 1)
    return c - step * forward if odd else c + step * forward


def first_kernel(near, n_col, nb_rows, nb_cols, place_ref, *refs):
    y_refs, refs = refs[: len(near)], refs[len(near) :]
    x_refs, refs = refs[:3], refs[3:]
    acc, sums, y_blocks, slots_of, n_of, heads, places, todo, y_sems, smem_sem = refs
    r, c, l = place_ref[0], place_ref[1], place_ref[2]
    copies = []
    for at, (m, y_ref) in enumerate(zip(near, y_refs)):
        copies.append(pltpu.make_async_copy(y_ref, tile_rows(y_blocks, jnp.bitwise_xor(r, m)), y_sems.at[at]))
        copies[-1].start()
    clear_blocks(acc)
    clear_blocks(sums)
    for copy in copies:
        copy.wait()
    headers = [tile_rows(y_blocks, jnp.bitwise_xor(r, m), HEAD)[...] for m in near]
    read_headers(headers + [ref[0:HEAD, :] for ref in x_refs], heads, places, smem_sem).wait()
    list_column(slots_of, n_of, places, list(enumerate(near)), r, nb_rows)
    shares = [(c, l, 0, y_blocks, r * ROWS), (c, 1 - l, len(near), x_refs[0], 0)]
    shares.append((chain_tile(c, 1, True), l, len(near) + 1, x_refs[1], 0))
    shares.append((chain_tile(c, 1, False), l, len(near) + 2, x_refs[2], 0))
    for tile, layer, at, x_ref, x_base in shares:
        valid, first_inner = inner_of(n_col, nb_rows, nb_cols, tile, layer)
        n_slots = jnp.where(valid, places[at, SLOTS], 0)
        list_pairs(todo, 0, places, at, n_slots, first_inner, slots_of, n_of, nb_rows, nb_cols)
        multiply_pairs(todo, 0, x_ref, y_blocks, acc, sums, x_base)


def list_scratch(n_row, nb_rows, nb_cols, shares):
    return [
        pltpu.SMEM((n_row * nb_rows * 8,), jnp.int32),
        pltpu.SMEM((n_row * nb_rows,), jnp.int32),
        pltpu.VMEM((shares, BLK), jnp.int32),
        pltpu.SMEM((shares, BLK), jnp.int32),
        pltpu.SMEM((1, SLOTS * nb_cols + 1 + UNROLL), jnp.int32),
    ]


def multiply_first(place, near, ys, xs, n_row, n_col, nb_rows, nb_cols):
    shares = len(near) + len(xs)
    return pl.pallas_call(
        functools.partial(first_kernel, near, n_col, nb_rows, nb_cols),
        out_shape=[
            jax.ShapeDtypeStruct((nb_rows * nb_cols + 1, BLK, BLK), jnp.float32),
            jax.ShapeDtypeStruct((nb_cols + 1, 8, BLK), jnp.float32),
            jax.ShapeDtypeStruct((n_row * ROWS, BLK), jnp.bfloat16),
        ],
        in_specs=[SMEM] + [ANY] * len(near) + [VMEM] * len(xs),
        out_specs=[VMEM] * 3,
        scratch_shapes=list_scratch(n_row, nb_rows, nb_cols, shares)
        + [pltpu.SemaphoreType.DMA((len(near),)), pltpu.SemaphoreType.DMA],
        compiler_params=pltpu.CompilerParams(vmem_limit_bytes=24 * MIB),
        cost_estimate=SMALL,
        name="multiply_first",
    )(place, *[ys[m] for m in near], *xs)


def second_kernel(near, n_row, n_col, nb_rows, nb_cols, x_kinds, place_ref, *refs):
    distant = [m for m in range(n_row) if m not in near]
    y_refs, refs = refs[: len(distant)], refs[len(distant) :]
    x_refs, refs = refs[: len(x_kinds)], refs[len(x_kinds) :]
    acc, sums, y_blocks, slots_of, n_of, heads, places, todo, y_sems, smem_sem = refs[3:]
    r, c, l = place_ref[0], place_ref[1], place_ref[2]
    copies = []
    for at, (m, y_ref) in enumerate(zip(distant, y_refs)):
        copies.append(pltpu.make_async_copy(y_ref, tile_rows(y_blocks, jnp.bitwise_xor(r, m)), y_sems.at[at]))
        copies[-1].start()
    for copy in copies:
        copy.wait()
    headers = column_headers(y_blocks, r, n_row) + [ref[0:HEAD, :] for ref in x_refs]
    read_headers(headers, heads, places, smem_sem).wait()
    list_column(slots_of, n_of, places, [(m, m) for m in range(n_row)], r, nb_rows)
    shares = [((0, False, False, True), 0, y_blocks, r * ROWS)]
    shares += [(kind, n_row + at, x_ref, 0) for at, (kind, x_ref) in enumerate(zip(x_kinds, x_refs))]
    for (step, odd, other, rest), at, x_ref, x_base in shares:
        tile = chain_tile(c, step, odd)
        valid, first_inner = inner_of(n_col, nb_rows, nb_cols, tile, 1 - l if other else l)
        if rest:
            for m in near:
                valid = jnp.logical_and(valid, jnp.bitwise_xor(tile, r) != m)
        n_slots = jnp.where(valid, places[at, SLOTS], 0)
        list_pairs(todo, 0, places, at, n_slots, first_inner, slots_of, n_of, nb_rows, nb_cols)
        multiply_pairs(todo, 0, x_ref, y_blocks, acc, sums, x_base)


def multiply_second(place, near, ys, xs, x_kinds, acc, sums, y_blocks, n_col, nb_rows, nb_cols):
    n_row = len(ys)
    distant = [ys[m] for m in range(n_row) if m not in near]
    operands = [place, *distant, *xs, acc, sums, y_blocks]
    lists = list_scratch(n_row, nb_rows, nb_cols, n_row + len(xs))
    return pl.pallas_call(
        functools.partial(second_kernel, near, n_row, n_col, nb_rows, nb_cols, x_kinds),
        out_shape=[jax.ShapeDtypeStruct(x.shape, x.dtype) for x in (acc, sums, y_blocks)]
        + [jax.ShapeDtypeStruct(x.shape, x.dtype) for x in lists[:2]],
        in_specs=[SMEM] + [ANY] * len(distant) + [VMEM] * (len(xs) + 3),
        out_specs=[VMEM] * 3 + [SMEM] * 2,
        input_output_aliases={len(operands) - 3 + at: at for at in range(3)},
        scratch_shapes=lists[2:] + [pltpu.SemaphoreType.DMA((len(distant),)), pltpu.SemaphoreType.DMA],
        compiler_params=pltpu.CompilerParams(vmem_limit_bytes=24 * MIB),
        cost_estimate=SMALL,
        name="multiply_second",
    )(*operands)


def late_kernel(n_col, nb_rows, nb_cols, x_kinds, is_last, place_ref, slots_of, n_of, y_blocks, *refs):
    x_refs, refs = refs[: len(x_kinds)], refs[len(x_kinds) :]
    _, before_sums, acc = refs[:3]
    sums, heads, places, todo, smem_sem = refs[-5:]
    c, l = place_ref[1], place_ref[2]
    to_smem = read_headers([ref[0:HEAD, :] for ref in x_refs], heads, places, smem_sem)
    for j in range(sums.shape[0]):
        sums[j] = before_sums[j]
    to_smem.wait()
    for at, (x_ref, (step, odd, other)) in enumerate(zip(x_refs, x_kinds)):
        valid, first_inner = inner_of(n_col, nb_rows, nb_cols, chain_tile(c, step, odd), 1 - l if other else l)
        n_slots = jnp.where(valid, places[at, SLOTS], 0)
        list_pairs(todo, 0, places, at, n_slots, first_inner, slots_of, n_of, nb_rows, nb_cols)
        multiply_pairs(todo, 0, x_ref, y_blocks, acc, sums)
    if is_last:
        totals = refs[3]
        for j in range(nb_cols):
            totals[:, j * BLK : (j + 1) * BLK] = jnp.sum(sums[j], axis=0, keepdims=True)


def multiply_late(place, slots_of, n_of, y_blocks, xs, x_kinds, acc, sums, is_last, n_col, nb_rows, nb_cols):
    totals = jax.ShapeDtypeStruct((1, nb_cols * BLK), jnp.float32)
    same_sums = jax.ShapeDtypeStruct(sums.shape, sums.dtype)
    operands = [place, slots_of, n_of, y_blocks, *xs, acc, sums]
    return pl.pallas_call(
        functools.partial(late_kernel, n_col, nb_rows, nb_cols, x_kinds, is_last),
        out_shape=[jax.ShapeDtypeStruct(acc.shape, acc.dtype), totals if is_last else same_sums],
        in_specs=[SMEM] * 3 + [VMEM] * (len(operands) - 3),
        out_specs=[VMEM, VMEM],
        input_output_aliases={len(operands) - 2: 0},
        scratch_shapes=([pltpu.VMEM(sums.shape, jnp.float32)] if is_last else [])
        + list_scratch(0, nb_rows, nb_cols, len(xs))[2:]
        + [pltpu.SemaphoreType.DMA],
        compiler_params=pltpu.CompilerParams(vmem_limit_bytes=24 * MIB),
        cost_estimate=SMALL,
        name="multiply_last" if is_last else "multiply_late",
    )(*operands)


def scale_kernel(scaling, nb_rows, nb_cols, *refs):
    product, sums = refs[0], refs[1:-3]
    out, scaled, sems = refs[-3:]
    total = sums[0][...]
    for other in sums[1:]:
        total = total + other[...]
    factor = scaling / total

    def out_copy(i):
        rows = pl.ds(pl.multiple_of(i * BLK, BLK), BLK)
        return pltpu.make_async_copy(scaled.at[rows, :], out.at[rows, :], sems.at[i])

    def square(i, carry):
        for j in range(nb_cols):
            value = product[i * nb_cols + j]
            scaled[pl.ds(pl.multiple_of(i * BLK, BLK), BLK), j * BLK : (j + 1) * BLK] = (
                value * value * factor[:, j * BLK : (j + 1) * BLK]
            )
        out_copy(i).start()
        return carry

    lax.fori_loop(0, nb_rows, square, 0)

    def wait(i, carry):
        out_copy(i).wait()
        return carry

    lax.fori_loop(0, nb_rows, wait, 0)


def scale(product, sums, scaling, nb_rows, nb_cols):
    shape = (nb_rows * BLK, nb_cols * BLK)
    return pl.pallas_call(
        functools.partial(scale_kernel, scaling, nb_rows, nb_cols),
        out_shape=jax.ShapeDtypeStruct(shape, jnp.float32),
        in_specs=[VMEM] * (1 + len(sums)),
        out_specs=ANY,
        scratch_shapes=[pltpu.VMEM(shape, jnp.float32), pltpu.SemaphoreType.DMA((nb_rows,))],
        compiler_params=pltpu.CompilerParams(vmem_limit_bytes=16 * MIB),
        cost_estimate=pl.CostEstimate(flops=10**7, bytes_accessed=10 * 10**6, transcendentals=0),
        name="scale",
    )(product, *sums)


def even_tile(i, step):
    return i + step if i % 2 == 0 else i - step


def odd_tile(i, step):
    return i - step if i % 2 == 0 else i + step


def body(n_row, n_col, similarity, block_mask):
    nb_rows, nb_cols = block_mask.shape
    r, c, l = lax.axis_index("row"), lax.axis_index("col"), lax.axis_index("layer")
    place = jnp.stack([r, c, l]).astype(jnp.int32)
    mask = block_mask.T

    def holders(tile, step):
        return [i for i in range(n_col) if 0 <= tile(i, step) < n_col]

    def hop(x, tile, step):
        return lax.ppermute(x, "col", [(tile(i, 1), i) for i in holders(tile, step)])

    def sibling(x, cols):
        pairs = [(2 * i + layer, 2 * i + 1 - layer) for i in cols for layer in range(2)]
        return lax.ppermute(x, ("col", "layer"), pairs)

    own = compact(mask, similarity)
    even = hop(own, even_tile, 1)
    odd = hop(own, odd_tile, 1)
    near = [m for m in range(n_row) if m.bit_count() <= 1]
    ys = [own] + [None] * (n_row - 1)
    for m in near[1:]:
        ys[m] = lax.ppermute(own, "row", [(s, s ^ m) for s in range(n_row)])
    for m in range(1, n_row):
        if ys[m] is None:
            bit = 1 << (m.bit_length() - 1)
            ys[m] = lax.ppermute(ys[m ^ bit], "row", [(s, s ^ bit) for s in range(n_row)])
    first_xs = [sibling(own, range(n_col)), odd, even]
    shares = list(zip([(0, False, True, True), (1, True, False, True), (1, False, False, True)], first_xs))
    acc, sums, y_blocks = multiply_first(place, near, ys, first_xs, n_row, n_col, nb_rows, nb_cols)
    for step in range(1, n_col - 2):
        shares.append(((step, True, True, False), sibling(odd, holders(odd_tile, step))))
        shares.append(((step, False, True, False), sibling(even, holders(even_tile, step))))
        odd, even = hop(even, odd_tile, step + 1), hop(odd, even_tile, step + 1)
        shares += [((step + 1, True, False, False), odd), ((step + 1, False, False, False), even)]
    odd, even, sums = lax.optimization_barrier((odd, even, sums))
    last = hop(odd, even_tile, n_col - 1)
    x_kinds, xs = zip(*shares)
    acc, sums, y_blocks, slots_of, n_of = multiply_second(
        place, near, ys, xs, x_kinds, acc, sums, y_blocks, n_col, nb_rows, nb_cols
    )
    last, sums = lax.optimization_barrier((last, sums))
    other = sibling(last, holders(even_tile, n_col - 1))
    kinds = [(n_col - 1, False, False), (n_col - 2, True, True), (n_col - 2, False, True)]
    xs = [last, sibling(odd, holders(odd_tile, n_col - 2)), sibling(even, holders(even_tile, n_col - 2))]
    sizes = n_col, nb_rows, nb_cols
    acc, sums = multiply_late(place, slots_of, n_of, y_blocks, xs, kinds, acc, sums, False, *sizes)
    kinds = [(n_col - 1, False, True)]
    product, sums = multiply_late(place, slots_of, n_of, y_blocks, [other], kinds, acc, sums, True, *sizes)
    all_sums = [sums]
    for m in range(1, n_row):
        all_sums.append(lax.ppermute(sums, "row", [(s, s ^ m) for s in range(n_row)]))
    return scale(product, all_sums, float(nb_rows * BLK * n_row), nb_rows, nb_cols)


def solution(mesh):
    n_row, n_col = mesh.shape["row"], mesh.shape["col"]
    return jax.shard_map(
        functools.partial(body, n_row, n_col),
        mesh=mesh,
        in_specs=(P("row", ("col", "layer")), P("row", ("col", "layer"))),
        out_specs=P("row", ("col", "layer")),
        check_vma=False,
    )
```

time: 360 us -> 70 us (0.19)
  waiting for transfers between devices: 298 us -> 26.6 us
  matrix products: 21.9 us -> 0 us
  Pallas kernels: 0 us -> 21.9 us
  starting transfers between devices: 0.12 us -> 20.4 us
  between operations: 13.1 us -> 0.18 us
  blocking collectives: 10.2 us -> 0 us
  other arithmetic: 10 us -> 0.08 us
  local copies, waits for them, and re-layouts: 6.14 us -> 1.07 us
    all_gather x3 -> x0, waiting for transfers between devices: 279 us -> none  [the longest x1 166 us: body(): lax.all_gather(masked, 'col', axis=1, tiled=True)]
    ppermute x0 -> x17, waiting for transfers between devices: none -> 26.6 us  [the longest x5 21.7 us: hop(): lax.ppermute(x, 'col', [(tile(i, 1), i) for i in holders(tile, step)])]
    dot_general x1 -> x0, matrix products: 21.9 us -> none  [body(): jnp.dot(lax.all_gather(masked, 'col', axis=1, tiled=True), inner_panel, p...]
    pallas_call x0 -> x6, Pallas kernels: none -> 21.9 us  [the longest x1 5.94 us: multiply_first(): pl.pallas_call(functools.partial(first_kernel, near, n_col, nb_rows, nb_c...]
    ppermute x0 -> x17, starting transfers between devices: none -> 20.4 us  [the longest x5 6.95 us: hop(): lax.ppermute(x, 'col', [(tile(i, 1), i) for i in holders(tile, step)])]
    reduce_scatter x1 -> x0, waiting for transfers between devices: 17.9 us -> none  [body(): lax.psum_scatter(partial_value, 'layer', scatter_dimension=1, tiled=True)]
    psum x1 -> x0, blocking collectives: 10.2 us -> none  [body(): totals = lax.psum(jnp.sum(inflated, axis=0), 'row')]
    div x1 -> x0, other arithmetic: 5 us -> none  [body(): return scaling * inflated / totals]
  transfers between devices with their start and end apart: 4 -> 17, of which waited for: 4 -> 7; matrix products, arithmetic and copies ran while one was open for 1% -> 0% of each run, Pallas kernels for 0% -> 21%
where the time goes in v1:
time: 70 us; the launch traced here: 70.2 us
  waiting for transfers between devices  26.6 us (38%)
  Pallas kernels  21.9 us (31%)
  starting transfers between devices  20.4 us (29%)
  local copies, waits for them, and re-layouts  1.07 us (2%)
    ppermute x5, waiting for transfers between devices, hop(): lax.ppermute(x, 'col', [(tile(i, 1), i) for i in holders(tile, step)])  21.7 us
    ppermute x5, starting transfers between devices, hop(): lax.ppermute(x, 'col', [(tile(i, 1), i) for i in holders(tile, step)])  6.95 us
    pallas_call x1, Pallas kernels, multiply_first(): pl.pallas_call(functools.partial(first_kernel, near, n_col, nb_rows, nb_c...  5.94 us
    pallas_call x1, Pallas kernels, multiply_second(): pl.pallas_call(functools.partial(second_kernel, near, n_row, n_col, nb_ro...  5.87 us
    ppermute x6, starting transfers between devices, sibling(): return lax.ppermute(x, ('col', 'layer'), pairs)  5.22 us
    pallas_call x2, Pallas kernels, multiply_late(): pl.pallas_call(functools.partial(late_kernel, n_col, nb_rows, nb_cols, x_...  4.87 us
    ppermute x3, starting transfers between devices, body(): lax.ppermute(sums, 'row', [(s, s ^ m) for s in range(n_row)])  4.53 us
    ppermute x2, starting transfers between devices, body(): ys[m] = lax.ppermute(own, 'row', [(s, s ^ m) for s in range(n_row)])  3.19 us
  transfers between devices with their start and end apart: 17, of which 7 were waited for; matrix products, arithmetic and copies ran while one was open for 0% of the time, Pallas kernels for 21%

profile of v1, /device:TPU:0, one launch (start us, length us, event | category | flops | bytes accessed | tf_op | source)
XLA Modules:
  0.0 70.2 jit_solution(13956887581232792285)
XLA Ops:
  0.0 2.9 %compact.1.refs_0_ = bf16[2320,128]{1,0:T(8,128)(2,1)} custom-call(s32[6,12]{1,0:T(8,128)} %bitcast.4, bf16[1536,768]{1,0:T(8,128)(2,1)} %sim_ref.1), custom_call_target="tpu_custom_call" | custom-call | bytes 1179648 | tf_op jit(solution)/shard_map/compact/pallas_call | solution.py:63
  2.9 3.0 %collective-permute-start.4 = (bf16[2320,128]{1,0:T(8,128)(2,1)}, bf16[2320,128]{1,0:T(8,128)(2,1)S(1)}, u32[]{:S(2)}, u32[]{:S(2)}) collective-permute-start(bf16[2320,128]{1,0:T(8,128)(2,1)} %compact.1.refs_0_), channel_id=1, source_target_pairs={{2,0},{0,2},{6,4},{4,6},{3,1},{1,3},{7,5},{5,7},{10,8},{8,10},{14,... | collective-permute-start | bytes 1781768 | tf_op jit(solution)/shard_map/ppermute | solution.py:374
  5.9 0.7 collective-permute-start.3
  6.6 1.6 %collective-permute-start.9 = (bf16[2320,128]{1,0:T(8,128)(2,1)}, bf16[2320,128]{1,0:T(8,128)(2,1)}, u32[]{:S(2)}, u32[]{:S(2)}) collective-permute-start(bf16[2320,128]{1,0:T(8,128)(2,1)} %compact.1.refs_0_), channel_id=1, source_target_pairs={{0,16},{8,24},{16,0},{24,8},{1,17},{9,25},{17,1},{25,9},{2,18},{10... | collective-permute-start | bytes 1781768 | tf_op jit(solution)/shard_map/ppermute | solution.py:386
  8.2 0.0 collective-permute-start.2
  8.2 1.6 %collective-permute-start = (bf16[2320,128]{1,0:T(8,128)(2,1)}, bf16[2320,128]{1,0:T(8,128)(2,1)}, u32[]{:S(2)}, u32[]{:S(2)}) collective-permute-start(bf16[2320,128]{1,0:T(8,128)(2,1)} %compact.1.refs_0_), channel_id=1, source_target_pairs={{0,8},{8,0},{16,24},{24,16},{1,9},{9,1},{17,25},{25,17},{2,10},{10... | collective-permute-start | bytes 1781768 | tf_op jit(solution)/shard_map/ppermute | solution.py:386
  9.8 9.8 %collective-permute-done.4.refs_5_.refs_3_ = bf16[2320,128]{1,0:T(8,128)(2,1)S(1)} collective-permute-done((bf16[2320,128]{1,0:T(8,128)(2,1)}, bf16[2320,128]{1,0:T(8,128)(2,1)S(1)}, u32[]{:S(2)}, u32[]{:S(2)}) %collective-permute-start.4) | collective-permute-done | bytes 593952 | tf_op jit(solution)/shard_map/ppermute | solution.py:374
  19.6 0.7 collective-permute-start.7
  20.3 0.0 collective-permute-done.3.refs_4_.refs_2_
  20.3 1.3 %collective-permute-start.8 = (bf16[2320,128]{1,0:T(8,128)(2,1)S(1)}, bf16[2320,128]{1,0:T(8,128)(2,1)S(1)}, u32[]{:S(2)}, u32[]{:S(2)}) collective-permute-start(bf16[2320,128]{1,0:T(8,128)(2,1)S(1)} %collective-permute-done.3.refs_4_.refs_2_), channel_id=1, source_target_pairs={{2,0},{4,6},{3,1},{5,7},{10,8},{12,14},{11,9},{13,15},{18,16},{20,... | collective-permute-start | bytes 1781768 | tf_op jit(solution)/shard_map/ppermute | solution.py:374
  21.6 0.1 pad_add_fusion.place_ref
  21.7 0.2 collective-permute-done.9.refs_2_
  21.9 0.0 collective-permute-start.6
  21.9 0.0 collective-permute-done.2.refs_3_.refs_1_
  22.0 0.7 collective-permute-start.5
  22.6 1.7 %collective-permute-done.refs_1_ = bf16[2320,128]{1,0:T(8,128)(2,1)} collective-permute-done((bf16[2320,128]{1,0:T(8,128)(2,1)}, bf16[2320,128]{1,0:T(8,128)(2,1)}, u32[]{:S(2)}, u32[]{:S(2)}) %collective-permute-start) | collective-permute-done | bytes 593952 | tf_op jit(solution)/shard_map/ppermute | solution.py:386
  24.3 0.5 collective-permute-start.1
  24.8 0.0 copy-start
  24.8 1.1 %copy-done = bf16[2320,128]{1,0:T(8,128)(2,1)S(1)} copy-done((bf16[2320,128]{1,0:T(8,128)(2,1)S(1)}, bf16[2320,128]{1,0:T(8,128)(2,1)}, u32[]{:S(2)}) %copy-start) | copy-done | bytes 593944
  25.9 5.9 %multiply_first.1 = (f32[73,128,128]{2,1,0:T(8,128)S(1)}, f32[7,8,128]{2,1,0:T(8,128)S(1)}, bf16[9280,128]{1,0:T(8,128)(2,1)S(1)}) custom-call(s32[3]{0:T(128)S(1)} %pad_add_fusion.place_ref, bf16[2320,128]{1,0:T(8,128)(2,1)S(1)} %copy-done, bf16[2320,128]{1,0:T(8,128)(2,1)} %collective-permute-done.refs_1_, ...), custom_call_target="tpu_custom_call" | custom-call | flops 100000000 | bytes 1000000 | tf_op jit(solution)/shard_map/multiply_first/pallas_call | solution.py:209
  31.9 0.0 collective-permute-done.7.refs_6_
  31.9 6.5 %collective-permute-done.8.refs_7_ = bf16[2320,128]{1,0:T(8,128)(2,1)S(1)} collective-permute-done((bf16[2320,128]{1,0:T(8,128)(2,1)S(1)}, bf16[2320,128]{1,0:T(8,128)(2,1)S(1)}, u32[]{:S(2)}, u32[]{:S(2)}) %collective-permute-start.8) | collective-permute-done | bytes 593952 | tf_op jit(solution)/shard_map/ppermute | solution.py:374
  38.3 1.3 %collective-permute-start.10 = (bf16[2320,128]{1,0:T(8,128)(2,1)S(1)}, bf16[2320,128]{1,0:T(8,128)(2,1)S(1)}, u32[]{:S(2)}, u32[]{:S(2)}) collective-permute-start(bf16[2320,128]{1,0:T(8,128)(2,1)S(1)} %collective-permute-done.7.refs_6_), channel_id=1, source_target_pairs={{2,0},{4,6},{3,1},{5,7},{10,8},{12,14},{11,9},{13,15},{18,16},{20,... | collective-permute-start | bytes 1781768 | tf_op jit(solution)/shard_map/ppermute | solution.py:374
  39.6 0.7 collective-permute-start.12
  40.3 0.0 collective-permute-done.6.refs_5_
  40.3 1.9 %collective-permute-start.13 = (bf16[2320,128]{1,0:T(8,128)(2,1)S(1)}, bf16[2320,128]{1,0:T(8,128)(2,1)S(1)}, u32[]{:S(2)}, u32[]{:S(2)}) collective-permute-start(bf16[2320,128]{1,0:T(8,128)(2,1)S(1)} %collective-permute-done.8.refs_7_), channel_id=1, source_target_pairs={{0,1},{1,0},{6,7},{7,6},{8,9},{9,8},{14,15},{15,14},{16,17},{17,16... | collective-permute-start | bytes 1781768 | tf_op jit(solution)/shard_map/ppermute | solution.py:378
  42.3 0.0 collective-permute-done.5.refs_4_
  42.3 0.0 collective-permute-done.1.refs_0_
  42.3 5.9 %multiply_second.1 = (f32[73,128,128]{2,1,0:T(8,128)S(1)}, f32[7,8,128]{2,1,0:T(8,128)S(1)}, bf16[9280,128]{1,0:T(8,128)(2,1)S(1)}, s32[384]{0:T(512)S(1)}, s32[48]{0:T(128)S(1)}) custom-call(s32[3]{0:T(128)S(1)} %pad_add_fusion.place_ref, ...), custom_call_target="tpu_custom_call", output_to_operand_aliasing={{0}: (9, {}), {1}: (10, {}), {2}: (11, {})} | custom-call | flops 100000000 | bytes 1000000 | tf_op jit(solution)/shard_map/multiply_second/pallas_call | solution.py:259
  48.2 5.4 %collective-permute-done.10.refs_0_ = bf16[2320,128]{1,0:T(8,128)(2,1)S(1)} collective-permute-done((bf16[2320,128]{1,0:T(8,128)(2,1)S(1)}, bf16[2320,128]{1,0:T(8,128)(2,1)S(1)}, u32[]{:S(2)}, u32[]{:S(2)}) %collective-permute-start.10) | collective-permute-done | bytes 593952 | tf_op jit(solution)/shard_map/ppermute | solution.py:374
  53.6 1.9 %collective-permute-start.11 = (bf16[2320,128]{1,0:T(8,128)(2,1)S(1)}, bf16[2320,128]{1,0:T(8,128)(2,1)S(1)}, u32[]{:S(2)}, u32[]{:S(2)}) collective-permute-start(bf16[2320,128]{1,0:T(8,128)(2,1)S(1)} %collective-permute-done.10.refs_0_), channel_id=1, source_target_pairs={{0,1},{1,0},{6,7},{7,6},{8,9},{9,8},{14,15},{15,14},{16,17},{17,16... | collective-permute-start | bytes 1781768 | tf_op jit(solution)/shard_map/ppermute | solution.py:378
  55.5 0.0 collective-permute-done.13.refs_2_
  55.5 0.0 collective-permute-done.12.refs_1_
  55.5 2.6 %multiply_late.1 = (f32[73,128,128]{2,1,0:T(8,128)S(1)}, f32[7,8,128]{2,1,0:T(8,128)S(1)}) custom-call(s32[3]{0:T(128)S(1)} %pad_add_fusion.place_ref, s32[384]{0:T(512)S(1)} %get-tuple-element.26.slots_of, s32[48]{0:T(128)S(1)} %get-tuple-element.27.n_of, bf16[9280,128]{1,0:T(8,128)(2,1)S(1)} %get-tuple-element.28.y_blocks, ...), custom_call_target="tpu_custom_call", output_to_operand_aliasing={{0}: (7, {})} | custom-call | flops 100000000 | bytes 1000000 | tf_op jit(solution)/shard_map/multiply_late/pallas_call | solution.py:297
  58.2 0.0 collective-permute-done.11.refs_0_
  58.2 2.2 %multiply_last.1 = (f32[73,128,128]{2,1,0:T(8,128)S(1)}, f32[1,768]{1,0:T(1,128)S(1)}) custom-call(s32[3]{0:T(128)S(1)} %pad_add_fusion.place_ref, s32[384]{0:T(512)S(1)} %get-tuple-element.26.slots_of, s32[48]{0:T(128)S(1)} %get-tuple-element.27.n_of, bf16[9280,128]{1,0:T(8,128)(2,1)S(1)} %get-tuple-element.28.y_blocks, ...), custom_call_target="tpu_custom_call", output_to_operand_aliasing={{0}: (5, {})} | custom-call | flops 100000000 | bytes 1000000 | tf_op jit(solution)/shard_map/multiply_last/pallas_call | solution.py:297
  60.4 3.9 %collective-permute-start.16 = (f32[1,768]{1,0:T(1,128)S(1)}, f32[1,768]{1,0:T(1,128)S(1)}, u32[]{:S(2)}, u32[]{:S(2)}) collective-permute-start(f32[1,768]{1,0:T(1,128)S(1)} %get-tuple-element.38.refs_1_), channel_id=1, source_target_pairs={{0,24},{8,16},{16,8},{24,0},{1,25},{9,17},{17,9},{25,1},{2,26},{10... | collective-permute-start | bytes 9224 | tf_op jit(solution)/shard_map/ppermute | solution.py:415
  64.3 0.0 collective-permute-start.15
  64.3 0.6 collective-permute-start.14
  65.0 0.9 %collective-permute-done.16.refs_4_ = f32[1,768]{1,0:T(1,128)S(1)} collective-permute-done((f32[1,768]{1,0:T(1,128)S(1)}, f32[1,768]{1,0:T(1,128)S(1)}, u32[]{:S(2)}, u32[]{:S(2)}) %collective-permute-start.16) | collective-permute-done | bytes 3104 | tf_op jit(solution)/shard_map/ppermute | solution.py:415
  65.9 2.0 %collective-permute-done.15.refs_3_ = f32[1,768]{1,0:T(1,128)S(1)} collective-permute-done((f32[1,768]{1,0:T(1,128)S(1)}, f32[1,768]{1,0:T(1,128)S(1)}, u32[]{:S(2)}, u32[]{:S(2)}) %collective-permute-start.15) | collective-permute-done | bytes 3104 | tf_op jit(solution)/shard_map/ppermute | solution.py:415
  67.9 0.0 collective-permute-done.14.refs_2_
  67.9 2.3 %scale.1 = f32[1536,768]{1,0:T(8,128)} custom-call(f32[73,128,128]{2,1,0:T(8,128)S(1)} %get-tuple-element.37.refs_0_, f32[1,768]{1,0:T(1,128)S(1)} %get-tuple-element.38.refs_1_, f32[1,768]{1,0:T(1,128)S(1)} %collective-permute-done.14.refs_2_, f32[1,768]{1,0:T(1,128)S(1)} %collective-permute-done.15.refs_3_, f32[1,768]{1,0:T(1,128)S(1)} %collective-permute-done.16.refs_4_), custom_call_target="tpu_custom_call" | custom-call | flops 10000000 | bytes 10000000 | tf_op jit(solution)/shard_map/scale/pallas_call | solution.py:344
Async XLA Ops:
  2.9 16.7 %collective-permute-start.4 = (bf16[2320,128]{1,0:T(8,128)(2,1)}, bf16[2320,128]{1,0:T(8,128)(2,1)S(1)}, u32[]{:S(2)}, u32[]{:S(2)}) collective-permute-start(bf16[2320,128]{1,0:T(8,128)(2,1)} %compact.1.refs_0_), channel_id=1, source_target_pairs={{2,0},{0,2},{6,4},{4,6},{3,1},{1,3},{7,5},{5,7},{10,8},{8,10},{14,... | collective-permute-start | bytes 1781768 | tf_op jit(solution)/shard_map/ppermute | solution.py:374
  5.9 14.4 %collective-permute-start.3 = (bf16[2320,128]{1,0:T(8,128)(2,1)}, bf16[2320,128]{1,0:T(8,128)(2,1)S(1)}, u32[]{:S(2)}, u32[]{:S(2)}) collective-permute-start(bf16[2320,128]{1,0:T(8,128)(2,1)} %compact.1.refs_0_), channel_id=1, source_target_pairs={{4,2},{2,4},{5,3},{3,5},{12,10},{10,12},{13,11},{11,13},{20,18},{1... | collective-permute-start | bytes 1781768 | tf_op jit(solution)/shard_map/ppermute | solution.py:374
  6.6 15.3 %collective-permute-start.9 = (bf16[2320,128]{1,0:T(8,128)(2,1)}, bf16[2320,128]{1,0:T(8,128)(2,1)}, u32[]{:S(2)}, u32[]{:S(2)}) collective-permute-start(bf16[2320,128]{1,0:T(8,128)(2,1)} %compact.1.refs_0_), channel_id=1, source_target_pairs={{0,16},{8,24},{16,0},{24,8},{1,17},{9,25},{17,1},{25,9},{2,18},{10... | collective-permute-start | bytes 1781768 | tf_op jit(solution)/shard_map/ppermute | solution.py:386
  8.2 13.8 %collective-permute-start.2 = (bf16[2320,128]{1,0:T(8,128)(2,1)}, bf16[2320,128]{1,0:T(8,128)(2,1)S(1)}, u32[]{:S(2)}, u32[]{:S(2)}) collective-permute-start(bf16[2320,128]{1,0:T(8,128)(2,1)} %compact.1.refs_0_), channel_id=1, source_target_pairs={{0,1},{1,0},{2,3},{3,2},{4,5},{5,4},{6,7},{7,6},{8,9},{9,8},{10,11... | collective-permute-start | bytes 1781768 | tf_op jit(solution)/shard_map/ppermute | solution.py:378
  8.2 16.1 %collective-permute-start = (bf16[2320,128]{1,0:T(8,128)(2,1)}, bf16[2320,128]{1,0:T(8,128)(2,1)}, u32[]{:S(2)}, u32[]{:S(2)}) collective-permute-start(bf16[2320,128]{1,0:T(8,128)(2,1)} %compact.1.refs_0_), channel_id=1, source_target_pairs={{0,8},{8,0},{16,24},{24,16},{1,9},{9,1},{17,25},{25,17},{2,10},{10... | collective-permute-start | bytes 1781768 | tf_op jit(solution)/shard_map/ppermute | solution.py:386
  19.6 12.2 %collective-permute-start.7 = (bf16[2320,128]{1,0:T(8,128)(2,1)S(1)}, bf16[2320,128]{1,0:T(8,128)(2,1)S(1)}, u32[]{:S(2)}, u32[]{:S(2)}) collective-permute-start(bf16[2320,128]{1,0:T(8,128)(2,1)S(1)} %collective-permute-done.4.refs_5_.refs_3_), channel_id=1, source_target_pairs={{4,2},{2,4},{5,3},{3,5},{12,10},{10,12},{13,11},{11,13},{20,18},{1... | collective-permute-start | bytes 1781768 | tf_op jit(solution)/shard_map/ppermute | solution.py:374
  20.3 18.0 %collective-permute-start.8 = (bf16[2320,128]{1,0:T(8,128)(2,1)S(1)}, bf16[2320,128]{1,0:T(8,128)(2,1)S(1)}, u32[]{:S(2)}, u32[]{:S(2)}) collective-permute-start(bf16[2320,128]{1,0:T(8,128)(2,1)S(1)} %collective-permute-done.3.refs_4_.refs_2_), channel_id=1, source_target_pairs={{2,0},{4,6},{3,1},{5,7},{10,8},{12,14},{11,9},{13,15},{18,16},{20,... | collective-permute-start | bytes 1781768 | tf_op jit(solution)/shard_map/ppermute | solution.py:374
  21.9 18.4 %collective-permute-start.6 = (bf16[2320,128]{1,0:T(8,128)(2,1)S(1)}, bf16[2320,128]{1,0:T(8,128)(2,1)S(1)}, u32[]{:S(2)}, u32[]{:S(2)}) collective-permute-start(bf16[2320,128]{1,0:T(8,128)(2,1)S(1)} %collective-permute-done.4.refs_5_.refs_3_), channel_id=1, source_target_pairs={{0,1},{1,0},{2,3},{3,2},{4,5},{5,4},{6,7},{7,6},{8,9},{9,8},{10,11... | collective-permute-start | bytes 1781768 | tf_op jit(solution)/shard_map/ppermute | solution.py:378
  22.0 20.3 %collective-permute-start.5 = (bf16[2320,128]{1,0:T(8,128)(2,1)S(1)}, bf16[2320,128]{1,0:T(8,128)(2,1)S(1)}, u32[]{:S(2)}, u32[]{:S(2)}) collective-permute-start(bf16[2320,128]{1,0:T(8,128)(2,1)S(1)} %collective-permute-done.3.refs_4_.refs_2_), channel_id=1, source_target_pairs={{2,3},{3,2},{4,5},{5,4},{10,11},{11,10},{12,13},{13,12},{18,19},{1... | collective-permute-start | bytes 1781768 | tf_op jit(solution)/shard_map/ppermute | solution.py:378
  24.3 17.9 %collective-permute-start.1 = (bf16[2320,128]{1,0:T(8,128)(2,1)}, bf16[2320,128]{1,0:T(8,128)(2,1)S(1)}, u32[]{:S(2)}, u32[]{:S(2)}) collective-permute-start(bf16[2320,128]{1,0:T(8,128)(2,1)} %collective-permute-done.refs_1_), channel_id=1, source_target_pairs={{0,16},{8,24},{16,0},{24,8},{1,17},{9,25},{17,1},{25,9},{2,18},{10... | collective-permute-start | bytes 1781768 | tf_op jit(solution)/shard_map/ppermute | solution.py:390
  24.8 1.1 %copy-start = (bf16[2320,128]{1,0:T(8,128)(2,1)S(1)}, bf16[2320,128]{1,0:T(8,128)(2,1)}, u32[]{:S(2)}) copy-start(bf16[2320,128]{1,0:T(8,128)(2,1)} %compact.1.refs_0_) | copy-start | bytes 1781764
  38.3 15.2 %collective-permute-start.10 = (bf16[2320,128]{1,0:T(8,128)(2,1)S(1)}, bf16[2320,128]{1,0:T(8,128)(2,1)S(1)}, u32[]{:S(2)}, u32[]{:S(2)}) collective-permute-start(bf16[2320,128]{1,0:T(8,128)(2,1)S(1)} %collective-permute-done.7.refs_6_), channel_id=1, source_target_pairs={{2,0},{4,6},{3,1},{5,7},{10,8},{12,14},{11,9},{13,15},{18,16},{20,... | collective-permute-start | bytes 1781768 | tf_op jit(solution)/shard_map/ppermute | solution.py:374
  39.6 15.9 %collective-permute-start.12 = (bf16[2320,128]{1,0:T(8,128)(2,1)S(1)}, bf16[2320,128]{1,0:T(8,128)(2,1)S(1)}, u32[]{:S(2)}, u32[]{:S(2)}) collective-permute-start(bf16[2320,128]{1,0:T(8,128)(2,1)S(1)} %collective-permute-done.7.refs_6_), channel_id=1, source_target_pairs={{2,3},{3,2},{4,5},{5,4},{10,11},{11,10},{12,13},{13,12},{18,19},{1... | collective-permute-start | bytes 1781768 | tf_op jit(solution)/shard_map/ppermute | solution.py:378
  40.3 15.2 %collective-permute-start.13 = (bf16[2320,128]{1,0:T(8,128)(2,1)S(1)}, bf16[2320,128]{1,0:T(8,128)(2,1)S(1)}, u32[]{:S(2)}, u32[]{:S(2)}) collective-permute-start(bf16[2320,128]{1,0:T(8,128)(2,1)S(1)} %collective-permute-done.8.refs_7_), channel_id=1, source_target_pairs={{0,1},{1,0},{6,7},{7,6},{8,9},{9,8},{14,15},{15,14},{16,17},{17,16... | collective-permute-start | bytes 1781768 | tf_op jit(solution)/shard_map/ppermute | solution.py:378
  53.6 4.6 %collective-permute-start.11 = (bf16[2320,128]{1,0:T(8,128)(2,1)S(1)}, bf16[2320,128]{1,0:T(8,128)(2,1)S(1)}, u32[]{:S(2)}, u32[]{:S(2)}) collective-permute-start(bf16[2320,128]{1,0:T(8,128)(2,1)S(1)} %collective-permute-done.10.refs_0_), channel_id=1, source_target_pairs={{0,1},{1,0},{6,7},{7,6},{8,9},{9,8},{14,15},{15,14},{16,17},{17,16... | collective-permute-start | bytes 1781768 | tf_op jit(solution)/shard_map/ppermute | solution.py:378
  60.4 5.5 %collective-permute-start.16 = (f32[1,768]{1,0:T(1,128)S(1)}, f32[1,768]{1,0:T(1,128)S(1)}, u32[]{:S(2)}, u32[]{:S(2)}) collective-permute-start(f32[1,768]{1,0:T(1,128)S(1)} %get-tuple-element.38.refs_1_), channel_id=1, source_target_pairs={{0,24},{8,16},{16,8},{24,0},{1,25},{9,17},{17,9},{25,1},{2,26},{10... | collective-permute-start | bytes 9224 | tf_op jit(solution)/shard_map/ppermute | solution.py:415
  64.3 3.6 %collective-permute-start.15 = (f32[1,768]{1,0:T(1,128)S(1)}, f32[1,768]{1,0:T(1,128)S(1)}, u32[]{:S(2)}, u32[]{:S(2)}) collective-permute-start(f32[1,768]{1,0:T(1,128)S(1)} %get-tuple-element.38.refs_1_), channel_id=1, source_target_pairs={{0,16},{8,24},{16,0},{24,8},{1,17},{9,25},{17,1},{25,9},{2,18},{10... | collective-permute-start | bytes 9224 | tf_op jit(solution)/shard_map/ppermute | solution.py:415
  64.3 3.6 %collective-permute-start.14 = (f32[1,768]{1,0:T(1,128)S(1)}, f32[1,768]{1,0:T(1,128)S(1)}, u32[]{:S(2)}, u32[]{:S(2)}) collective-permute-start(f32[1,768]{1,0:T(1,128)S(1)} %get-tuple-element.38.refs_1_), channel_id=1, source_target_pairs={{0,8},{8,0},{16,24},{24,16},{1,9},{9,1},{17,25},{25,17},{2,10},{10... | collective-permute-start | bytes 9224 | tf_op jit(solution)/shard_map/ppermute | solution.py:415

commit v2 on v1

--- a/solution.py
+++ b/solution.py
@@ -11,8 +11,11 @@
 SLOTS = 18
 SHARE = SLOTS * BLK
 HEAD = 16
+HALF = 9
 ROWS = HEAD + SHARE
-UNROLL = 4
+FIRST_ROWS = HEAD + HALF * BLK
+UNROLL = 8
+LAG = 3
 MIB = 1024 * 1024
 
 SMEM = pl.BlockSpec(memory_space=pltpu.SMEM)
@@ -21,15 +24,18 @@
 SMALL = pl.CostEstimate(flops=10**8, bytes_accessed=10**6, transcendentals=0)
 
 
-def compact_kernel(mask_ref, sim_ref, out_ref, places, sems):
+def compact_kernel(mask_ref, sim_ref, out_ref, slots, places, in_sems, out_sems):
     nb_cols, nb_rows = mask_ref.shape
 
-    def block_copy(slot, i, k):
-        return pltpu.make_async_copy(
-            sim_ref.at[pl.ds(pl.multiple_of(i * BLK, BLK), BLK), pl.ds(k * BLK, BLK)],
-            out_ref.at[pl.ds(pl.multiple_of(HEAD + slot * BLK, HEAD), BLK), :],
-            sems.at[slot],
-        )
+    def slot_rows(ref, slot):
+        return ref.at[pl.ds(pl.multiple_of(HEAD + slot * BLK, HEAD), BLK), :]
+
+    def copy_in(slot, i, k):
+        block = sim_ref.at[pl.ds(pl.multiple_of(i * BLK, BLK), BLK), pl.ds(k * BLK, BLK)]
+        return pltpu.make_async_copy(block, slot_rows(slots, slot), in_sems.at[slot])
+
+    def copy_out(slot):
+        return pltpu.make_async_copy(slot_rows(slots, slot), slot_rows(out_ref, slot), out_sems.at[slot])
 
     def scan(i, count):
         for k in range(nb_cols):
@@ -37,7 +43,7 @@
 
             @pl.when(here != 0)
             def _():
-                block_copy(count, i, k).start()
+                copy_in(count, i, k).start()
                 places[count] = i * 8 + k
 
             count = count + here
@@ -50,13 +56,22 @@
     header = jnp.where(lane == SLOTS, count, 0)
     for slot in range(SLOTS):
         header = jnp.where(lane == slot, places[slot], header)
-    out_ref[0:HEAD, :] = header.astype(jnp.float32).astype(out_ref.dtype)
-
-    def wait(slot, carry):
-        block_copy(slot, 0, 0).wait()
-        return carry
-
-    lax.fori_loop(0, count, wait, 0)
+    slots[0:HEAD, :] = header.astype(jnp.float32).astype(slots.dtype)
+    header_out = pltpu.make_async_copy(slots.at[pl.ds(0, HEAD), :], out_ref.at[pl.ds(0, HEAD), :], out_sems.at[SLOTS])
+    header_out.start()
+
+    def pass_on(slot, carry):
+        copy_in(slot, 0, 0).wait()
+        copy_out(slot).start()
+        return carry
+
+    def finish(slot, carry):
+        copy_out(slot).wait()
+        return carry
+
+    lax.fori_loop(0, count, pass_on, 0)
+    lax.fori_loop(0, count, finish, 0)
+    header_out.wait()
 
 
 def compact(mask, similarity):
@@ -64,8 +79,13 @@
         compact_kernel,
         out_shape=jax.ShapeDtypeStruct((ROWS, BLK), similarity.dtype),
         in_specs=[SMEM, ANY],
-        out_specs=VMEM,
-        scratch_shapes=[pltpu.SMEM((SLOTS,), jnp.int32), pltpu.SemaphoreType.DMA((SLOTS,))],
+        out_specs=ANY,
+        scratch_shapes=[
+            pltpu.VMEM((ROWS, BLK), similarity.dtype),
+            pltpu.SMEM((SLOTS,), jnp.int32),
+            pltpu.SemaphoreType.DMA((SLOTS,)),
+            pltpu.SemaphoreType.DMA((SLOTS + 1,)),
+        ],
         cost_estimate=pl.CostEstimate(flops=0, bytes_accessed=2 * SHARE * BLK * 2, transcendentals=0),
         name="compact",
     )(mask, similarity)
@@ -74,6 +94,15 @@
 def multiply_pairs(todo, share, x_ref, y_blocks, acc, sums, x_base=0):
     def multiply(step, carry):
         terms = []
+
+        def add_term(packed, term):
+            at = jnp.bitwise_and(packed, 127)
+            j = jnp.bitwise_and(lax.shift_right_logical(packed, 19), 7)
+            old = acc[at]
+            new = old + term
+            acc[at] = new
+            sums[j] += jnp.sum((term * (old + new)).reshape(BLK // 8, 8, BLK), axis=0)
+
         for u in range(UNROLL):
             packed = todo[share, 1 + step * UNROLL + u]
             x = x_base + HEAD + lax.shift_right_logical(packed, 22) * BLK
@@ -81,34 +110,36 @@
             x_block = x_ref[pl.ds(pl.multiple_of(x, HEAD), BLK), :]
             y_block = y_blocks[pl.ds(pl.multiple_of(y, HEAD), BLK), :]
             terms.append((packed, jnp.dot(x_block, y_block, preferred_element_type=jnp.float32)))
-        for packed, term in terms:
-            at = jnp.bitwise_and(packed, 127)
-            j = jnp.bitwise_and(lax.shift_right_logical(packed, 19), 7)
-            old = acc[at]
-            new = old + term
-            acc[at] = new
-            sums[j] += jnp.sum((term * (old + new)).reshape(BLK // 8, 8, BLK), axis=0)
+            if u >= LAG:
+                add_term(*terms[u - LAG])
+        for packed, term in terms[UNROLL - LAG :]:
+            add_term(packed, term)
         return carry
 
     n_steps = lax.shift_right_logical(todo[share, 0] + UNROLL - 1, UNROLL.bit_length() - 1)
     lax.fori_loop(0, n_steps, multiply, 0)
 
 
-def list_pairs(todo, share, places, at, n_slots, first_inner, slots_of, n_of, nb_rows, nb_cols):
+def list_pairs(todo, share, places, at, n_slots, first_inner, slots_of, n_of, nb_rows, nb_cols, first_slot=0):
     def slot_pairs(slot, count):
         place = places[at, slot]
         k = first_inner + jnp.bitwise_and(place, 7)
         packed = (slot << 22) + lax.shift_right_logical(place, 3) * nb_cols
 
-        def pair(n, count):
-            todo[share, 1 + count] = packed + slots_of[k * 8 + n]
-            return count + 1
-
-        return lax.fori_loop(0, n_of[k], pair, count)
-
-    count = lax.fori_loop(0, n_slots, slot_pairs, jnp.int32(0))
+        n_pairs = n_of[k]
+
+        def pair(n, carry):
+            todo[share, 1 + count + n] = packed + slots_of[k * 8 + n]
+            return carry
+
+        pair(0, 0)
+        pair(1, 0)
+        lax.fori_loop(2, n_pairs, pair, 0)
+        return count + n_pairs
+
+    count = lax.fori_loop(first_slot, n_slots, slot_pairs, jnp.int32(0))
     for u in range(UNROLL):
-        todo[share, 1 + count + u] = (nb_cols << 19) + nb_rows * nb_cols
+        todo[share, 1 + count + u] = (first_slot << 22) + (nb_cols << 19) + nb_rows * nb_cols
     todo[share, 0] = count
 
 
@@ -120,12 +151,12 @@
     lax.fori_loop(0, ref.shape[0], clear, 0)
 
 
-def read_headers(headers, heads, places, sem):
+def read_headers(headers, heads, places):
     for at, header in enumerate(headers):
         heads[at : at + 1, :] = header.astype(jnp.float32)[0:1, :].astype(jnp.int32)
-    copy = pltpu.make_async_copy(heads, places, sem)
-    copy.start()
-    return copy
+    for at in range(len(headers)):
+        for slot in range(SLOTS + 1):
+            places[at, slot] = heads[at, slot]
 
 
 def inner_of(n_col, nb_rows, nb_cols, tile, layer):
@@ -169,24 +200,27 @@
 
 
 def first_kernel(near, n_col, nb_rows, nb_cols, place_ref, *refs):
-    y_refs, refs = refs[: len(near)], refs[len(near) :]
-    x_refs, refs = refs[:3], refs[3:]
-    acc, sums, y_blocks, slots_of, n_of, heads, places, todo, y_sems, smem_sem = refs
+    own_ref, refs = refs[0], refs[1:]
+    y_refs, refs = refs[: len(near) - 1], refs[len(near) - 1 :]
+    x_refs, refs = refs[:2], refs[2:]
+    acc, sums, y_blocks, slots_of, n_of, own_head, heads, places, todo, y_sems = refs
     r, c, l = place_ref[0], place_ref[1], place_ref[2]
+    head_copy = pltpu.make_async_copy(own_ref.at[pl.ds(0, HEAD), :], own_head, y_sems.at[len(near)])
+    head_copy.start()
     copies = []
-    for at, (m, y_ref) in enumerate(zip(near, y_refs)):
+    for at, (m, y_ref) in enumerate(zip(near, (own_ref, *y_refs))):
         copies.append(pltpu.make_async_copy(y_ref, tile_rows(y_blocks, jnp.bitwise_xor(r, m)), y_sems.at[at]))
         copies[-1].start()
+    head_copy.wait()
+    headers = [own_head[...]] + [ref[0:HEAD, :] for ref in (*y_refs, *x_refs)]
+    read_headers(headers, heads, places)
     clear_blocks(acc)
     clear_blocks(sums)
+    list_column(slots_of, n_of, places, list(enumerate(near)), r, nb_rows)
     for copy in copies:
         copy.wait()
-    headers = [tile_rows(y_blocks, jnp.bitwise_xor(r, m), HEAD)[...] for m in near]
-    read_headers(headers + [ref[0:HEAD, :] for ref in x_refs], heads, places, smem_sem).wait()
-    list_column(slots_of, n_of, places, list(enumerate(near)), r, nb_rows)
     shares = [(c, l, 0, y_blocks, r * ROWS), (c, 1 - l, len(near), x_refs[0], 0)]
-    shares.append((chain_tile(c, 1, True), l, len(near) + 1, x_refs[1], 0))
-    shares.append((chain_tile(c, 1, False), l, len(near) + 2, x_refs[2], 0))
+    shares.append((chain_tile(c, 1, False), l, len(near) + 1, x_refs[1], 0))
     for tile, layer, at, x_ref, x_base in shares:
         valid, first_inner = inner_of(n_col, nb_rows, nb_cols, tile, layer)
         n_slots = jnp.where(valid, places[at, SLOTS], 0)
@@ -206,6 +240,7 @@
 
 def multiply_first(place, near, ys, xs, n_row, n_col, nb_rows, nb_cols):
     shares = len(near) + len(xs)
+    lists = list_scratch(n_row, nb_rows, nb_cols, shares)
     return pl.pallas_call(
         functools.partial(first_kernel, near, n_col, nb_rows, nb_cols),
         out_shape=[
@@ -213,10 +248,12 @@
             jax.ShapeDtypeStruct((nb_cols + 1, 8, BLK), jnp.float32),
             jax.ShapeDtypeStruct((n_row * ROWS, BLK), jnp.bfloat16),
         ],
-        in_specs=[SMEM] + [ANY] * len(near) + [VMEM] * len(xs),
+        in_specs=[SMEM, ANY] + [VMEM] * (shares - 1),
         out_specs=[VMEM] * 3,
-        scratch_shapes=list_scratch(n_row, nb_rows, nb_cols, shares)
-        + [pltpu.SemaphoreType.DMA((len(near),)), pltpu.SemaphoreType.DMA],
+        scratch_shapes=lists[:2]
+        + [pltpu.VMEM((HEAD, BLK), jnp.bfloat16)]
+        + lists[2:]
+        + [pltpu.SemaphoreType.DMA((len(near) + 1,))],
         compiler_params=pltpu.CompilerParams(vmem_limit_bytes=24 * MIB),
         cost_estimate=SMALL,
         name="multiply_first",
@@ -227,7 +264,8 @@
     distant = [m for m in range(n_row) if m not in near]
     y_refs, refs = refs[: len(distant)], refs[len(distant) :]
     x_refs, refs = refs[: len(x_kinds)], refs[len(x_kinds) :]
-    acc, sums, y_blocks, slots_of, n_of, heads, places, todo, y_sems, smem_sem = refs[3:]
+    half_refs, refs = refs[:2], refs[2:]
+    acc, sums, y_blocks, slots_of, n_of, heads, places, todo, y_sems = refs[3:]
     r, c, l = place_ref[0], place_ref[1], place_ref[2]
     copies = []
     for at, (m, y_ref) in enumerate(zip(distant, y_refs)):
@@ -235,8 +273,8 @@
         copies[-1].start()
     for copy in copies:
         copy.wait()
-    headers = column_headers(y_blocks, r, n_row) + [ref[0:HEAD, :] for ref in x_refs]
-    read_headers(headers, heads, places, smem_sem).wait()
+    headers = column_headers(y_blocks, r, n_row) + [ref[0:HEAD, :] for ref in (*x_refs, half_refs[0])]
+    read_headers(headers, heads, places)
     list_column(slots_of, n_of, places, [(m, m) for m in range(n_row)], r, nb_rows)
     shares = [((0, False, False, True), 0, y_blocks, r * ROWS)]
     shares += [(kind, n_row + at, x_ref, 0) for at, (kind, x_ref) in enumerate(zip(x_kinds, x_refs))]
@@ -249,21 +287,32 @@
         n_slots = jnp.where(valid, places[at, SLOTS], 0)
         list_pairs(todo, 0, places, at, n_slots, first_inner, slots_of, n_of, nb_rows, nb_cols)
         multiply_pairs(todo, 0, x_ref, y_blocks, acc, sums, x_base)
-
-
-def multiply_second(place, near, ys, xs, x_kinds, acc, sums, y_blocks, n_col, nb_rows, nb_cols):
+    is_end = jnp.logical_or(c == 0, c == n_col - 1)
+    step, at = n_col - 2, n_row + len(x_refs)
+    tile = jnp.where(is_end, chain_tile(c, step, False), chain_tile(c, step, True))
+    valid, first_inner = inner_of(n_col, nb_rows, nb_cols, tile, 1 - l)
+    n_slots = jnp.where(valid, places[at, SLOTS], 0)
+    for first_slot, end, x_ref, x_base in (
+        (0, jnp.minimum(n_slots, HALF), half_refs[0], 0),
+        (HALF, n_slots, half_refs[1], -FIRST_ROWS),
+    ):
+        list_pairs(todo, 0, places, at, end, first_inner, slots_of, n_of, nb_rows, nb_cols, first_slot)
+        multiply_pairs(todo, 0, x_ref, y_blocks, acc, sums, x_base)
+
+
+def multiply_second(place, near, ys, xs, x_kinds, halves, acc, sums, y_blocks, n_col, nb_rows, nb_cols):
     n_row = len(ys)
     distant = [ys[m] for m in range(n_row) if m not in near]
-    operands = [place, *distant, *xs, acc, sums, y_blocks]
-    lists = list_scratch(n_row, nb_rows, nb_cols, n_row + len(xs))
+    operands = [place, *distant, *xs, *halves, acc, sums, y_blocks]
+    lists = list_scratch(n_row, nb_rows, nb_cols, n_row + len(xs) + 1)
     return pl.pallas_call(
         functools.partial(second_kernel, near, n_row, n_col, nb_rows, nb_cols, x_kinds),
         out_shape=[jax.ShapeDtypeStruct(x.shape, x.dtype) for x in (acc, sums, y_blocks)]
         + [jax.ShapeDtypeStruct(x.shape, x.dtype) for x in lists[:2]],
-        in_specs=[SMEM] + [ANY] * len(distant) + [VMEM] * (len(xs) + 3),
+        in_specs=[SMEM] + [ANY] * len(distant) + [VMEM] * (len(xs) + 5),
         out_specs=[VMEM] * 3 + [SMEM] * 2,
         input_output_aliases={len(operands) - 3 + at: at for at in range(3)},
-        scratch_shapes=lists[2:] + [pltpu.SemaphoreType.DMA((len(distant),)), pltpu.SemaphoreType.DMA],
+        scratch_shapes=lists[2:] + [pltpu.SemaphoreType.DMA((len(distant),))],
         compiler_params=pltpu.CompilerParams(vmem_limit_bytes=24 * MIB),
         cost_estimate=SMALL,
         name="multiply_second",
@@ -273,12 +322,11 @@
 def late_kernel(n_col, nb_rows, nb_cols, x_kinds, is_last, place_ref, slots_of, n_of, y_blocks, *refs):
     x_refs, refs = refs[: len(x_kinds)], refs[len(x_kinds) :]
     _, before_sums, acc = refs[:3]
-    sums, heads, places, todo, smem_sem = refs[-5:]
+    sums, heads, places, todo = refs[-4:]
     c, l = place_ref[1], place_ref[2]
-    to_smem = read_headers([ref[0:HEAD, :] for ref in x_refs], heads, places, smem_sem)
+    read_headers([ref[0:HEAD, :] for ref in x_refs], heads, places)
     for j in range(sums.shape[0]):
         sums[j] = before_sums[j]
-    to_smem.wait()
     for at, (x_ref, (step, odd, other)) in enumerate(zip(x_refs, x_kinds)):
         valid, first_inner = inner_of(n_col, nb_rows, nb_cols, chain_tile(c, step, odd), 1 - l if other else l)
         n_slots = jnp.where(valid, places[at, SLOTS], 0)
@@ -301,8 +349,7 @@
         out_specs=[VMEM, VMEM],
         input_output_aliases={len(operands) - 2: 0},
         scratch_shapes=([pltpu.VMEM(sums.shape, jnp.float32)] if is_last else [])
-        + list_scratch(0, nb_rows, nb_cols, len(xs))[2:]
-        + [pltpu.SemaphoreType.DMA],
+        + list_scratch(0, nb_rows, nb_cols, len(xs))[2:],
         compiler_params=pltpu.CompilerParams(vmem_limit_bytes=24 * MIB),
         cost_estimate=SMALL,
         name="multiply_last" if is_last else "multiply_late",
@@ -388,26 +435,28 @@
         if ys[m] is None:
             bit = 1 << (m.bit_length() - 1)
             ys[m] = lax.ppermute(ys[m ^ bit], "row", [(s, s ^ bit) for s in range(n_row)])
-    first_xs = [sibling(own, range(n_col)), odd, even]
-    shares = list(zip([(0, False, True, True), (1, True, False, True), (1, False, False, True)], first_xs))
+    first_xs = [sibling(own, range(n_col)), even]
+    shares = [((0, False, True, True), first_xs[0]), ((1, True, False, False), odd), ((1, False, False, True), even)]
+    first_xs[1], _ = lax.optimization_barrier((even, odd))
     acc, sums, y_blocks = multiply_first(place, near, ys, first_xs, n_row, n_col, nb_rows, nb_cols)
     for step in range(1, n_col - 2):
         shares.append(((step, True, True, False), sibling(odd, holders(odd_tile, step))))
         shares.append(((step, False, True, False), sibling(even, holders(even_tile, step))))
         odd, even = hop(even, odd_tile, step + 1), hop(odd, even_tile, step + 1)
         shares += [((step + 1, True, False, False), odd), ((step + 1, False, False, False), even)]
-    odd, even, sums = lax.optimization_barrier((odd, even, sums))
+    odd, sums = lax.optimization_barrier((odd, sums))
     last = hop(odd, even_tile, n_col - 1)
+    arrived = jnp.where(jnp.logical_or(c == 0, c == n_col - 1), even, odd)
+    halves = [sibling(arrived[:FIRST_ROWS], range(n_col)), sibling(arrived[FIRST_ROWS:], range(n_col))]
     x_kinds, xs = zip(*shares)
     acc, sums, y_blocks, slots_of, n_of = multiply_second(
-        place, near, ys, xs, x_kinds, acc, sums, y_blocks, n_col, nb_rows, nb_cols
+        place, near, ys, xs, x_kinds, halves, acc, sums, y_blocks, n_col, nb_rows, nb_cols
     )
     last, sums = lax.optimization_barrier((last, sums))
     other = sibling(last, holders(even_tile, n_col - 1))
-    kinds = [(n_col - 1, False, False), (n_col - 2, True, True), (n_col - 2, False, True)]
-    xs = [last, sibling(odd, holders(odd_tile, n_col - 2)), sibling(even, holders(even_tile, n_col - 2))]
+    kinds = [(n_col - 1, False, False)]
     sizes = n_col, nb_rows, nb_cols
-    acc, sums = multiply_late(place, slots_of, n_of, y_blocks, xs, kinds, acc, sums, False, *sizes)
+    acc, sums = multiply_late(place, slots_of, n_of, y_blocks, [last], kinds, acc, sums, False, *sizes)
     kinds = [(n_col - 1, False, True)]
     product, sums = multiply_late(place, slots_of, n_of, y_blocks, [other], kinds, acc, sums, True, *sizes)
     all_sums = [sums]

time: 70 us -> 65.9 us (0.941); the launches traced: 70.2 us -> 65.3 us
  Pallas kernels: 21.9 us -> 17.9 us
  starting transfers between devices: 20.4 us -> 17.2 us
  waiting for transfers between devices: 26.6 us -> 28.8 us
    pallas_call x2, Pallas kernels: 4.87 us -> 2.2 us  [multiply_late(): pl.pallas_call(functools.partial(late_kernel, n_col, nb_rows, nb_cols, x_...]
    ppermute x6, starting transfers between devices: 5.22 us -> 3.23 us  [sibling(): return lax.ppermute(x, ('col', 'layer'), pairs)]
    ppermute x6, waiting for transfers between devices: 0.02 us -> 1.99 us  [sibling(): return lax.ppermute(x, ('col', 'layer'), pairs)]
    pallas_call x1, Pallas kernels: 5.87 us -> 4.89 us  [multiply_second(): pl.pallas_call(functools.partial(second_kernel, near, n_row, n_col, nb_ro...]
    ppermute x3, starting transfers between devices: 4.53 us -> 3.55 us  [body(): lax.ppermute(sums, 'row', [(s, s ^ m) for s in range(n_row)])]
  transfers between devices with their start and end apart: 17 -> 17, of which waited for: 7 -> 11; matrix products, arithmetic and copies ran while one was open for 0% -> 0% of each run, Pallas kernels for 21% -> 18%
where the time goes in v2:
time: 65.9 us; the launch traced here: 65.3 us
  waiting for transfers between devices  28.8 us (44%)
  Pallas kernels  17.9 us (27%)
  starting transfers between devices  17.2 us (26%)
  local copies, waits for them, and re-layouts  1.11 us (2%)
    ppermute x5, waiting for transfers between devices, hop(): lax.ppermute(x, 'col', [(tile(i, 1), i) for i in holders(tile, step)])  21.7 us
    ppermute x5, starting transfers between devices, hop(): lax.ppermute(x, 'col', [(tile(i, 1), i) for i in holders(tile, step)])  6.81 us
    pallas_call x1, Pallas kernels, multiply_first(): pl.pallas_call(functools.partial(first_kernel, near, n_col, nb_rows, nb_c...  5.64 us
    pallas_call x1, Pallas kernels, multiply_second(): pl.pallas_call(functools.partial(second_kernel, near, n_row, n_col, nb_ro...  4.89 us
    ppermute x3, starting transfers between devices, body(): lax.ppermute(sums, 'row', [(s, s ^ m) for s in range(n_row)])  3.55 us
    ppermute x6, starting transfers between devices, sibling(): return lax.ppermute(x, ('col', 'layer'), pairs)  3.23 us
    ppermute x2, starting transfers between devices, body(): ys[m] = lax.ppermute(own, 'row', [(s, s ^ m) for s in range(n_row)])  3.17 us
    ppermute x3, waiting for transfers between devices, body(): lax.ppermute(sums, 'row', [(s, s ^ m) for s in range(n_row)])  3.06 us
  transfers between devices with their start and end apart: 17, of which 11 were waited for; matrix products, arithmetic and copies ran while one was open for 0% of the time, Pallas kernels for 18%

profile of v2, /device:TPU:0, one launch (start us, length us, event | category | flops | bytes accessed | tf_op | source)
XLA Modules:
  0.0 65.3 jit_solution(5294375586254985656)
XLA Ops:
  0.0 2.9 %compact.1.refs_0_ = bf16[2320,128]{1,0:T(8,128)(2,1)} custom-call(s32[6,12]{1,0:T(8,128)} %bitcast.4, bf16[1536,768]{1,0:T(8,128)(2,1)} %sim_ref.1), custom_call_target="tpu_custom_call" | custom-call | bytes 1179648 | tf_op jit(solution)/shard_map/compact/pallas_call | solution.py:78
  2.9 2.9 %collective-permute-start.4 = (bf16[2320,128]{1,0:T(8,128)(2,1)}, bf16[2320,128]{1,0:T(8,128)(2,1)S(1)}, u32[]{:S(2)}, u32[]{:S(2)}) collective-permute-start(bf16[2320,128]{1,0:T(8,128)(2,1)} %compact.1.refs_0_), channel_id=1, source_target_pairs={{2,0},{0,2},{6,4},{4,6},{3,1},{1,3},{7,5},{5,7},{10,8},{8,10},{14,... | collective-permute-start | bytes 1781768 | tf_op jit(solution)/shard_map/ppermute | solution.py:421
  5.7 0.7 %collective-permute-start.3 = (bf16[2320,128]{1,0:T(8,128)(2,1)}, bf16[2320,128]{1,0:T(8,128)(2,1)S(1)}, u32[]{:S(2)}, u32[]{:S(2)}) collective-permute-start(bf16[2320,128]{1,0:T(8,128)(2,1)} %compact.1.refs_0_), channel_id=1, source_target_pairs={{4,2},{2,4},{5,3},{3,5},{12,10},{10,12},{13,11},{11,13},{20,18},{1... | collective-permute-start | bytes 1781768 | tf_op jit(solution)/shard_map/ppermute | solution.py:421
  6.4 1.7 %collective-permute-start.9 = (bf16[2320,128]{1,0:T(8,128)(2,1)}, bf16[2320,128]{1,0:T(8,128)(2,1)}, u32[]{:S(2)}, u32[]{:S(2)}) collective-permute-start(bf16[2320,128]{1,0:T(8,128)(2,1)} %compact.1.refs_0_), channel_id=1, source_target_pairs={{0,16},{8,24},{16,0},{24,8},{1,17},{9,25},{17,1},{25,9},{2,18},{10... | collective-permute-start | bytes 1781768 | tf_op jit(solution)/shard_map/ppermute | solution.py:433
  8.1 0.0 collective-permute-start.2
  8.1 1.5 %collective-permute-start = (bf16[2320,128]{1,0:T(8,128)(2,1)}, bf16[2320,128]{1,0:T(8,128)(2,1)}, u32[]{:S(2)}, u32[]{:S(2)}) collective-permute-start(bf16[2320,128]{1,0:T(8,128)(2,1)} %compact.1.refs_0_), channel_id=1, source_target_pairs={{0,8},{8,0},{16,24},{24,16},{1,9},{9,1},{17,25},{25,17},{2,10},{10... | collective-permute-start | bytes 1781768 | tf_op jit(solution)/shard_map/ppermute | solution.py:433
  9.6 10.0 %collective-permute-done.4.refs_4_.refs_3_ = bf16[2320,128]{1,0:T(8,128)(2,1)S(1)} collective-permute-done((bf16[2320,128]{1,0:T(8,128)(2,1)}, bf16[2320,128]{1,0:T(8,128)(2,1)S(1)}, u32[]{:S(2)}, u32[]{:S(2)}) %collective-permute-start.4) | collective-permute-done | bytes 593952 | tf_op jit(solution)/shard_map/ppermute | solution.py:421
  19.6 0.7 %collective-permute-start.7 = (bf16[2320,128]{1,0:T(8,128)(2,1)S(1)}, bf16[2320,128]{1,0:T(8,128)(2,1)S(1)}, u32[]{:S(2)}, u32[]{:S(2)}) collective-permute-start(bf16[2320,128]{1,0:T(8,128)(2,1)S(1)} %collective-permute-done.4.refs_4_.refs_3_), channel_id=1, source_target_pairs={{4,2},{2,4},{5,3},{3,5},{12,10},{10,12},{13,11},{11,13},{20,18},{1... | collective-permute-start | bytes 1781768 | tf_op jit(solution)/shard_map/ppermute | solution.py:421
  20.3 0.0 collective-permute-done.3.refs_2_
  20.3 1.3 %collective-permute-start.8 = (bf16[2320,128]{1,0:T(8,128)(2,1)S(1)}, bf16[2320,128]{1,0:T(8,128)(2,1)S(1)}, u32[]{:S(2)}, u32[]{:S(2)}) collective-permute-start(bf16[2320,128]{1,0:T(8,128)(2,1)S(1)} %collective-permute-done.3.refs_2_), channel_id=1, source_target_pairs={{2,0},{4,6},{3,1},{5,7},{10,8},{12,14},{11,9},{13,15},{18,16},{20,... | collective-permute-start | bytes 1781768 | tf_op jit(solution)/shard_map/ppermute | solution.py:421
  21.6 0.1 pad_add_fusion.place_ref
  21.7 0.2 collective-permute-done.9.refs_2_
  21.9 0.0 collective-permute-start.6
  21.9 0.0 collective-permute-done.2.refs_3_.refs_1_
  21.9 0.7 %collective-permute-start.5 = (bf16[2320,128]{1,0:T(8,128)(2,1)S(1)}, bf16[2320,128]{1,0:T(8,128)(2,1)S(1)}, u32[]{:S(2)}, u32[]{:S(2)}) collective-permute-start(bf16[2320,128]{1,0:T(8,128)(2,1)S(1)} %collective-permute-done.3.refs_2_), channel_id=1, source_target_pairs={{2,3},{3,2},{4,5},{5,4},{10,11},{11,10},{12,13},{13,12},{18,19},{1... | collective-permute-start | bytes 1781768 | tf_op jit(solution)/shard_map/ppermute | solution.py:425
  22.6 1.7 %collective-permute-done.refs_1_ = bf16[2320,128]{1,0:T(8,128)(2,1)} collective-permute-done((bf16[2320,128]{1,0:T(8,128)(2,1)}, bf16[2320,128]{1,0:T(8,128)(2,1)}, u32[]{:S(2)}, u32[]{:S(2)}) %collective-permute-start) | collective-permute-done | bytes 593952 | tf_op jit(solution)/shard_map/ppermute | solution.py:433
  24.3 0.4 collective-permute-start.1
  24.7 0.0 copy-start
  24.7 1.1 %copy-done = bf16[2320,128]{1,0:T(8,128)(2,1)S(1)} copy-done((bf16[2320,128]{1,0:T(8,128)(2,1)S(1)}, bf16[2320,128]{1,0:T(8,128)(2,1)}, u32[]{:S(2)}) %copy-start) | copy-done | bytes 593944
  25.7 5.6 %multiply_first.1 = (f32[73,128,128]{2,1,0:T(8,128)S(1)}, f32[7,8,128]{2,1,0:T(8,128)S(1)}, bf16[9280,128]{1,0:T(8,128)(2,1)S(1)}) custom-call(s32[3]{0:T(128)S(1)} %pad_add_fusion.place_ref, bf16[2320,128]{1,0:T(8,128)(2,1)S(1)} %copy-done, bf16[2320,128]{1,0:T(8,128)(2,1)} %collective-permute-done.refs_1_, ...), custom_call_target="tpu_custom_call" | custom-call | flops 100000000 | bytes 1000000 | tf_op jit(solution)/shard_map/multiply_first/pallas_call | solution.py:244
  31.4 0.0 collective-permute-done.7.refs_6_
  31.4 1.3 %collective-permute-start.12 = (bf16[2320,128]{1,0:T(8,128)(2,1)S(1)}, bf16[2320,128]{1,0:T(8,128)(2,1)S(1)}, u32[]{:S(2)}, u32[]{:S(2)}) collective-permute-start(bf16[2320,128]{1,0:T(8,128)(2,1)S(1)} %collective-permute-done.7.refs_6_), channel_id=1, source_target_pairs={{2,0},{4,6},{3,1},{5,7},{10,8},{12,14},{11,9},{13,15},{18,16},{20,... | collective-permute-start | bytes 1781768 | tf_op jit(solution)/shard_map/ppermute | solution.py:421
  32.7 5.8 %collective-permute-done.8.refs_7_ = bf16[2320,128]{1,0:T(8,128)(2,1)S(1)} collective-permute-done((bf16[2320,128]{1,0:T(8,128)(2,1)S(1)}, bf16[2320,128]{1,0:T(8,128)(2,1)S(1)}, u32[]{:S(2)}, u32[]{:S(2)}) %collective-permute-start.8) | collective-permute-done | bytes 593952 | tf_op jit(solution)/shard_map/ppermute | solution.py:421
  38.5 0.1 broadcast_select_fusion
  38.6 0.1 collective-permute-start.10
  38.7 0.0 collective-permute-done.6.refs_5_
  38.8 0.6 collective-permute-start.11
  39.3 0.0 collective-permute-done.5.refs_4_
  39.3 0.2 collective-permute-done.1.refs_0_
  39.5 1.2 %collective-permute-done.11.refs_9_ = bf16[1152,128]{1,0:T(8,128)(2,1)S(1)} collective-permute-done((bf16[1152,128]{1,0:T(8,128)(2,1)S(1)}, bf16[1152,128]{1,0:T(8,128)(2,1)S(1)}, u32[]{:S(2)}, u32[]{:S(2)}) %collective-permute-start.11) | collective-permute-done | bytes 294944 | tf_op jit(solution)/shard_map/ppermute | solution.py:425
  40.7 0.0 collective-permute-done.10.refs_8_
  40.7 4.9 %multiply_second.1 = (f32[73,128,128]{2,1,0:T(8,128)S(1)}, f32[7,8,128]{2,1,0:T(8,128)S(1)}, bf16[9280,128]{1,0:T(8,128)(2,1)S(1)}, s32[384]{0:T(512)S(1)}, s32[48]{0:T(128)S(1)}) custom-call(s32[3]{0:T(128)S(1)} %pad_add_fusion.place_ref, ...), custom_call_target="tpu_custom_call", output_to_operand_aliasing={{0}: (11, {}), {1}: (12, {}), {2}: (13, {})} | custom-call | flops 100000000 | bytes 1000000 | tf_op jit(solution)/shard_map/multiply_second/pallas_call | solution.py:308
  45.6 5.8 %collective-permute-done.12.refs_0_ = bf16[2320,128]{1,0:T(8,128)(2,1)S(1)} collective-permute-done((bf16[2320,128]{1,0:T(8,128)(2,1)S(1)}, bf16[2320,128]{1,0:T(8,128)(2,1)S(1)}, u32[]{:S(2)}, u32[]{:S(2)}) %collective-permute-start.12) | collective-permute-done | bytes 593952 | tf_op jit(solution)/shard_map/ppermute | solution.py:421
  51.4 1.9 %collective-permute-start.13 = (bf16[2320,128]{1,0:T(8,128)(2,1)S(1)}, bf16[2320,128]{1,0:T(8,128)(2,1)S(1)}, u32[]{:S(2)}, u32[]{:S(2)}) collective-permute-start(bf16[2320,128]{1,0:T(8,128)(2,1)S(1)} %collective-permute-done.12.refs_0_), channel_id=1, source_target_pairs={{0,1},{1,0},{6,7},{7,6},{8,9},{9,8},{14,15},{15,14},{16,17},{17,16... | collective-permute-start | bytes 1781768 | tf_op jit(solution)/shard_map/ppermute | solution.py:425
  53.4 1.2 %multiply_late.1 = (f32[73,128,128]{2,1,0:T(8,128)S(1)}, f32[7,8,128]{2,1,0:T(8,128)S(1)}) custom-call(s32[3]{0:T(128)S(1)} %pad_add_fusion.place_ref, s32[384]{0:T(512)S(1)} %get-tuple-element.28.slots_of, s32[48]{0:T(128)S(1)} %get-tuple-element.29.n_of, bf16[9280,128]{1,0:T(8,128)(2,1)S(1)} %get-tuple-element.30.y_blocks, ...), custom_call_target="tpu_custom_call", output_to_operand_aliasing={{0}: (5, {})} | custom-call | flops 100000000 | bytes 1000000 | tf_op jit(solution)/shard_map/multiply_late/pallas_call | solution.py:345
  54.5 0.8 %collective-permute-done.13.refs_0_ = bf16[2320,128]{1,0:T(8,128)(2,1)S(1)} collective-permute-done((bf16[2320,128]{1,0:T(8,128)(2,1)S(1)}, bf16[2320,128]{1,0:T(8,128)(2,1)S(1)}, u32[]{:S(2)}, u32[]{:S(2)}) %collective-permute-start.13) | collective-permute-done | bytes 593952 | tf_op jit(solution)/shard_map/ppermute | solution.py:425
  55.3 1.0 %multiply_last.1 = (f32[73,128,128]{2,1,0:T(8,128)S(1)}, f32[1,768]{1,0:T(1,128)S(1)}) custom-call(s32[3]{0:T(128)S(1)} %pad_add_fusion.place_ref, s32[384]{0:T(512)S(1)} %get-tuple-element.28.slots_of, s32[48]{0:T(128)S(1)} %get-tuple-element.29.n_of, bf16[9280,128]{1,0:T(8,128)(2,1)S(1)} %get-tuple-element.30.y_blocks, ...), custom_call_target="tpu_custom_call", output_to_operand_aliasing={{0}: (5, {})} | custom-call | flops 100000000 | bytes 1000000 | tf_op jit(solution)/shard_map/multiply_last/pallas_call | solution.py:345
  56.4 2.7 %collective-permute-start.16 = (f32[1,768]{1,0:T(1,128)S(1)}, f32[1,768]{1,0:T(1,128)S(1)}, u32[]{:S(2)}, u32[]{:S(2)}) collective-permute-start(f32[1,768]{1,0:T(1,128)S(1)} %get-tuple-element.38.refs_1_), channel_id=1, source_target_pairs={{0,24},{8,16},{16,8},{24,0},{1,25},{9,17},{17,9},{25,1},{2,26},{10... | collective-permute-start | bytes 9224 | tf_op jit(solution)/shard_map/ppermute | solution.py:464
  59.0 0.4 collective-permute-start.15
  59.4 0.5 collective-permute-start.14
  59.9 1.0 %collective-permute-done.16.refs_4_ = f32[1,768]{1,0:T(1,128)S(1)} collective-permute-done((f32[1,768]{1,0:T(1,128)S(1)}, f32[1,768]{1,0:T(1,128)S(1)}, u32[]{:S(2)}, u32[]{:S(2)}) %collective-permute-start.16) | collective-permute-done | bytes 3104 | tf_op jit(solution)/shard_map/ppermute | solution.py:464
  60.9 1.7 %collective-permute-done.15.refs_3_ = f32[1,768]{1,0:T(1,128)S(1)} collective-permute-done((f32[1,768]{1,0:T(1,128)S(1)}, f32[1,768]{1,0:T(1,128)S(1)}, u32[]{:S(2)}, u32[]{:S(2)}) %collective-permute-start.15) | collective-permute-done | bytes 3104 | tf_op jit(solution)/shard_map/ppermute | solution.py:464
  62.6 0.4 collective-permute-done.14.refs_2_
  63.0 2.3 %scale.1 = f32[1536,768]{1,0:T(8,128)} custom-call(f32[73,128,128]{2,1,0:T(8,128)S(1)} %get-tuple-element.37.refs_0_, f32[1,768]{1,0:T(1,128)S(1)} %get-tuple-element.38.refs_1_, f32[1,768]{1,0:T(1,128)S(1)} %collective-permute-done.14.refs_2_, f32[1,768]{1,0:T(1,128)S(1)} %collective-permute-done.15.refs_3_, f32[1,768]{1,0:T(1,128)S(1)} %collective-permute-done.16.refs_4_), custom_call_target="tpu_custom_call" | custom-call | flops 10000000 | bytes 10000000 | tf_op jit(solution)/shard_map/scale/pallas_call | solution.py:391
  (2 shorter events, 0.0 us)
Async XLA Ops:
  2.9 16.7 %collective-permute-start.4 = (bf16[2320,128]{1,0:T(8,128)(2,1)}, bf16[2320,128]{1,0:T(8,128)(2,1)S(1)}, u32[]{:S(2)}, u32[]{:S(2)}) collective-permute-start(bf16[2320,128]{1,0:T(8,128)(2,1)} %compact.1.refs_0_), channel_id=1, source_target_pairs={{2,0},{0,2},{6,4},{4,6},{3,1},{1,3},{7,5},{5,7},{10,8},{8,10},{14,... | collective-permute-start | bytes 1781768 | tf_op jit(solution)/shard_map/ppermute | solution.py:421
  5.7 14.6 %collective-permute-start.3 = (bf16[2320,128]{1,0:T(8,128)(2,1)}, bf16[2320,128]{1,0:T(8,128)(2,1)S(1)}, u32[]{:S(2)}, u32[]{:S(2)}) collective-permute-start(bf16[2320,128]{1,0:T(8,128)(2,1)} %compact.1.refs_0_), channel_id=1, source_target_pairs={{4,2},{2,4},{5,3},{3,5},{12,10},{10,12},{13,11},{11,13},{20,18},{1... | collective-permute-start | bytes 1781768 | tf_op jit(solution)/shard_map/ppermute | solution.py:421
  6.4 15.5 %collective-permute-start.9 = (bf16[2320,128]{1,0:T(8,128)(2,1)}, bf16[2320,128]{1,0:T(8,128)(2,1)}, u32[]{:S(2)}, u32[]{:S(2)}) collective-permute-start(bf16[2320,128]{1,0:T(8,128)(2,1)} %compact.1.refs_0_), channel_id=1, source_target_pairs={{0,16},{8,24},{16,0},{24,8},{1,17},{9,25},{17,1},{25,9},{2,18},{10... | collective-permute-start | bytes 1781768 | tf_op jit(solution)/shard_map/ppermute | solution.py:433
  8.1 13.8 %collective-permute-start.2 = (bf16[2320,128]{1,0:T(8,128)(2,1)}, bf16[2320,128]{1,0:T(8,128)(2,1)S(1)}, u32[]{:S(2)}, u32[]{:S(2)}) collective-permute-start(bf16[2320,128]{1,0:T(8,128)(2,1)} %compact.1.refs_0_), channel_id=1, source_target_pairs={{0,1},{1,0},{2,3},{3,2},{4,5},{5,4},{6,7},{7,6},{8,9},{9,8},{10,11... | collective-permute-start | bytes 1781768 | tf_op jit(solution)/shard_map/ppermute | solution.py:425
  8.1 16.1 %collective-permute-start = (bf16[2320,128]{1,0:T(8,128)(2,1)}, bf16[2320,128]{1,0:T(8,128)(2,1)}, u32[]{:S(2)}, u32[]{:S(2)}) collective-permute-start(bf16[2320,128]{1,0:T(8,128)(2,1)} %compact.1.refs_0_), channel_id=1, source_target_pairs={{0,8},{8,0},{16,24},{24,16},{1,9},{9,1},{17,25},{25,17},{2,10},{10... | collective-permute-start | bytes 1781768 | tf_op jit(solution)/shard_map/ppermute | solution.py:433
  19.6 11.8 %collective-permute-start.7 = (bf16[2320,128]{1,0:T(8,128)(2,1)S(1)}, bf16[2320,128]{1,0:T(8,128)(2,1)S(1)}, u32[]{:S(2)}, u32[]{:S(2)}) collective-permute-start(bf16[2320,128]{1,0:T(8,128)(2,1)S(1)} %collective-permute-done.4.refs_4_.refs_3_), channel_id=1, source_target_pairs={{4,2},{2,4},{5,3},{3,5},{12,10},{10,12},{13,11},{11,13},{20,18},{1... | collective-permute-start | bytes 1781768 | tf_op jit(solution)/shard_map/ppermute | solution.py:421
  20.3 18.2 %collective-permute-start.8 = (bf16[2320,128]{1,0:T(8,128)(2,1)S(1)}, bf16[2320,128]{1,0:T(8,128)(2,1)S(1)}, u32[]{:S(2)}, u32[]{:S(2)}) collective-permute-start(bf16[2320,128]{1,0:T(8,128)(2,1)S(1)} %collective-permute-done.3.refs_2_), channel_id=1, source_target_pairs={{2,0},{4,6},{3,1},{5,7},{10,8},{12,14},{11,9},{13,15},{18,16},{20,... | collective-permute-start | bytes 1781768 | tf_op jit(solution)/shard_map/ppermute | solution.py:421
  21.9 16.8 %collective-permute-start.6 = (bf16[2320,128]{1,0:T(8,128)(2,1)S(1)}, bf16[2320,128]{1,0:T(8,128)(2,1)S(1)}, u32[]{:S(2)}, u32[]{:S(2)}) collective-permute-start(bf16[2320,128]{1,0:T(8,128)(2,1)S(1)} %collective-permute-done.4.refs_4_.refs_3_), channel_id=1, source_target_pairs={{0,1},{1,0},{2,3},{3,2},{4,5},{5,4},{6,7},{7,6},{8,9},{9,8},{10,11... | collective-permute-start | bytes 1781768 | tf_op jit(solution)/shard_map/ppermute | solution.py:425
  21.9 17.4 %collective-permute-start.5 = (bf16[2320,128]{1,0:T(8,128)(2,1)S(1)}, bf16[2320,128]{1,0:T(8,128)(2,1)S(1)}, u32[]{:S(2)}, u32[]{:S(2)}) collective-permute-start(bf16[2320,128]{1,0:T(8,128)(2,1)S(1)} %collective-permute-done.3.refs_2_), channel_id=1, source_target_pairs={{2,3},{3,2},{4,5},{5,4},{10,11},{11,10},{12,13},{13,12},{18,19},{1... | collective-permute-start | bytes 1781768 | tf_op jit(solution)/shard_map/ppermute | solution.py:425
  24.3 15.3 %collective-permute-start.1 = (bf16[2320,128]{1,0:T(8,128)(2,1)}, bf16[2320,128]{1,0:T(8,128)(2,1)S(1)}, u32[]{:S(2)}, u32[]{:S(2)}) collective-permute-start(bf16[2320,128]{1,0:T(8,128)(2,1)} %collective-permute-done.refs_1_), channel_id=1, source_target_pairs={{0,16},{8,24},{16,0},{24,8},{1,17},{9,25},{17,1},{25,9},{2,18},{10... | collective-permute-start | bytes 1781768 | tf_op jit(solution)/shard_map/ppermute | solution.py:437
  24.7 1.1 %copy-start = (bf16[2320,128]{1,0:T(8,128)(2,1)S(1)}, bf16[2320,128]{1,0:T(8,128)(2,1)}, u32[]{:S(2)}) copy-start(bf16[2320,128]{1,0:T(8,128)(2,1)} %compact.1.refs_0_) | copy-start | bytes 1781764
  31.4 20.0 %collective-permute-start.12 = (bf16[2320,128]{1,0:T(8,128)(2,1)S(1)}, bf16[2320,128]{1,0:T(8,128)(2,1)S(1)}, u32[]{:S(2)}, u32[]{:S(2)}) collective-permute-start(bf16[2320,128]{1,0:T(8,128)(2,1)S(1)} %collective-permute-done.7.refs_6_), channel_id=1, source_target_pairs={{2,0},{4,6},{3,1},{5,7},{10,8},{12,14},{11,9},{13,15},{18,16},{20,... | collective-permute-start | bytes 1781768 | tf_op jit(solution)/shard_map/ppermute | solution.py:421
  38.6 2.1 %collective-permute-start.10 = (bf16[1168,128]{1,0:T(8,128)(2,1)S(1)}, bf16[1168,128]{1,0:T(8,128)(2,1)S(1)}, u32[]{:S(2)}, u32[]{:S(2)}) collective-permute-start(bf16[1168,128]{1,0:T(8,128)(2,1)S(1)} %slice.8), channel_id=1, source_target_pairs={{0,1},{1,0},{2,3},{3,2},{4,5},{5,4},{6,7},{7,6},{8,9},{9,8},{10,11... | collective-permute-start | bytes 897032 | tf_op jit(solution)/shard_map/ppermute | solution.py:425
  38.8 2.0 %collective-permute-start.11 = (bf16[1152,128]{1,0:T(8,128)(2,1)S(1)}, bf16[1152,128]{1,0:T(8,128)(2,1)S(1)}, u32[]{:S(2)}, u32[]{:S(2)}) collective-permute-start(bf16[1152,128]{1,0:T(8,128)(2,1)S(1)} %slice.9), channel_id=1, source_target_pairs={{0,1},{1,0},{2,3},{3,2},{4,5},{5,4},{6,7},{7,6},{8,9},{9,8},{10,11... | collective-permute-start | bytes 884744 | tf_op jit(solution)/shard_map/ppermute | solution.py:425
  51.4 3.9 %collective-permute-start.13 = (bf16[2320,128]{1,0:T(8,128)(2,1)S(1)}, bf16[2320,128]{1,0:T(8,128)(2,1)S(1)}, u32[]{:S(2)}, u32[]{:S(2)}) collective-permute-start(bf16[2320,128]{1,0:T(8,128)(2,1)S(1)} %collective-permute-done.12.refs_0_), channel_id=1, source_target_pairs={{0,1},{1,0},{6,7},{7,6},{8,9},{9,8},{14,15},{15,14},{16,17},{17,16... | collective-permute-start | bytes 1781768 | tf_op jit(solution)/shard_map/ppermute | solution.py:425
  56.4 4.6 %collective-permute-start.16 = (f32[1,768]{1,0:T(1,128)S(1)}, f32[1,768]{1,0:T(1,128)S(1)}, u32[]{:S(2)}, u32[]{:S(2)}) collective-permute-start(f32[1,768]{1,0:T(1,128)S(1)} %get-tuple-element.38.refs_1_), channel_id=1, source_target_pairs={{0,24},{8,16},{16,8},{24,0},{1,25},{9,17},{17,9},{25,1},{2,26},{10... | collective-permute-start | bytes 9224 | tf_op jit(solution)/shard_map/ppermute | solution.py:464
  59.0 3.6 %collective-permute-start.15 = (f32[1,768]{1,0:T(1,128)S(1)}, f32[1,768]{1,0:T(1,128)S(1)}, u32[]{:S(2)}, u32[]{:S(2)}) collective-permute-start(f32[1,768]{1,0:T(1,128)S(1)} %get-tuple-element.38.refs_1_), channel_id=1, source_target_pairs={{0,16},{8,24},{16,0},{24,8},{1,17},{9,25},{17,1},{25,9},{2,18},{10... | collective-permute-start | bytes 9224 | tf_op jit(solution)/shard_map/ppermute | solution.py:464
  59.4 3.6 %collective-permute-start.14 = (f32[1,768]{1,0:T(1,128)S(1)}, f32[1,768]{1,0:T(1,128)S(1)}, u32[]{:S(2)}, u32[]{:S(2)}) collective-permute-start(f32[1,768]{1,0:T(1,128)S(1)} %get-tuple-element.38.refs_1_), channel_id=1, source_target_pairs={{0,8},{8,0},{16,24},{24,16},{1,9},{9,1},{17,25},{25,17},{2,10},{10... | collective-permute-start | bytes 9224 | tf_op jit(solution)/shard_map/ppermute | solution.py:464

commit v3 on v2

--- a/solution.py
+++ b/solution.py
@@ -24,18 +24,14 @@
 SMALL = pl.CostEstimate(flops=10**8, bytes_accessed=10**6, transcendentals=0)
 
 
-def compact_kernel(mask_ref, sim_ref, out_ref, slots, places, in_sems, out_sems):
+def compact_kernel(mask_ref, sim_ref, out_ref, places, sems):
     nb_cols, nb_rows = mask_ref.shape
 
-    def slot_rows(ref, slot):
-        return ref.at[pl.ds(pl.multiple_of(HEAD + slot * BLK, HEAD), BLK), :]
-
-    def copy_in(slot, i, k):
+    def block_copy(slot, i, k):
         block = sim_ref.at[pl.ds(pl.multiple_of(i * BLK, BLK), BLK), pl.ds(k * BLK, BLK)]
-        return pltpu.make_async_copy(block, slot_rows(slots, slot), in_sems.at[slot])
-
-    def copy_out(slot):
-        return pltpu.make_async_copy(slot_rows(slots, slot), slot_rows(out_ref, slot), out_sems.at[slot])
+        return pltpu.make_async_copy(
+            block, out_ref.at[pl.ds(pl.multiple_of(HEAD + slot * BLK, HEAD), BLK), :], sems.at[slot]
+        )
 
     def scan(i, count):
         for k in range(nb_cols):
@@ -43,7 +39,7 @@
 
             @pl.when(here != 0)
             def _():
-                copy_in(count, i, k).start()
+                block_copy(count, i, k).start()
                 places[count] = i * 8 + k
 
             count = count + here
@@ -56,36 +52,22 @@
     header = jnp.where(lane == SLOTS, count, 0)
     for slot in range(SLOTS):
         header = jnp.where(lane == slot, places[slot], header)
-    slots[0:HEAD, :] = header.astype(jnp.float32).astype(slots.dtype)
-    header_out = pltpu.make_async_copy(slots.at[pl.ds(0, HEAD), :], out_ref.at[pl.ds(0, HEAD), :], out_sems.at[SLOTS])
-    header_out.start()
-
-    def pass_on(slot, carry):
-        copy_in(slot, 0, 0).wait()
-        copy_out(slot).start()
-        return carry
-
-    def finish(slot, carry):
-        copy_out(slot).wait()
-        return carry
-
-    lax.fori_loop(0, count, pass_on, 0)
-    lax.fori_loop(0, count, finish, 0)
-    header_out.wait()
+    out_ref[0:HEAD, :] = header.astype(jnp.float32).astype(out_ref.dtype)
+
+    def wait(slot, carry):
+        block_copy(slot, 0, 0).wait()
+        return carry
+
+    lax.fori_loop(0, count, wait, 0)
 
 
 def compact(mask, similarity):
     return pl.pallas_call(
         compact_kernel,
-        out_shape=jax.ShapeDtypeStruct((ROWS, BLK), similarity.dtype),
+        out_shape=pltpu.VMEM((ROWS, BLK), similarity.dtype),
         in_specs=[SMEM, ANY],
-        out_specs=ANY,
-        scratch_shapes=[
-            pltpu.VMEM((ROWS, BLK), similarity.dtype),
-            pltpu.SMEM((SLOTS,), jnp.int32),
-            pltpu.SemaphoreType.DMA((SLOTS,)),
-            pltpu.SemaphoreType.DMA((SLOTS + 1,)),
-        ],
+        out_specs=VMEM,
+        scratch_shapes=[pltpu.SMEM((SLOTS,), jnp.int32), pltpu.SemaphoreType.DMA((SLOTS,))],
         cost_estimate=pl.CostEstimate(flops=0, bytes_accessed=2 * SHARE * BLK * 2, transcendentals=0),
         name="compact",
     )(mask, similarity)
@@ -414,19 +396,16 @@
     place = jnp.stack([r, c, l]).astype(jnp.int32)
     mask = block_mask.T
 
-    def holders(tile, step):
-        return [i for i in range(n_col) if 0 <= tile(i, step) < n_col]
-
-    def hop(x, tile, step):
-        return lax.ppermute(x, "col", [(tile(i, 1), i) for i in holders(tile, step)])
-
-    def sibling(x, cols):
-        pairs = [(2 * i + layer, 2 * i + 1 - layer) for i in cols for layer in range(2)]
-        return lax.ppermute(x, ("col", "layer"), pairs)
+    def hop(x, tile):
+        targets = [tile(i, 1) if 0 <= tile(i, 1) < n_col else i for i in range(n_col)]
+        return lax.ppermute(x, "col", list(enumerate(targets)))
+
+    def sibling(x):
+        return lax.ppermute(x, "layer", [(0, 1), (1, 0)])
 
     own = compact(mask, similarity)
-    even = hop(own, even_tile, 1)
-    odd = hop(own, odd_tile, 1)
+    even = hop(own, even_tile)
+    odd = hop(own, odd_tile)
     near = [m for m in range(n_row) if m.bit_count() <= 1]
     ys = [own] + [None] * (n_row - 1)
     for m in near[1:]:
@@ -435,25 +414,25 @@
         if ys[m] is None:
             bit = 1 << (m.bit_length() - 1)
             ys[m] = lax.ppermute(ys[m ^ bit], "row", [(s, s ^ bit) for s in range(n_row)])
-    first_xs = [sibling(own, range(n_col)), even]
+    first_xs = [sibling(own), even]
     shares = [((0, False, True, True), first_xs[0]), ((1, True, False, False), odd), ((1, False, False, True), even)]
     first_xs[1], _ = lax.optimization_barrier((even, odd))
     acc, sums, y_blocks = multiply_first(place, near, ys, first_xs, n_row, n_col, nb_rows, nb_cols)
     for step in range(1, n_col - 2):
-        shares.append(((step, True, True, False), sibling(odd, holders(odd_tile, step))))
-        shares.append(((step, False, True, False), sibling(even, holders(even_tile, step))))
-        odd, even = hop(even, odd_tile, step + 1), hop(odd, even_tile, step + 1)
+        shares.append(((step, True, True, False), sibling(odd)))
+        shares.append(((step, False, True, False), sibling(even)))
+        odd, even = hop(even, odd_tile), hop(odd, even_tile)
         shares += [((step + 1, True, False, False), odd), ((step + 1, False, False, False), even)]
     odd, sums = lax.optimization_barrier((odd, sums))
-    last = hop(odd, even_tile, n_col - 1)
+    last = hop(odd, even_tile)
     arrived = jnp.where(jnp.logical_or(c == 0, c == n_col - 1), even, odd)
-    halves = [sibling(arrived[:FIRST_ROWS], range(n_col)), sibling(arrived[FIRST_ROWS:], range(n_col))]
+    halves = [sibling(arrived[:FIRST_ROWS]), sibling(arrived[FIRST_ROWS:])]
     x_kinds, xs = zip(*shares)
     acc, sums, y_blocks, slots_of, n_of = multiply_second(
         place, near, ys, xs, x_kinds, halves, acc, sums, y_blocks, n_col, nb_rows, nb_cols
     )
     last, sums = lax.optimization_barrier((last, sums))
-    other = sibling(last, holders(even_tile, n_col - 1))
+    other = sibling(last)
     kinds = [(n_col - 1, False, False)]
     sizes = n_col, nb_rows, nb_cols
     acc, sums = multiply_late(place, slots_of, n_of, y_blocks, [last], kinds, acc, sums, False, *sizes)

time: 65.9 us -> 61.6 us (0.935)
  waiting for transfers between devices: 28.8 us -> 20.1 us
  starting transfers between devices: 17.2 us -> 24.5 us
  Pallas kernels: 17.9 us -> 16 us
  local copies, waits for them, and re-layouts: 1.11 us -> 0.04 us
    ppermute x11, waiting for transfers between devices: 23.7 us -> 14.8 us  [the longest x5 14 us: hop(): return lax.ppermute(x, 'col', list(enumerate(targets)))]
    ppermute x11, starting transfers between devices: 10 us -> 16.4 us  [the longest x5 15.2 us: hop(): return lax.ppermute(x, 'col', list(enumerate(targets)))]
    ppermute x1, waiting for transfers between devices: 0.23 us -> 2.27 us  [body(): lax.ppermute(ys[m ^ bit], 'row', [(s, s ^ bit) for s in range(n_row)])]
    ppermute x2, waiting for transfers between devices: 1.89 us -> 0.01 us  [body(): ys[m] = lax.ppermute(own, 'row', [(s, s ^ m) for s in range(n_row)])]
    ppermute x1, starting transfers between devices: 0.39 us -> 1.61 us  [body(): lax.ppermute(ys[m ^ bit], 'row', [(s, s ^ bit) for s in range(n_row)])]
    unnamed x2 -> x0, local copies, waits for them, and re-layouts: 1.07 us -> none
    pallas_call x1, Pallas kernels: 2.88 us -> 2.01 us  [compact(): pl.pallas_call(compact_kernel, out_shape=pltpu.VMEM((ROWS, BLK), similari...]
  transfers between devices with their start and end apart: 17 -> 17, of which waited for: 11 -> 8; matrix products, arithmetic and copies ran while one was open for 0% -> 0% of each run, Pallas kernels for 18% -> 18%
where the time goes in v3:
time: 61.6 us; the launch traced here: 60.9 us
  starting transfers between devices  24.5 us (40%)
  waiting for transfers between devices  20.1 us (33%)
  Pallas kernels  16 us (26%)
    ppermute x5, starting transfers between devices, hop(): return lax.ppermute(x, 'col', list(enumerate(targets)))  15.2 us
    ppermute x5, waiting for transfers between devices, hop(): return lax.ppermute(x, 'col', list(enumerate(targets)))  14 us
    pallas_call x1, Pallas kernels, multiply_first(): pl.pallas_call(functools.partial(first_kernel, near, n_col, nb_rows, nb_c...  5.16 us
    pallas_call x1, Pallas kernels, multiply_second(): pl.pallas_call(functools.partial(second_kernel, near, n_row, n_col, nb_ro...  4.44 us
    ppermute x3, starting transfers between devices, body(): lax.ppermute(sums, 'row', [(s, s ^ m) for s in range(n_row)])  3.61 us
    ppermute x3, waiting for transfers between devices, body(): lax.ppermute(sums, 'row', [(s, s ^ m) for s in range(n_row)])  3 us
    ppermute x2, starting transfers between devices, body(): ys[m] = lax.ppermute(own, 'row', [(s, s ^ m) for s in range(n_row)])  2.91 us
    pallas_call x1, Pallas kernels, scale(): pl.pallas_call(functools.partial(scale_kernel, scaling, nb_rows, nb_cols)...  2.31 us
  transfers between devices with their start and end apart: 17, of which 8 were waited for; matrix products, arithmetic and copies ran while one was open for 0% of the time, Pallas kernels for 18%

profile of v3, /device:TPU:0, one launch (start us, length us, event | category | flops | bytes accessed | tf_op | source)
XLA Modules:
  0.0 60.9 jit_solution(4851793571609523549)
XLA Ops:
  0.0 2.0 %compact.1.refs_0_ = bf16[2320,128]{1,0:T(8,128)(2,1)S(1)} custom-call(s32[6,12]{1,0:T(8,128)} %bitcast.4, bf16[1536,768]{1,0:T(8,128)(2,1)} %sim_ref.1), custom_call_target="tpu_custom_call" | custom-call | bytes 1179648 | tf_op jit(solution)/shard_map/compact/pallas_call | solution.py:65
  2.0 3.2 %collective-permute-start.4 = (bf16[2320,128]{1,0:T(8,128)(2,1)S(1)}, bf16[2320,128]{1,0:T(8,128)(2,1)S(1)}, u32[]{:S(2)}, u32[]{:S(2)}) collective-permute-start(bf16[2320,128]{1,0:T(8,128)(2,1)S(1)} %compact.1.refs_0_), channel_id=1, source_target_pairs={{0,2},{2,0},{4,6},{6,4},{1,3},{3,1},{5,7},{7,5},{8,10},{10,8},{12,... | collective-permute-start | bytes 1781768 | tf_op jit(solution)/shard_map/ppermute | solution.py:401
  5.2 1.5 %collective-permute-start.3 = (bf16[2320,128]{1,0:T(8,128)(2,1)S(1)}, bf16[2320,128]{1,0:T(8,128)(2,1)}, u32[]{:S(2)}, u32[]{:S(2)}) collective-permute-start(bf16[2320,128]{1,0:T(8,128)(2,1)S(1)} %compact.1.refs_0_), channel_id=1, source_target_pairs={{0,0},{2,4},{4,2},{6,6},{1,1},{3,5},{5,3},{7,7},{8,8},{10,12},{12,... | collective-permute-start | bytes 1781768 | tf_op jit(solution)/shard_map/ppermute | solution.py:401
  6.7 1.4 %collective-permute-start.9 = (bf16[2320,128]{1,0:T(8,128)(2,1)S(1)}, bf16[2320,128]{1,0:T(8,128)(2,1)}, u32[]{:S(2)}, u32[]{:S(2)}) collective-permute-start(bf16[2320,128]{1,0:T(8,128)(2,1)S(1)} %compact.1.refs_0_), channel_id=1, source_target_pairs={{0,16},{8,24},{16,0},{24,8},{1,17},{9,25},{17,1},{25,9},{2,18},{10... | collective-permute-start | bytes 1781768 | tf_op jit(solution)/shard_map/ppermute | solution.py:412
  8.1 0.0 collective-permute-start.2
  8.1 1.5 %collective-permute-start = (bf16[2320,128]{1,0:T(8,128)(2,1)S(1)}, bf16[2320,128]{1,0:T(8,128)(2,1)}, u32[]{:S(2)}, u32[]{:S(2)}) collective-permute-start(bf16[2320,128]{1,0:T(8,128)(2,1)S(1)} %compact.1.refs_0_), channel_id=1, source_target_pairs={{0,8},{8,0},{16,24},{24,16},{1,9},{9,1},{17,25},{25,17},{2,10},{10... | collective-permute-start | bytes 1781768 | tf_op jit(solution)/shard_map/ppermute | solution.py:412
  9.6 9.0 %collective-permute-done.4.refs_4_.refs_3_ = bf16[2320,128]{1,0:T(8,128)(2,1)S(1)} collective-permute-done((bf16[2320,128]{1,0:T(8,128)(2,1)S(1)}, bf16[2320,128]{1,0:T(8,128)(2,1)S(1)}, u32[]{:S(2)}, u32[]{:S(2)}) %collective-permute-start.4) | collective-permute-done | bytes 593952 | tf_op jit(solution)/shard_map/ppermute | solution.py:401
  18.6 0.7 %collective-permute-start.7 = (bf16[2320,128]{1,0:T(8,128)(2,1)S(1)}, bf16[2320,128]{1,0:T(8,128)(2,1)S(1)}, u32[]{:S(2)}, u32[]{:S(2)}) collective-permute-start(bf16[2320,128]{1,0:T(8,128)(2,1)S(1)} %collective-permute-done.4.refs_4_.refs_3_), channel_id=1, source_target_pairs={{0,0},{2,4},{4,2},{6,6},{1,1},{3,5},{5,3},{7,7},{8,8},{10,12},{12,... | collective-permute-start | bytes 1781768 | tf_op jit(solution)/shard_map/ppermute | solution.py:401
  19.3 0.0 collective-permute-done.3.refs_2_
  19.3 4.5 %collective-permute-start.8 = (bf16[2320,128]{1,0:T(8,128)(2,1)}, bf16[2320,128]{1,0:T(8,128)(2,1)S(1)}, u32[]{:S(2)}, u32[]{:S(2)}) collective-permute-start(bf16[2320,128]{1,0:T(8,128)(2,1)} %collective-permute-done.3.refs_2_), channel_id=1, source_target_pairs={{0,2},{2,0},{4,6},{6,4},{1,3},{3,1},{5,7},{7,5},{8,10},{10,8},{12,... | collective-permute-start | bytes 1781768 | tf_op jit(solution)/shard_map/ppermute | solution.py:401
  23.8 0.1 pad_add_fusion.place_ref
  23.9 0.0 collective-permute-done.9.refs_2_
  23.9 0.0 collective-permute-start.6
  23.9 0.0 collective-permute-done.2.refs_3_.refs_1_
  23.9 0.5 collective-permute-start.5
  24.4 0.0 collective-permute-done.refs_1_
  24.4 1.6 %collective-permute-start.1 = (bf16[2320,128]{1,0:T(8,128)(2,1)}, bf16[2320,128]{1,0:T(8,128)(2,1)S(1)}, u32[]{:S(2)}, u32[]{:S(2)}) collective-permute-start(bf16[2320,128]{1,0:T(8,128)(2,1)} %collective-permute-done.refs_1_), channel_id=1, source_target_pairs={{0,16},{8,24},{16,0},{24,8},{1,17},{9,25},{17,1},{25,9},{2,18},{10... | collective-permute-start | bytes 1781768 | tf_op jit(solution)/shard_map/ppermute | solution.py:416
  26.0 5.2 %multiply_first.1 = (f32[73,128,128]{2,1,0:T(8,128)S(1)}, f32[7,8,128]{2,1,0:T(8,128)S(1)}, bf16[9280,128]{1,0:T(8,128)(2,1)S(1)}) custom-call(s32[3]{0:T(128)S(1)} %pad_add_fusion.place_ref, bf16[2320,128]{1,0:T(8,128)(2,1)S(1)} %compact.1.refs_0_, bf16[2320,128]{1,0:T(8,128)(2,1)} %collective-permute-done.refs_1_, ...), custom_call_target="tpu_custom_call" | custom-call | flops 100000000 | bytes 1000000 | tf_op jit(solution)/shard_map/multiply_first/pallas_call | solution.py:226
  31.2 0.0 collective-permute-done.7.refs_6_
  31.2 5.4 %collective-permute-start.12 = (bf16[2320,128]{1,0:T(8,128)(2,1)S(1)}, bf16[2320,128]{1,0:T(8,128)(2,1)S(1)}, u32[]{:S(2)}, u32[]{:S(2)}) collective-permute-start(bf16[2320,128]{1,0:T(8,128)(2,1)S(1)} %collective-permute-done.7.refs_6_), channel_id=1, source_target_pairs={{0,2},{2,0},{4,6},{6,4},{1,3},{3,1},{5,7},{7,5},{8,10},{10,8},{12,... | collective-permute-start | bytes 1781768 | tf_op jit(solution)/shard_map/ppermute | solution.py:401
  36.6 0.4 collective-permute-done.8.refs_7_
  37.0 0.1 broadcast_select_fusion
  37.1 0.1 collective-permute-start.10
  37.2 0.0 collective-permute-done.6.refs_5_
  37.2 0.6 collective-permute-start.11
  37.8 0.0 collective-permute-done.5.refs_4_
  37.8 2.3 %collective-permute-done.1.refs_0_ = bf16[2320,128]{1,0:T(8,128)(2,1)S(1)} collective-permute-done((bf16[2320,128]{1,0:T(8,128)(2,1)}, bf16[2320,128]{1,0:T(8,128)(2,1)S(1)}, u32[]{:S(2)}, u32[]{:S(2)}) %collective-permute-start.1) | collective-permute-done | bytes 593952 | tf_op jit(solution)/shard_map/ppermute | solution.py:416
  40.0 0.0 collective-permute-done.11.refs_9_
  40.0 0.0 collective-permute-done.10.refs_8_
  40.0 4.4 %multiply_second.1 = (f32[73,128,128]{2,1,0:T(8,128)S(1)}, f32[7,8,128]{2,1,0:T(8,128)S(1)}, bf16[9280,128]{1,0:T(8,128)(2,1)S(1)}, s32[384]{0:T(512)S(1)}, s32[48]{0:T(128)S(1)}) custom-call(s32[3]{0:T(128)S(1)} %pad_add_fusion.place_ref, ...), custom_call_target="tpu_custom_call", output_to_operand_aliasing={{0}: (11, {}), {1}: (12, {}), {2}: (13, {})} | custom-call | flops 100000000 | bytes 1000000 | tf_op jit(solution)/shard_map/multiply_second/pallas_call | solution.py:290
  44.5 4.5 %collective-permute-done.12.refs_0_ = bf16[2320,128]{1,0:T(8,128)(2,1)S(1)} collective-permute-done((bf16[2320,128]{1,0:T(8,128)(2,1)S(1)}, bf16[2320,128]{1,0:T(8,128)(2,1)S(1)}, u32[]{:S(2)}, u32[]{:S(2)}) %collective-permute-start.12) | collective-permute-done | bytes 593952 | tf_op jit(solution)/shard_map/ppermute | solution.py:401
  49.0 0.0 collective-permute-start.13
  49.0 1.2 %multiply_late.1 = (f32[73,128,128]{2,1,0:T(8,128)S(1)}, f32[7,8,128]{2,1,0:T(8,128)S(1)}) custom-call(s32[3]{0:T(128)S(1)} %pad_add_fusion.place_ref, s32[384]{0:T(512)S(1)} %get-tuple-element.28.slots_of, s32[48]{0:T(128)S(1)} %get-tuple-element.29.n_of, bf16[9280,128]{1,0:T(8,128)(2,1)S(1)} %get-tuple-element.30.y_blocks, ...), custom_call_target="tpu_custom_call", output_to_operand_aliasing={{0}: (5, {})} | custom-call | flops 100000000 | bytes 1000000 | tf_op jit(solution)/shard_map/multiply_late/pallas_call | solution.py:327
  50.2 0.8 %collective-permute-done.13.refs_0_ = bf16[2320,128]{1,0:T(8,128)(2,1)S(1)} collective-permute-done((bf16[2320,128]{1,0:T(8,128)(2,1)S(1)}, bf16[2320,128]{1,0:T(8,128)(2,1)S(1)}, u32[]{:S(2)}, u32[]{:S(2)}) %collective-permute-start.13) | collective-permute-done | bytes 593952 | tf_op jit(solution)/shard_map/ppermute | solution.py:404
  51.0 0.9 %multiply_last.1 = (f32[73,128,128]{2,1,0:T(8,128)S(1)}, f32[1,768]{1,0:T(1,128)S(1)}) custom-call(s32[3]{0:T(128)S(1)} %pad_add_fusion.place_ref, s32[384]{0:T(512)S(1)} %get-tuple-element.28.slots_of, s32[48]{0:T(128)S(1)} %get-tuple-element.29.n_of, bf16[9280,128]{1,0:T(8,128)(2,1)S(1)} %get-tuple-element.30.y_blocks, ...), custom_call_target="tpu_custom_call", output_to_operand_aliasing={{0}: (5, {})} | custom-call | flops 100000000 | bytes 1000000 | tf_op jit(solution)/shard_map/multiply_last/pallas_call | solution.py:327
  52.0 2.7 %collective-permute-start.16 = (f32[1,768]{1,0:T(1,128)S(1)}, f32[1,768]{1,0:T(1,128)S(1)}, u32[]{:S(2)}, u32[]{:S(2)}) collective-permute-start(f32[1,768]{1,0:T(1,128)S(1)} %get-tuple-element.38.refs_1_), channel_id=1, source_target_pairs={{0,24},{8,16},{16,8},{24,0},{1,25},{9,17},{17,9},{25,1},{2,26},{10... | collective-permute-start | bytes 9224 | tf_op jit(solution)/shard_map/ppermute | solution.py:443
  54.6 0.4 collective-permute-start.15
  55.0 0.6 collective-permute-start.14
  55.6 1.0 %collective-permute-done.16.refs_4_ = f32[1,768]{1,0:T(1,128)S(1)} collective-permute-done((f32[1,768]{1,0:T(1,128)S(1)}, f32[1,768]{1,0:T(1,128)S(1)}, u32[]{:S(2)}, u32[]{:S(2)}) %collective-permute-start.16) | collective-permute-done | bytes 3104 | tf_op jit(solution)/shard_map/ppermute | solution.py:443
  56.6 1.7 %collective-permute-done.15.refs_3_ = f32[1,768]{1,0:T(1,128)S(1)} collective-permute-done((f32[1,768]{1,0:T(1,128)S(1)}, f32[1,768]{1,0:T(1,128)S(1)}, u32[]{:S(2)}, u32[]{:S(2)}) %collective-permute-start.15) | collective-permute-done | bytes 3104 | tf_op jit(solution)/shard_map/ppermute | solution.py:443
  58.2 0.4 collective-permute-done.14.refs_2_
  58.6 2.3 %scale.1 = f32[1536,768]{1,0:T(8,128)} custom-call(f32[73,128,128]{2,1,0:T(8,128)S(1)} %get-tuple-element.37.refs_0_, f32[1,768]{1,0:T(1,128)S(1)} %get-tuple-element.38.refs_1_, f32[1,768]{1,0:T(1,128)S(1)} %collective-permute-done.14.refs_2_, f32[1,768]{1,0:T(1,128)S(1)} %collective-permute-done.15.refs_3_, f32[1,768]{1,0:T(1,128)S(1)} %collective-permute-done.16.refs_4_), custom_call_target="tpu_custom_call" | custom-call | flops 10000000 | bytes 10000000 | tf_op jit(solution)/shard_map/scale/pallas_call | solution.py:373
  (2 shorter events, 0.0 us)
Async XLA Ops:
  2.0 16.6 %collective-permute-start.4 = (bf16[2320,128]{1,0:T(8,128)(2,1)S(1)}, bf16[2320,128]{1,0:T(8,128)(2,1)S(1)}, u32[]{:S(2)}, u32[]{:S(2)}) collective-permute-start(bf16[2320,128]{1,0:T(8,128)(2,1)S(1)} %compact.1.refs_0_), channel_id=1, source_target_pairs={{0,2},{2,0},{4,6},{6,4},{1,3},{3,1},{5,7},{7,5},{8,10},{10,8},{12,... | collective-permute-start | bytes 1781768 | tf_op jit(solution)/shard_map/ppermute | solution.py:401
  5.2 14.1 %collective-permute-start.3 = (bf16[2320,128]{1,0:T(8,128)(2,1)S(1)}, bf16[2320,128]{1,0:T(8,128)(2,1)}, u32[]{:S(2)}, u32[]{:S(2)}) collective-permute-start(bf16[2320,128]{1,0:T(8,128)(2,1)S(1)} %compact.1.refs_0_), channel_id=1, source_target_pairs={{0,0},{2,4},{4,2},{6,6},{1,1},{3,5},{5,3},{7,7},{8,8},{10,12},{12,... | collective-permute-start | bytes 1781768 | tf_op jit(solution)/shard_map/ppermute | solution.py:401
  6.7 17.2 %collective-permute-start.9 = (bf16[2320,128]{1,0:T(8,128)(2,1)S(1)}, bf16[2320,128]{1,0:T(8,128)(2,1)}, u32[]{:S(2)}, u32[]{:S(2)}) collective-permute-start(bf16[2320,128]{1,0:T(8,128)(2,1)S(1)} %compact.1.refs_0_), channel_id=1, source_target_pairs={{0,16},{8,24},{16,0},{24,8},{1,17},{9,25},{17,1},{25,9},{2,18},{10... | collective-permute-start | bytes 1781768 | tf_op jit(solution)/shard_map/ppermute | solution.py:412
  8.1 15.8 %collective-permute-start.2 = (bf16[2320,128]{1,0:T(8,128)(2,1)S(1)}, bf16[2320,128]{1,0:T(8,128)(2,1)S(1)}, u32[]{:S(2)}, u32[]{:S(2)}) collective-permute-start(bf16[2320,128]{1,0:T(8,128)(2,1)S(1)} %compact.1.refs_0_), channel_id=1, source_target_pairs={{0,1},{1,0},{2,3},{3,2},{4,5},{5,4},{6,7},{7,6},{8,9},{9,8},{10,11... | collective-permute-start | bytes 1781768 | tf_op jit(solution)/shard_map/ppermute | solution.py:404
  8.1 16.3 %collective-permute-start = (bf16[2320,128]{1,0:T(8,128)(2,1)S(1)}, bf16[2320,128]{1,0:T(8,128)(2,1)}, u32[]{:S(2)}, u32[]{:S(2)}) collective-permute-start(bf16[2320,128]{1,0:T(8,128)(2,1)S(1)} %compact.1.refs_0_), channel_id=1, source_target_pairs={{0,8},{8,0},{16,24},{24,16},{1,9},{9,1},{17,25},{25,17},{2,10},{10... | collective-permute-start | bytes 1781768 | tf_op jit(solution)/shard_map/ppermute | solution.py:412
  18.6 12.6 %collective-permute-start.7 = (bf16[2320,128]{1,0:T(8,128)(2,1)S(1)}, bf16[2320,128]{1,0:T(8,128)(2,1)S(1)}, u32[]{:S(2)}, u32[]{:S(2)}) collective-permute-start(bf16[2320,128]{1,0:T(8,128)(2,1)S(1)} %collective-permute-done.4.refs_4_.refs_3_), channel_id=1, source_target_pairs={{0,0},{2,4},{4,2},{6,6},{1,1},{3,5},{5,3},{7,7},{8,8},{10,12},{12,... | collective-permute-start | bytes 1781768 | tf_op jit(solution)/shard_map/ppermute | solution.py:401
  19.3 17.7 %collective-permute-start.8 = (bf16[2320,128]{1,0:T(8,128)(2,1)}, bf16[2320,128]{1,0:T(8,128)(2,1)S(1)}, u32[]{:S(2)}, u32[]{:S(2)}) collective-permute-start(bf16[2320,128]{1,0:T(8,128)(2,1)} %collective-permute-done.3.refs_2_), channel_id=1, source_target_pairs={{0,2},{2,0},{4,6},{6,4},{1,3},{3,1},{5,7},{7,5},{8,10},{10,8},{12,... | collective-permute-start | bytes 1781768 | tf_op jit(solution)/shard_map/ppermute | solution.py:401
  23.9 13.3 %collective-permute-start.6 = (bf16[2320,128]{1,0:T(8,128)(2,1)S(1)}, bf16[2320,128]{1,0:T(8,128)(2,1)S(1)}, u32[]{:S(2)}, u32[]{:S(2)}) collective-permute-start(bf16[2320,128]{1,0:T(8,128)(2,1)S(1)} %collective-permute-done.4.refs_4_.refs_3_), channel_id=1, source_target_pairs={{0,1},{1,0},{2,3},{3,2},{4,5},{5,4},{6,7},{7,6},{8,9},{9,8},{10,11... | collective-permute-start | bytes 1781768 | tf_op jit(solution)/shard_map/ppermute | solution.py:404
  23.9 13.8 %collective-permute-start.5 = (bf16[2320,128]{1,0:T(8,128)(2,1)}, bf16[2320,128]{1,0:T(8,128)(2,1)S(1)}, u32[]{:S(2)}, u32[]{:S(2)}) collective-permute-start(bf16[2320,128]{1,0:T(8,128)(2,1)} %collective-permute-done.3.refs_2_), channel_id=1, source_target_pairs={{0,1},{1,0},{2,3},{3,2},{4,5},{5,4},{6,7},{7,6},{8,9},{9,8},{10,11... | collective-permute-start | bytes 1781768 | tf_op jit(solution)/shard_map/ppermute | solution.py:404
  24.4 15.6 %collective-permute-start.1 = (bf16[2320,128]{1,0:T(8,128)(2,1)}, bf16[2320,128]{1,0:T(8,128)(2,1)S(1)}, u32[]{:S(2)}, u32[]{:S(2)}) collective-permute-start(bf16[2320,128]{1,0:T(8,128)(2,1)} %collective-permute-done.refs_1_), channel_id=1, source_target_pairs={{0,16},{8,24},{16,0},{24,8},{1,17},{9,25},{17,1},{25,9},{2,18},{10... | collective-permute-start | bytes 1781768 | tf_op jit(solution)/shard_map/ppermute | solution.py:416
  31.2 17.8 %collective-permute-start.12 = (bf16[2320,128]{1,0:T(8,128)(2,1)S(1)}, bf16[2320,128]{1,0:T(8,128)(2,1)S(1)}, u32[]{:S(2)}, u32[]{:S(2)}) collective-permute-start(bf16[2320,128]{1,0:T(8,128)(2,1)S(1)} %collective-permute-done.7.refs_6_), channel_id=1, source_target_pairs={{0,2},{2,0},{4,6},{6,4},{1,3},{3,1},{5,7},{7,5},{8,10},{10,8},{12,... | collective-permute-start | bytes 1781768 | tf_op jit(solution)/shard_map/ppermute | solution.py:401
  37.1 3.0 %collective-permute-start.10 = (bf16[1168,128]{1,0:T(8,128)(2,1)S(1)}, bf16[1168,128]{1,0:T(8,128)(2,1)S(1)}, u32[]{:S(2)}, u32[]{:S(2)}) collective-permute-start(bf16[1168,128]{1,0:T(8,128)(2,1)S(1)} %slice.8), channel_id=1, source_target_pairs={{0,1},{1,0},{2,3},{3,2},{4,5},{5,4},{6,7},{7,6},{8,9},{9,8},{10,11... | collective-permute-start | bytes 897032 | tf_op jit(solution)/shard_map/ppermute | solution.py:404
  37.2 2.8 %collective-permute-start.11 = (bf16[1152,128]{1,0:T(8,128)(2,1)S(1)}, bf16[1152,128]{1,0:T(8,128)(2,1)S(1)}, u32[]{:S(2)}, u32[]{:S(2)}) collective-permute-start(bf16[1152,128]{1,0:T(8,128)(2,1)S(1)} %slice.9), channel_id=1, source_target_pairs={{0,1},{1,0},{2,3},{3,2},{4,5},{5,4},{6,7},{7,6},{8,9},{9,8},{10,11... | collective-permute-start | bytes 884744 | tf_op jit(solution)/shard_map/ppermute | solution.py:404
  49.0 2.0 %collective-permute-start.13 = (bf16[2320,128]{1,0:T(8,128)(2,1)S(1)}, bf16[2320,128]{1,0:T(8,128)(2,1)S(1)}, u32[]{:S(2)}, u32[]{:S(2)}) collective-permute-start(bf16[2320,128]{1,0:T(8,128)(2,1)S(1)} %collective-permute-done.12.refs_0_), channel_id=1, source_target_pairs={{0,1},{1,0},{2,3},{3,2},{4,5},{5,4},{6,7},{7,6},{8,9},{9,8},{10,11... | collective-permute-start | bytes 1781768 | tf_op jit(solution)/shard_map/ppermute | solution.py:404
  52.0 4.6 %collective-permute-start.16 = (f32[1,768]{1,0:T(1,128)S(1)}, f32[1,768]{1,0:T(1,128)S(1)}, u32[]{:S(2)}, u32[]{:S(2)}) collective-permute-start(f32[1,768]{1,0:T(1,128)S(1)} %get-tuple-element.38.refs_1_), channel_id=1, source_target_pairs={{0,24},{8,16},{16,8},{24,0},{1,25},{9,17},{17,9},{25,1},{2,26},{10... | collective-permute-start | bytes 9224 | tf_op jit(solution)/shard_map/ppermute | solution.py:443
  54.6 3.6 %collective-permute-start.15 = (f32[1,768]{1,0:T(1,128)S(1)}, f32[1,768]{1,0:T(1,128)S(1)}, u32[]{:S(2)}, u32[]{:S(2)}) collective-permute-start(f32[1,768]{1,0:T(1,128)S(1)} %get-tuple-element.38.refs_1_), channel_id=1, source_target_pairs={{0,16},{8,24},{16,0},{24,8},{1,17},{9,25},{17,1},{25,9},{2,18},{10... | collective-permute-start | bytes 9224 | tf_op jit(solution)/shard_map/ppermute | solution.py:443
  55.0 3.6 %collective-permute-start.14 = (f32[1,768]{1,0:T(1,128)S(1)}, f32[1,768]{1,0:T(1,128)S(1)}, u32[]{:S(2)}, u32[]{:S(2)}) collective-permute-start(f32[1,768]{1,0:T(1,128)S(1)} %get-tuple-element.38.refs_1_), channel_id=1, source_target_pairs={{0,8},{8,0},{16,24},{24,16},{1,9},{9,1},{17,25},{25,17},{2,10},{10... | collective-permute-start | bytes 9224 | tf_op jit(solution)/shard_map/ppermute | solution.py:443

commit v4 on v3

--- a/solution.py
+++ b/solution.py
@@ -316,12 +316,13 @@
         multiply_pairs(todo, 0, x_ref, y_blocks, acc, sums)
     if is_last:
         totals = refs[3]
+        totals[...] = jnp.zeros(totals.shape, totals.dtype)
         for j in range(nb_cols):
-            totals[:, j * BLK : (j + 1) * BLK] = jnp.sum(sums[j], axis=0, keepdims=True)
+            totals[j : j + 1, :] = jnp.sum(sums[j], axis=0, keepdims=True)
 
 
 def multiply_late(place, slots_of, n_of, y_blocks, xs, x_kinds, acc, sums, is_last, n_col, nb_rows, nb_cols):
-    totals = jax.ShapeDtypeStruct((1, nb_cols * BLK), jnp.float32)
+    totals = jax.ShapeDtypeStruct((8, BLK), jnp.float32)
     same_sums = jax.ShapeDtypeStruct(sums.shape, sums.dtype)
     operands = [place, slots_of, n_of, y_blocks, *xs, acc, sums]
     return pl.pallas_call(
@@ -344,7 +345,7 @@
     total = sums[0][...]
     for other in sums[1:]:
         total = total + other[...]
-    factor = scaling / total
+    factor = scaling / total[0:nb_cols, :]
 
     def out_copy(i):
         rows = pl.ds(pl.multiple_of(i * BLK, BLK), BLK)
@@ -354,7 +355,7 @@
         for j in range(nb_cols):
             value = product[i * nb_cols + j]
             scaled[pl.ds(pl.multiple_of(i * BLK, BLK), BLK), j * BLK : (j + 1) * BLK] = (
-                value * value * factor[:, j * BLK : (j + 1) * BLK]
+                value * value * factor[j : j + 1, :]
             )
         out_copy(i).start()
         return carry

time: 61.6 us -> 61.8 us (level)
  starting transfers between devices: 24.5 us -> 25.6 us
  waiting for transfers between devices: 20.1 us -> 19 us
    ppermute x5, starting transfers between devices: 15.2 us -> 16.3 us  [hop(): return lax.ppermute(x, 'col', list(enumerate(targets)))]
    pallas_call x1, Pallas kernels: 5.16 us -> 4.33 us  [multiply_first(): pl.pallas_call(functools.partial(first_kernel, near, n_col, nb_rows, nb_c...]
    pallas_call x1, Pallas kernels: 4.44 us -> 5.16 us  [multiply_second(): pl.pallas_call(functools.partial(second_kernel, near, n_row, n_col, nb_ro...]
    ppermute x5, waiting for transfers between devices: 14 us -> 13.3 us  [hop(): return lax.ppermute(x, 'col', list(enumerate(targets)))]
  transfers between devices with their start and end apart: 17 -> 17, of which waited for: 8 -> 7; matrix products, arithmetic and copies ran while one was open for 0% -> 0% of each run, Pallas kernels for 18% -> 18%
where the time goes in v4:
time: 61.8 us; the launch traced here: 61.2 us
  starting transfers between devices  25.6 us (41%)
  waiting for transfers between devices  19 us (31%)
  Pallas kernels  16.3 us (26%)
    ppermute x5, starting transfers between devices, hop(): return lax.ppermute(x, 'col', list(enumerate(targets)))  16.3 us
    ppermute x5, waiting for transfers between devices, hop(): return lax.ppermute(x, 'col', list(enumerate(targets)))  13.3 us
    pallas_call x1, Pallas kernels, multiply_second(): pl.pallas_call(functools.partial(second_kernel, near, n_row, n_col, nb_ro...  5.16 us
    pallas_call x1, Pallas kernels, multiply_first(): pl.pallas_call(functools.partial(first_kernel, near, n_col, nb_rows, nb_c...  4.33 us
    ppermute x3, starting transfers between devices, body(): lax.ppermute(sums, 'row', [(s, s ^ m) for s in range(n_row)])  3.55 us
    ppermute x2, starting transfers between devices, body(): ys[m] = lax.ppermute(own, 'row', [(s, s ^ m) for s in range(n_row)])  3.05 us
    ppermute x3, waiting for transfers between devices, body(): lax.ppermute(sums, 'row', [(s, s ^ m) for s in range(n_row)])  2.71 us
    pallas_call x2, Pallas kernels, multiply_late(): pl.pallas_call(functools.partial(late_kernel, n_col, nb_rows, nb_cols, x_...  2.63 us
  transfers between devices with their start and end apart: 17, of which 7 were waited for; matrix products, arithmetic and copies ran while one was open for 0% of the time, Pallas kernels for 18%

profile of v4, /device:TPU:0, one launch (start us, length us, event | category | flops | bytes accessed | tf_op | source)
XLA Modules:
  0.0 61.2 jit_solution(13060594243120428269)
XLA Ops:
  0.0 1.9 %compact.1.refs_0_ = bf16[2320,128]{1,0:T(8,128)(2,1)S(1)} custom-call(s32[6,12]{1,0:T(8,128)} %bitcast.4, bf16[1536,768]{1,0:T(8,128)(2,1)} %sim_ref.1), custom_call_target="tpu_custom_call" | custom-call | bytes 1179648 | tf_op jit(solution)/shard_map/compact/pallas_call | solution.py:65
  1.9 3.3 %collective-permute-start.4 = (bf16[2320,128]{1,0:T(8,128)(2,1)S(1)}, bf16[2320,128]{1,0:T(8,128)(2,1)S(1)}, u32[]{:S(2)}, u32[]{:S(2)}) collective-permute-start(bf16[2320,128]{1,0:T(8,128)(2,1)S(1)} %compact.1.refs_0_), channel_id=1, source_target_pairs={{0,2},{2,0},{4,6},{6,4},{1,3},{3,1},{5,7},{7,5},{8,10},{10,8},{12,... | collective-permute-start | bytes 1781768 | tf_op jit(solution)/shard_map/ppermute | solution.py:402
  5.2 1.5 %collective-permute-start.3 = (bf16[2320,128]{1,0:T(8,128)(2,1)S(1)}, bf16[2320,128]{1,0:T(8,128)(2,1)}, u32[]{:S(2)}, u32[]{:S(2)}) collective-permute-start(bf16[2320,128]{1,0:T(8,128)(2,1)S(1)} %compact.1.refs_0_), channel_id=1, source_target_pairs={{0,0},{2,4},{4,2},{6,6},{1,1},{3,5},{5,3},{7,7},{8,8},{10,12},{12,... | collective-permute-start | bytes 1781768 | tf_op jit(solution)/shard_map/ppermute | solution.py:402
  6.6 1.5 %collective-permute-start.9 = (bf16[2320,128]{1,0:T(8,128)(2,1)S(1)}, bf16[2320,128]{1,0:T(8,128)(2,1)}, u32[]{:S(2)}, u32[]{:S(2)}) collective-permute-start(bf16[2320,128]{1,0:T(8,128)(2,1)S(1)} %compact.1.refs_0_), channel_id=1, source_target_pairs={{0,16},{8,24},{16,0},{24,8},{1,17},{9,25},{17,1},{25,9},{2,18},{10... | collective-permute-start | bytes 1781768 | tf_op jit(solution)/shard_map/ppermute | solution.py:413
  8.1 0.0 collective-permute-start.2
  8.1 1.5 %collective-permute-start = (bf16[2320,128]{1,0:T(8,128)(2,1)S(1)}, bf16[2320,128]{1,0:T(8,128)(2,1)}, u32[]{:S(2)}, u32[]{:S(2)}) collective-permute-start(bf16[2320,128]{1,0:T(8,128)(2,1)S(1)} %compact.1.refs_0_), channel_id=1, source_target_pairs={{0,8},{8,0},{16,24},{24,16},{1,9},{9,1},{17,25},{25,17},{2,10},{10... | collective-permute-start | bytes 1781768 | tf_op jit(solution)/shard_map/ppermute | solution.py:413
  9.7 8.9 %collective-permute-done.4.refs_4_.refs_3_ = bf16[2320,128]{1,0:T(8,128)(2,1)S(1)} collective-permute-done((bf16[2320,128]{1,0:T(8,128)(2,1)S(1)}, bf16[2320,128]{1,0:T(8,128)(2,1)S(1)}, u32[]{:S(2)}, u32[]{:S(2)}) %collective-permute-start.4) | collective-permute-done | bytes 593952 | tf_op jit(solution)/shard_map/ppermute | solution.py:402
  18.6 0.7 %collective-permute-start.7 = (bf16[2320,128]{1,0:T(8,128)(2,1)S(1)}, bf16[2320,128]{1,0:T(8,128)(2,1)S(1)}, u32[]{:S(2)}, u32[]{:S(2)}) collective-permute-start(bf16[2320,128]{1,0:T(8,128)(2,1)S(1)} %collective-permute-done.4.refs_4_.refs_3_), channel_id=1, source_target_pairs={{0,0},{2,4},{4,2},{6,6},{1,1},{3,5},{5,3},{7,7},{8,8},{10,12},{12,... | collective-permute-start | bytes 1781768 | tf_op jit(solution)/shard_map/ppermute | solution.py:402
  19.3 0.0 collective-permute-done.3.refs_2_
  19.3 4.6 %collective-permute-start.8 = (bf16[2320,128]{1,0:T(8,128)(2,1)}, bf16[2320,128]{1,0:T(8,128)(2,1)S(1)}, u32[]{:S(2)}, u32[]{:S(2)}) collective-permute-start(bf16[2320,128]{1,0:T(8,128)(2,1)} %collective-permute-done.3.refs_2_), channel_id=1, source_target_pairs={{0,2},{2,0},{4,6},{6,4},{1,3},{3,1},{5,7},{7,5},{8,10},{10,8},{12,... | collective-permute-start | bytes 1781768 | tf_op jit(solution)/shard_map/ppermute | solution.py:402
  23.9 0.1 pad_add_fusion.place_ref
  24.0 0.0 collective-permute-done.9.refs_2_
  24.0 0.0 collective-permute-start.6
  24.0 0.0 collective-permute-done.2.refs_3_.refs_1_
  24.0 0.5 collective-permute-start.5
  24.5 0.0 collective-permute-done.refs_1_
  24.5 1.6 %collective-permute-start.1 = (bf16[2320,128]{1,0:T(8,128)(2,1)}, bf16[2320,128]{1,0:T(8,128)(2,1)S(1)}, u32[]{:S(2)}, u32[]{:S(2)}) collective-permute-start(bf16[2320,128]{1,0:T(8,128)(2,1)} %collective-permute-done.refs_1_), channel_id=1, source_target_pairs={{0,16},{8,24},{16,0},{24,8},{1,17},{9,25},{17,1},{25,9},{2,18},{10... | collective-permute-start | bytes 1781768 | tf_op jit(solution)/shard_map/ppermute | solution.py:417
  26.1 4.3 %multiply_first.1 = (f32[73,128,128]{2,1,0:T(8,128)S(1)}, f32[7,8,128]{2,1,0:T(8,128)S(1)}, bf16[9280,128]{1,0:T(8,128)(2,1)S(1)}) custom-call(s32[3]{0:T(128)S(1)} %pad_add_fusion.place_ref, bf16[2320,128]{1,0:T(8,128)(2,1)S(1)} %compact.1.refs_0_, bf16[2320,128]{1,0:T(8,128)(2,1)} %collective-permute-done.refs_1_, ...), custom_call_target="tpu_custom_call" | custom-call | flops 100000000 | bytes 1000000 | tf_op jit(solution)/shard_map/multiply_first/pallas_call | solution.py:226
  30.4 0.0 collective-permute-done.7.refs_6_
  30.4 6.3 %collective-permute-start.12 = (bf16[2320,128]{1,0:T(8,128)(2,1)S(1)}, bf16[2320,128]{1,0:T(8,128)(2,1)S(1)}, u32[]{:S(2)}, u32[]{:S(2)}) collective-permute-start(bf16[2320,128]{1,0:T(8,128)(2,1)S(1)} %collective-permute-done.7.refs_6_), channel_id=1, source_target_pairs={{0,2},{2,0},{4,6},{6,4},{1,3},{3,1},{5,7},{7,5},{8,10},{10,8},{12,... | collective-permute-start | bytes 1781768 | tf_op jit(solution)/shard_map/ppermute | solution.py:402
  36.7 0.5 collective-permute-done.8.refs_7_
  37.2 0.1 broadcast_select_fusion
  37.3 0.1 collective-permute-start.10
  37.4 0.0 collective-permute-done.6.refs_5_
  37.4 0.6 collective-permute-start.11
  37.9 0.0 collective-permute-done.5.refs_4_
  37.9 2.2 %collective-permute-done.1.refs_0_ = bf16[2320,128]{1,0:T(8,128)(2,1)S(1)} collective-permute-done((bf16[2320,128]{1,0:T(8,128)(2,1)}, bf16[2320,128]{1,0:T(8,128)(2,1)S(1)}, u32[]{:S(2)}, u32[]{:S(2)}) %collective-permute-start.1) | collective-permute-done | bytes 593952 | tf_op jit(solution)/shard_map/ppermute | solution.py:417
  40.1 0.0 collective-permute-done.11.refs_9_
  40.1 0.0 collective-permute-done.10.refs_8_
  40.1 5.2 %multiply_second.1 = (f32[73,128,128]{2,1,0:T(8,128)S(1)}, f32[7,8,128]{2,1,0:T(8,128)S(1)}, bf16[9280,128]{1,0:T(8,128)(2,1)S(1)}, s32[384]{0:T(512)S(1)}, s32[48]{0:T(128)S(1)}) custom-call(s32[3]{0:T(128)S(1)} %pad_add_fusion.place_ref, ...), custom_call_target="tpu_custom_call", output_to_operand_aliasing={{0}: (11, {}), {1}: (12, {}), {2}: (13, {})} | custom-call | flops 100000000 | bytes 1000000 | tf_op jit(solution)/shard_map/multiply_second/pallas_call | solution.py:290
  45.3 3.9 %collective-permute-done.12.refs_0_ = bf16[2320,128]{1,0:T(8,128)(2,1)S(1)} collective-permute-done((bf16[2320,128]{1,0:T(8,128)(2,1)S(1)}, bf16[2320,128]{1,0:T(8,128)(2,1)S(1)}, u32[]{:S(2)}, u32[]{:S(2)}) %collective-permute-start.12) | collective-permute-done | bytes 593952 | tf_op jit(solution)/shard_map/ppermute | solution.py:402
  49.2 0.0 collective-permute-start.13
  49.2 1.3 %multiply_late.1 = (f32[73,128,128]{2,1,0:T(8,128)S(1)}, f32[7,8,128]{2,1,0:T(8,128)S(1)}) custom-call(s32[3]{0:T(128)S(1)} %pad_add_fusion.place_ref, s32[384]{0:T(512)S(1)} %get-tuple-element.28.slots_of, s32[48]{0:T(128)S(1)} %get-tuple-element.29.n_of, bf16[9280,128]{1,0:T(8,128)(2,1)S(1)} %get-tuple-element.30.y_blocks, ...), custom_call_target="tpu_custom_call", output_to_operand_aliasing={{0}: (5, {})} | custom-call | flops 100000000 | bytes 1000000 | tf_op jit(solution)/shard_map/multiply_late/pallas_call | solution.py:328
  50.5 0.7 %collective-permute-done.13.refs_0_ = bf16[2320,128]{1,0:T(8,128)(2,1)S(1)} collective-permute-done((bf16[2320,128]{1,0:T(8,128)(2,1)S(1)}, bf16[2320,128]{1,0:T(8,128)(2,1)S(1)}, u32[]{:S(2)}, u32[]{:S(2)}) %collective-permute-start.13) | collective-permute-done | bytes 593952 | tf_op jit(solution)/shard_map/ppermute | solution.py:405
  51.2 1.4 %multiply_last.1 = (f32[73,128,128]{2,1,0:T(8,128)S(1)}, f32[8,128]{1,0:T(8,128)S(1)}) custom-call(s32[3]{0:T(128)S(1)} %pad_add_fusion.place_ref, s32[384]{0:T(512)S(1)} %get-tuple-element.28.slots_of, s32[48]{0:T(128)S(1)} %get-tuple-element.29.n_of, bf16[9280,128]{1,0:T(8,128)(2,1)S(1)} %get-tuple-element.30.y_blocks, ...), custom_call_target="tpu_custom_call", output_to_operand_aliasing={{0}: (5, {})} | custom-call | flops 100000000 | bytes 1000000 | tf_op jit(solution)/shard_map/multiply_last/pallas_call | solution.py:328
  52.6 2.7 %collective-permute-start.16 = (f32[8,128]{1,0:T(8,128)S(1)}, f32[8,128]{1,0:T(8,128)S(1)}, u32[]{:S(2)}, u32[]{:S(2)}) collective-permute-start(f32[8,128]{1,0:T(8,128)S(1)} %get-tuple-element.38.refs_1_), channel_id=1, source_target_pairs={{0,24},{8,16},{16,8},{24,0},{1,25},{9,17},{17,9},{25,1},{2,26},{10... | collective-permute-start | bytes 12296 | tf_op jit(solution)/shard_map/ppermute | solution.py:444
  55.2 0.0 collective-permute-start.15
  55.2 0.9 %collective-permute-start.14 = (f32[8,128]{1,0:T(8,128)S(1)}, f32[8,128]{1,0:T(8,128)S(1)}, u32[]{:S(2)}, u32[]{:S(2)}) collective-permute-start(f32[8,128]{1,0:T(8,128)S(1)} %get-tuple-element.38.refs_1_), channel_id=1, source_target_pairs={{0,8},{8,0},{16,24},{24,16},{1,9},{9,1},{17,25},{25,17},{2,10},{10... | collective-permute-start | bytes 12296 | tf_op jit(solution)/shard_map/ppermute | solution.py:444
  56.1 1.0 %collective-permute-done.16.refs_4_ = f32[8,128]{1,0:T(8,128)S(1)} collective-permute-done((f32[8,128]{1,0:T(8,128)S(1)}, f32[8,128]{1,0:T(8,128)S(1)}, u32[]{:S(2)}, u32[]{:S(2)}) %collective-permute-start.16) | collective-permute-done | bytes 4128 | tf_op jit(solution)/shard_map/ppermute | solution.py:444
  57.1 1.7 %collective-permute-done.15.refs_3_ = f32[8,128]{1,0:T(8,128)S(1)} collective-permute-done((f32[8,128]{1,0:T(8,128)S(1)}, f32[8,128]{1,0:T(8,128)S(1)}, u32[]{:S(2)}, u32[]{:S(2)}) %collective-permute-start.15) | collective-permute-done | bytes 4128 | tf_op jit(solution)/shard_map/ppermute | solution.py:444
  58.8 0.0 collective-permute-done.14.refs_2_
  58.8 2.3 %scale.1 = f32[1536,768]{1,0:T(8,128)} custom-call(f32[73,128,128]{2,1,0:T(8,128)S(1)} %get-tuple-element.37.refs_0_, f32[8,128]{1,0:T(8,128)S(1)} %get-tuple-element.38.refs_1_, f32[8,128]{1,0:T(8,128)S(1)} %collective-permute-done.14.refs_2_, f32[8,128]{1,0:T(8,128)S(1)} %collective-permute-done.15.refs_3_, f32[8,128]{1,0:T(8,128)S(1)} %collective-permute-done.16.refs_4_), custom_call_target="tpu_custom_call" | custom-call | flops 10000000 | bytes 10000000 | tf_op jit(solution)/shard_map/scale/pallas_call | solution.py:374
  (2 shorter events, 0.0 us)
Async XLA Ops:
  1.9 16.7 %collective-permute-start.4 = (bf16[2320,128]{1,0:T(8,128)(2,1)S(1)}, bf16[2320,128]{1,0:T(8,128)(2,1)S(1)}, u32[]{:S(2)}, u32[]{:S(2)}) collective-permute-start(bf16[2320,128]{1,0:T(8,128)(2,1)S(1)} %compact.1.refs_0_), channel_id=1, source_target_pairs={{0,2},{2,0},{4,6},{6,4},{1,3},{3,1},{5,7},{7,5},{8,10},{10,8},{12,... | collective-permute-start | bytes 1781768 | tf_op jit(solution)/shard_map/ppermute | solution.py:402
  5.2 14.2 %collective-permute-start.3 = (bf16[2320,128]{1,0:T(8,128)(2,1)S(1)}, bf16[2320,128]{1,0:T(8,128)(2,1)}, u32[]{:S(2)}, u32[]{:S(2)}) collective-permute-start(bf16[2320,128]{1,0:T(8,128)(2,1)S(1)} %compact.1.refs_0_), channel_id=1, source_target_pairs={{0,0},{2,4},{4,2},{6,6},{1,1},{3,5},{5,3},{7,7},{8,8},{10,12},{12,... | collective-permute-start | bytes 1781768 | tf_op jit(solution)/shard_map/ppermute | solution.py:402
  6.6 17.3 %collective-permute-start.9 = (bf16[2320,128]{1,0:T(8,128)(2,1)S(1)}, bf16[2320,128]{1,0:T(8,128)(2,1)}, u32[]{:S(2)}, u32[]{:S(2)}) collective-permute-start(bf16[2320,128]{1,0:T(8,128)(2,1)S(1)} %compact.1.refs_0_), channel_id=1, source_target_pairs={{0,16},{8,24},{16,0},{24,8},{1,17},{9,25},{17,1},{25,9},{2,18},{10... | collective-permute-start | bytes 1781768 | tf_op jit(solution)/shard_map/ppermute | solution.py:413
  8.1 15.8 %collective-permute-start.2 = (bf16[2320,128]{1,0:T(8,128)(2,1)S(1)}, bf16[2320,128]{1,0:T(8,128)(2,1)S(1)}, u32[]{:S(2)}, u32[]{:S(2)}) collective-permute-start(bf16[2320,128]{1,0:T(8,128)(2,1)S(1)} %compact.1.refs_0_), channel_id=1, source_target_pairs={{0,1},{1,0},{2,3},{3,2},{4,5},{5,4},{6,7},{7,6},{8,9},{9,8},{10,11... | collective-permute-start | bytes 1781768 | tf_op jit(solution)/shard_map/ppermute | solution.py:405
  8.1 16.3 %collective-permute-start = (bf16[2320,128]{1,0:T(8,128)(2,1)S(1)}, bf16[2320,128]{1,0:T(8,128)(2,1)}, u32[]{:S(2)}, u32[]{:S(2)}) collective-permute-start(bf16[2320,128]{1,0:T(8,128)(2,1)S(1)} %compact.1.refs_0_), channel_id=1, source_target_pairs={{0,8},{8,0},{16,24},{24,16},{1,9},{9,1},{17,25},{25,17},{2,10},{10... | collective-permute-start | bytes 1781768 | tf_op jit(solution)/shard_map/ppermute | solution.py:413
  18.6 11.8 %collective-permute-start.7 = (bf16[2320,128]{1,0:T(8,128)(2,1)S(1)}, bf16[2320,128]{1,0:T(8,128)(2,1)S(1)}, u32[]{:S(2)}, u32[]{:S(2)}) collective-permute-start(bf16[2320,128]{1,0:T(8,128)(2,1)S(1)} %collective-permute-done.4.refs_4_.refs_3_), channel_id=1, source_target_pairs={{0,0},{2,4},{4,2},{6,6},{1,1},{3,5},{5,3},{7,7},{8,8},{10,12},{12,... | collective-permute-start | bytes 1781768 | tf_op jit(solution)/shard_map/ppermute | solution.py:402
  19.3 17.8 %collective-permute-start.8 = (bf16[2320,128]{1,0:T(8,128)(2,1)}, bf16[2320,128]{1,0:T(8,128)(2,1)S(1)}, u32[]{:S(2)}, u32[]{:S(2)}) collective-permute-start(bf16[2320,128]{1,0:T(8,128)(2,1)} %collective-permute-done.3.refs_2_), channel_id=1, source_target_pairs={{0,2},{2,0},{4,6},{6,4},{1,3},{3,1},{5,7},{7,5},{8,10},{10,8},{12,... | collective-permute-start | bytes 1781768 | tf_op jit(solution)/shard_map/ppermute | solution.py:402
  24.0 13.4 %collective-permute-start.6 = (bf16[2320,128]{1,0:T(8,128)(2,1)S(1)}, bf16[2320,128]{1,0:T(8,128)(2,1)S(1)}, u32[]{:S(2)}, u32[]{:S(2)}) collective-permute-start(bf16[2320,128]{1,0:T(8,128)(2,1)S(1)} %collective-permute-done.4.refs_4_.refs_3_), channel_id=1, source_target_pairs={{0,1},{1,0},{2,3},{3,2},{4,5},{5,4},{6,7},{7,6},{8,9},{9,8},{10,11... | collective-permute-start | bytes 1781768 | tf_op jit(solution)/shard_map/ppermute | solution.py:405
  24.0 13.9 %collective-permute-start.5 = (bf16[2320,128]{1,0:T(8,128)(2,1)}, bf16[2320,128]{1,0:T(8,128)(2,1)S(1)}, u32[]{:S(2)}, u32[]{:S(2)}) collective-permute-start(bf16[2320,128]{1,0:T(8,128)(2,1)} %collective-permute-done.3.refs_2_), channel_id=1, source_target_pairs={{0,1},{1,0},{2,3},{3,2},{4,5},{5,4},{6,7},{7,6},{8,9},{9,8},{10,11... | collective-permute-start | bytes 1781768 | tf_op jit(solution)/shard_map/ppermute | solution.py:405
  24.5 15.6 %collective-permute-start.1 = (bf16[2320,128]{1,0:T(8,128)(2,1)}, bf16[2320,128]{1,0:T(8,128)(2,1)S(1)}, u32[]{:S(2)}, u32[]{:S(2)}) collective-permute-start(bf16[2320,128]{1,0:T(8,128)(2,1)} %collective-permute-done.refs_1_), channel_id=1, source_target_pairs={{0,16},{8,24},{16,0},{24,8},{1,17},{9,25},{17,1},{25,9},{2,18},{10... | collective-permute-start | bytes 1781768 | tf_op jit(solution)/shard_map/ppermute | solution.py:417
  30.4 18.8 %collective-permute-start.12 = (bf16[2320,128]{1,0:T(8,128)(2,1)S(1)}, bf16[2320,128]{1,0:T(8,128)(2,1)S(1)}, u32[]{:S(2)}, u32[]{:S(2)}) collective-permute-start(bf16[2320,128]{1,0:T(8,128)(2,1)S(1)} %collective-permute-done.7.refs_6_), channel_id=1, source_target_pairs={{0,2},{2,0},{4,6},{6,4},{1,3},{3,1},{5,7},{7,5},{8,10},{10,8},{12,... | collective-permute-start | bytes 1781768 | tf_op jit(solution)/shard_map/ppermute | solution.py:402
  37.3 2.9 %collective-permute-start.10 = (bf16[1168,128]{1,0:T(8,128)(2,1)S(1)}, bf16[1168,128]{1,0:T(8,128)(2,1)S(1)}, u32[]{:S(2)}, u32[]{:S(2)}) collective-permute-start(bf16[1168,128]{1,0:T(8,128)(2,1)S(1)} %slice.8), channel_id=1, source_target_pairs={{0,1},{1,0},{2,3},{3,2},{4,5},{5,4},{6,7},{7,6},{8,9},{9,8},{10,11... | collective-permute-start | bytes 897032 | tf_op jit(solution)/shard_map/ppermute | solution.py:405
  37.4 2.7 %collective-permute-start.11 = (bf16[1152,128]{1,0:T(8,128)(2,1)S(1)}, bf16[1152,128]{1,0:T(8,128)(2,1)S(1)}, u32[]{:S(2)}, u32[]{:S(2)}) collective-permute-start(bf16[1152,128]{1,0:T(8,128)(2,1)S(1)} %slice.9), channel_id=1, source_target_pairs={{0,1},{1,0},{2,3},{3,2},{4,5},{5,4},{6,7},{7,6},{8,9},{9,8},{10,11... | collective-permute-start | bytes 884744 | tf_op jit(solution)/shard_map/ppermute | solution.py:405
  49.2 2.0 %collective-permute-start.13 = (bf16[2320,128]{1,0:T(8,128)(2,1)S(1)}, bf16[2320,128]{1,0:T(8,128)(2,1)S(1)}, u32[]{:S(2)}, u32[]{:S(2)}) collective-permute-start(bf16[2320,128]{1,0:T(8,128)(2,1)S(1)} %collective-permute-done.12.refs_0_), channel_id=1, source_target_pairs={{0,1},{1,0},{2,3},{3,2},{4,5},{5,4},{6,7},{7,6},{8,9},{9,8},{10,11... | collective-permute-start | bytes 1781768 | tf_op jit(solution)/shard_map/ppermute | solution.py:405
  52.6 4.6 %collective-permute-start.16 = (f32[8,128]{1,0:T(8,128)S(1)}, f32[8,128]{1,0:T(8,128)S(1)}, u32[]{:S(2)}, u32[]{:S(2)}) collective-permute-start(f32[8,128]{1,0:T(8,128)S(1)} %get-tuple-element.38.refs_1_), channel_id=1, source_target_pairs={{0,24},{8,16},{16,8},{24,0},{1,25},{9,17},{17,9},{25,1},{2,26},{10... | collective-permute-start | bytes 12296 | tf_op jit(solution)/shard_map/ppermute | solution.py:444
  55.2 3.6 %collective-permute-start.15 = (f32[8,128]{1,0:T(8,128)S(1)}, f32[8,128]{1,0:T(8,128)S(1)}, u32[]{:S(2)}, u32[]{:S(2)}) collective-permute-start(f32[8,128]{1,0:T(8,128)S(1)} %get-tuple-element.38.refs_1_), channel_id=1, source_target_pairs={{0,16},{8,24},{16,0},{24,8},{1,17},{9,25},{17,1},{25,9},{2,18},{10... | collective-permute-start | bytes 12296 | tf_op jit(solution)/shard_map/ppermute | solution.py:444
  55.2 3.6 %collective-permute-start.14 = (f32[8,128]{1,0:T(8,128)S(1)}, f32[8,128]{1,0:T(8,128)S(1)}, u32[]{:S(2)}, u32[]{:S(2)}) collective-permute-start(f32[8,128]{1,0:T(8,128)S(1)} %get-tuple-element.38.refs_1_), channel_id=1, source_target_pairs={{0,8},{8,0},{16,24},{24,16},{1,9},{9,1},{17,25},{25,17},{2,10},{10... | collective-permute-start | bytes 12296 | tf_op jit(solution)/shard_map/ppermute | solution.py:444

commit v5 on v4

--- a/solution.py
+++ b/solution.py
@@ -340,11 +340,10 @@
 
 
 def scale_kernel(scaling, nb_rows, nb_cols, *refs):
-    product, sums = refs[0], refs[1:-3]
-    out, scaled, sems = refs[-3:]
-    total = sums[0][...]
-    for other in sums[1:]:
-        total = total + other[...]
+    product, sums, out, scaled, sems = refs
+    total = sums[0]
+    for other in range(1, sums.shape[0]):
+        total = total + sums[other]
     factor = scaling / total[0:nb_cols, :]
 
     def out_copy(i):
@@ -374,13 +373,13 @@
     return pl.pallas_call(
         functools.partial(scale_kernel, scaling, nb_rows, nb_cols),
         out_shape=jax.ShapeDtypeStruct(shape, jnp.float32),
-        in_specs=[VMEM] * (1 + len(sums)),
+        in_specs=[VMEM, VMEM],
         out_specs=ANY,
         scratch_shapes=[pltpu.VMEM(shape, jnp.float32), pltpu.SemaphoreType.DMA((nb_rows,))],
         compiler_params=pltpu.CompilerParams(vmem_limit_bytes=16 * MIB),
         cost_estimate=pl.CostEstimate(flops=10**7, bytes_accessed=10 * 10**6, transcendentals=0),
         name="scale",
-    )(product, *sums)
+    )(product, sums)
 
 
 def even_tile(i, step):
@@ -439,9 +438,7 @@
     acc, sums = multiply_late(place, slots_of, n_of, y_blocks, [last], kinds, acc, sums, False, *sizes)
     kinds = [(n_col - 1, False, True)]
     product, sums = multiply_late(place, slots_of, n_of, y_blocks, [other], kinds, acc, sums, True, *sizes)
-    all_sums = [sums]
-    for m in range(1, n_row):
-        all_sums.append(lax.ppermute(sums, "row", [(s, s ^ m) for s in range(n_row)]))
+    all_sums = lax.all_gather(sums, "row", axis=0)
     return scale(product, all_sums, float(nb_rows * BLK * n_row), nb_rows, nb_cols)
 
 

time: 61.8 us -> 63.5 us (1.028)
  blocking collectives: 0 us -> 7.81 us
  starting transfers between devices: 25.6 us -> 21.5 us
  waiting for transfers between devices: 19 us -> 16.5 us
    all_gather x0 -> x1, blocking collectives: none -> 7.81 us  [body(): all_sums = lax.all_gather(sums, 'row', axis=0)]
    ppermute x3 -> x0, starting transfers between devices: 3.55 us -> none  [body(): lax.ppermute(sums, 'row', [(s, s ^ m) for s in range(n_row)])]
    ppermute x3 -> x0, waiting for transfers between devices: 2.71 us -> none  [body(): lax.ppermute(sums, 'row', [(s, s ^ m) for s in range(n_row)])]
    ppermute x5, waiting for transfers between devices: 13.3 us -> 14 us  [hop(): return lax.ppermute(x, 'col', list(enumerate(targets)))]
  transfers between devices with their start and end apart: 17 -> 14, of which waited for: 7 -> 5; matrix products, arithmetic and copies ran while one was open for 0% -> 0% of each run, Pallas kernels for 18% -> 17%
where the time goes in v5:
time: 63.5 us; the launch traced here: 62.9 us
  starting transfers between devices  21.5 us (34%)
  Pallas kernels  16.8 us (26%)
  waiting for transfers between devices  16.5 us (26%)
  blocking collectives  7.81 us (12%)
    ppermute x5, starting transfers between devices, hop(): return lax.ppermute(x, 'col', list(enumerate(targets)))  15.8 us
    ppermute x5, waiting for transfers between devices, hop(): return lax.ppermute(x, 'col', list(enumerate(targets)))  14 us
    all_gather x1, blocking collectives, body(): all_sums = lax.all_gather(sums, 'row', axis=0)  7.81 us
    pallas_call x1, Pallas kernels, multiply_second(): pl.pallas_call(functools.partial(second_kernel, near, n_row, n_col, nb_ro...  4.87 us
    pallas_call x1, Pallas kernels, multiply_first(): pl.pallas_call(functools.partial(first_kernel, near, n_col, nb_rows, nb_c...  4.58 us
    pallas_call x2, Pallas kernels, multiply_late(): pl.pallas_call(functools.partial(late_kernel, n_col, nb_rows, nb_cols, x_...  3.01 us
    ppermute x2, starting transfers between devices, body(): ys[m] = lax.ppermute(own, 'row', [(s, s ^ m) for s in range(n_row)])  2.99 us
    pallas_call x1, Pallas kernels, scale(): pl.pallas_call(functools.partial(scale_kernel, scaling, nb_rows, nb_cols)...  2.31 us
  transfers between devices with their start and end apart: 14, of which 5 were waited for; matrix products, arithmetic and copies ran while one was open for 0% of the time, Pallas kernels for 17%

profile of v5, /device:TPU:0, one launch (start us, length us, event | category | flops | bytes accessed | tf_op | source)
XLA Modules:
  0.0 62.9 jit_solution(3717737097598802467)
XLA Ops:
  0.0 2.0 %compact.1.refs_0_ = bf16[2320,128]{1,0:T(8,128)(2,1)S(1)} custom-call(s32[6,12]{1,0:T(8,128)} %bitcast.6, bf16[1536,768]{1,0:T(8,128)(2,1)} %sim_ref.1), custom_call_target="tpu_custom_call" | custom-call | bytes 1179648 | tf_op jit(solution)/shard_map/compact/pallas_call | solution.py:65
  2.0 3.1 %collective-permute-start.4 = (bf16[2320,128]{1,0:T(8,128)(2,1)S(1)}, bf16[2320,128]{1,0:T(8,128)(2,1)S(1)}, u32[]{:S(2)}, u32[]{:S(2)}) collective-permute-start(bf16[2320,128]{1,0:T(8,128)(2,1)S(1)} %compact.1.refs_0_), channel_id=1, source_target_pairs={{0,2},{2,0},{4,6},{6,4},{1,3},{3,1},{5,7},{7,5},{8,10},{10,8},{12,... | collective-permute-start | bytes 1781768 | tf_op jit(solution)/shard_map/ppermute | solution.py:401
  5.1 1.5 %collective-permute-start.3 = (bf16[2320,128]{1,0:T(8,128)(2,1)S(1)}, bf16[2320,128]{1,0:T(8,128)(2,1)}, u32[]{:S(2)}, u32[]{:S(2)}) collective-permute-start(bf16[2320,128]{1,0:T(8,128)(2,1)S(1)} %compact.1.refs_0_), channel_id=1, source_target_pairs={{0,0},{2,4},{4,2},{6,6},{1,1},{3,5},{5,3},{7,7},{8,8},{10,12},{12,... | collective-permute-start | bytes 1781768 | tf_op jit(solution)/shard_map/ppermute | solution.py:401
  6.6 1.5 %collective-permute-start.9 = (bf16[2320,128]{1,0:T(8,128)(2,1)S(1)}, bf16[2320,128]{1,0:T(8,128)(2,1)}, u32[]{:S(2)}, u32[]{:S(2)}) collective-permute-start(bf16[2320,128]{1,0:T(8,128)(2,1)S(1)} %compact.1.refs_0_), channel_id=1, source_target_pairs={{0,16},{8,24},{16,0},{24,8},{1,17},{9,25},{17,1},{25,9},{2,18},{10... | collective-permute-start | bytes 1781768 | tf_op jit(solution)/shard_map/ppermute | solution.py:412
  8.1 0.0 collective-permute-start.2
  8.1 1.5 %collective-permute-start = (bf16[2320,128]{1,0:T(8,128)(2,1)S(1)}, bf16[2320,128]{1,0:T(8,128)(2,1)}, u32[]{:S(2)}, u32[]{:S(2)}) collective-permute-start(bf16[2320,128]{1,0:T(8,128)(2,1)S(1)} %compact.1.refs_0_), channel_id=1, source_target_pairs={{0,8},{8,0},{16,24},{24,16},{1,9},{9,1},{17,25},{25,17},{2,10},{10... | collective-permute-start | bytes 1781768 | tf_op jit(solution)/shard_map/ppermute | solution.py:412
  9.6 9.0 %collective-permute-done.4.refs_4_.refs_3_ = bf16[2320,128]{1,0:T(8,128)(2,1)S(1)} collective-permute-done((bf16[2320,128]{1,0:T(8,128)(2,1)S(1)}, bf16[2320,128]{1,0:T(8,128)(2,1)S(1)}, u32[]{:S(2)}, u32[]{:S(2)}) %collective-permute-start.4) | collective-permute-done | bytes 593952 | tf_op jit(solution)/shard_map/ppermute | solution.py:401
  18.6 0.7 %collective-permute-start.7 = (bf16[2320,128]{1,0:T(8,128)(2,1)S(1)}, bf16[2320,128]{1,0:T(8,128)(2,1)S(1)}, u32[]{:S(2)}, u32[]{:S(2)}) collective-permute-start(bf16[2320,128]{1,0:T(8,128)(2,1)S(1)} %collective-permute-done.4.refs_4_.refs_3_), channel_id=1, source_target_pairs={{0,0},{2,4},{4,2},{6,6},{1,1},{3,5},{5,3},{7,7},{8,8},{10,12},{12,... | collective-permute-start | bytes 1781768 | tf_op jit(solution)/shard_map/ppermute | solution.py:401
  19.3 0.0 collective-permute-done.3.refs_2_
  19.3 4.6 %collective-permute-start.8 = (bf16[2320,128]{1,0:T(8,128)(2,1)}, bf16[2320,128]{1,0:T(8,128)(2,1)S(1)}, u32[]{:S(2)}, u32[]{:S(2)}) collective-permute-start(bf16[2320,128]{1,0:T(8,128)(2,1)} %collective-permute-done.3.refs_2_), channel_id=1, source_target_pairs={{0,2},{2,0},{4,6},{6,4},{1,3},{3,1},{5,7},{7,5},{8,10},{10,8},{12,... | collective-permute-start | bytes 1781768 | tf_op jit(solution)/shard_map/ppermute | solution.py:401
  23.9 0.1 pad_add_fusion.place_ref
  24.0 0.0 collective-permute-done.9.refs_2_
  24.0 0.0 collective-permute-start.6
  24.0 0.0 collective-permute-done.2.refs_3_.refs_1_
  24.0 0.5 collective-permute-start.5
  24.5 0.0 collective-permute-done.refs_1_
  24.5 1.6 %collective-permute-start.1 = (bf16[2320,128]{1,0:T(8,128)(2,1)}, bf16[2320,128]{1,0:T(8,128)(2,1)S(1)}, u32[]{:S(2)}, u32[]{:S(2)}) collective-permute-start(bf16[2320,128]{1,0:T(8,128)(2,1)} %collective-permute-done.refs_1_), channel_id=1, source_target_pairs={{0,16},{8,24},{16,0},{24,8},{1,17},{9,25},{17,1},{25,9},{2,18},{10... | collective-permute-start | bytes 1781768 | tf_op jit(solution)/shard_map/ppermute | solution.py:416
  26.1 4.6 %multiply_first.1 = (f32[73,128,128]{2,1,0:T(8,128)S(1)}, f32[7,8,128]{2,1,0:T(8,128)S(1)}, bf16[9280,128]{1,0:T(8,128)(2,1)S(1)}) custom-call(s32[3]{0:T(128)S(1)} %pad_add_fusion.place_ref, bf16[2320,128]{1,0:T(8,128)(2,1)S(1)} %compact.1.refs_0_, bf16[2320,128]{1,0:T(8,128)(2,1)} %collective-permute-done.refs_1_, ...), custom_call_target="tpu_custom_call" | custom-call | flops 100000000 | bytes 1000000 | tf_op jit(solution)/shard_map/multiply_first/pallas_call | solution.py:226
  30.6 0.0 collective-permute-done.7.refs_6_
  30.7 6.0 %collective-permute-start.12 = (bf16[2320,128]{1,0:T(8,128)(2,1)S(1)}, bf16[2320,128]{1,0:T(8,128)(2,1)S(1)}, u32[]{:S(2)}, u32[]{:S(2)}) collective-permute-start(bf16[2320,128]{1,0:T(8,128)(2,1)S(1)} %collective-permute-done.7.refs_6_), channel_id=1, source_target_pairs={{0,2},{2,0},{4,6},{6,4},{1,3},{3,1},{5,7},{7,5},{8,10},{10,8},{12,... | collective-permute-start | bytes 1781768 | tf_op jit(solution)/shard_map/ppermute | solution.py:401
  36.6 0.7 %collective-permute-done.8.refs_7_ = bf16[2320,128]{1,0:T(8,128)(2,1)S(1)} collective-permute-done((bf16[2320,128]{1,0:T(8,128)(2,1)}, bf16[2320,128]{1,0:T(8,128)(2,1)S(1)}, u32[]{:S(2)}, u32[]{:S(2)}) %collective-permute-start.8) | collective-permute-done | bytes 593952 | tf_op jit(solution)/shard_map/ppermute | solution.py:401
  37.4 0.1 broadcast_select_fusion
  37.5 0.1 collective-permute-start.10
  37.6 0.0 collective-permute-done.6.refs_5_
  37.6 0.6 collective-permute-start.11
  38.2 0.0 collective-permute-done.5.refs_4_
  38.2 2.0 %collective-permute-done.1.refs_0_ = bf16[2320,128]{1,0:T(8,128)(2,1)S(1)} collective-permute-done((bf16[2320,128]{1,0:T(8,128)(2,1)}, bf16[2320,128]{1,0:T(8,128)(2,1)S(1)}, u32[]{:S(2)}, u32[]{:S(2)}) %collective-permute-start.1) | collective-permute-done | bytes 593952 | tf_op jit(solution)/shard_map/ppermute | solution.py:416
  40.1 0.0 collective-permute-done.11.refs_9_
  40.1 0.0 collective-permute-done.10.refs_8_
  40.1 4.9 %multiply_second.1 = (f32[73,128,128]{2,1,0:T(8,128)S(1)}, f32[7,8,128]{2,1,0:T(8,128)S(1)}, bf16[9280,128]{1,0:T(8,128)(2,1)S(1)}, s32[384]{0:T(512)S(1)}, s32[48]{0:T(128)S(1)}) custom-call(s32[3]{0:T(128)S(1)} %pad_add_fusion.place_ref, ...), custom_call_target="tpu_custom_call", output_to_operand_aliasing={{0}: (11, {}), {1}: (12, {}), {2}: (13, {})} | custom-call | flops 100000000 | bytes 1000000 | tf_op jit(solution)/shard_map/multiply_second/pallas_call | solution.py:290
  45.0 4.3 %collective-permute-done.12.refs_0_ = bf16[2320,128]{1,0:T(8,128)(2,1)S(1)} collective-permute-done((bf16[2320,128]{1,0:T(8,128)(2,1)S(1)}, bf16[2320,128]{1,0:T(8,128)(2,1)S(1)}, u32[]{:S(2)}, u32[]{:S(2)}) %collective-permute-start.12) | collective-permute-done | bytes 593952 | tf_op jit(solution)/shard_map/ppermute | solution.py:401
  49.3 0.0 collective-permute-start.13
  49.3 1.5 %multiply_late.1 = (f32[73,128,128]{2,1,0:T(8,128)S(1)}, f32[7,8,128]{2,1,0:T(8,128)S(1)}) custom-call(s32[3]{0:T(128)S(1)} %pad_add_fusion.place_ref, s32[384]{0:T(512)S(1)} %get-tuple-element.28.slots_of, s32[48]{0:T(128)S(1)} %get-tuple-element.29.n_of, bf16[9280,128]{1,0:T(8,128)(2,1)S(1)} %get-tuple-element.30.y_blocks, ...), custom_call_target="tpu_custom_call", output_to_operand_aliasing={{0}: (5, {})} | custom-call | flops 100000000 | bytes 1000000 | tf_op jit(solution)/shard_map/multiply_late/pallas_call | solution.py:328
  50.8 0.5 collective-permute-done.13.refs_0_
  51.3 1.5 %multiply_last.1 = (f32[73,128,128]{2,1,0:T(8,128)S(1)}, f32[8,128]{1,0:T(8,128)S(1)}) custom-call(s32[3]{0:T(128)S(1)} %pad_add_fusion.place_ref, s32[384]{0:T(512)S(1)} %get-tuple-element.28.slots_of, s32[48]{0:T(128)S(1)} %get-tuple-element.29.n_of, bf16[9280,128]{1,0:T(8,128)(2,1)S(1)} %get-tuple-element.30.y_blocks, ...), custom_call_target="tpu_custom_call", output_to_operand_aliasing={{0}: (5, {})} | custom-call | flops 100000000 | bytes 1000000 | tf_op jit(solution)/shard_map/multiply_last/pallas_call | solution.py:328
  52.8 7.8 %all-gather = f32[32,128]{1,0:T(8,128)S(1)} all-gather(f32[8,128]{1,0:T(8,128)S(1)} %get-tuple-element.38), channel_id=2, replica_groups=mesh['row'=4,'col'=4,'layer'=2] {'row'}, dimensions={0}, use_global_device_ids=true | all-gather | bytes 20480 | tf_op jit(solution)/shard_map/all_gather | solution.py:441
  60.6 2.3 %scale.1 = f32[1536,768]{1,0:T(8,128)} custom-call(f32[73,128,128]{2,1,0:T(8,128)S(1)} %get-tuple-element.37.refs_0_, f32[4,8,128]{2,1,0:T(8,128)S(1)} %bitcast.5), custom_call_target="tpu_custom_call" | custom-call | flops 10000000 | bytes 10000000 | tf_op jit(solution)/shard_map/scale/pallas_call | solution.py:373
  (2 shorter events, 0.0 us)
Async XLA Ops:
  2.0 16.5 %collective-permute-start.4 = (bf16[2320,128]{1,0:T(8,128)(2,1)S(1)}, bf16[2320,128]{1,0:T(8,128)(2,1)S(1)}, u32[]{:S(2)}, u32[]{:S(2)}) collective-permute-start(bf16[2320,128]{1,0:T(8,128)(2,1)S(1)} %compact.1.refs_0_), channel_id=1, source_target_pairs={{0,2},{2,0},{4,6},{6,4},{1,3},{3,1},{5,7},{7,5},{8,10},{10,8},{12,... | collective-permute-start | bytes 1781768 | tf_op jit(solution)/shard_map/ppermute | solution.py:401
  5.1 14.1 %collective-permute-start.3 = (bf16[2320,128]{1,0:T(8,128)(2,1)S(1)}, bf16[2320,128]{1,0:T(8,128)(2,1)}, u32[]{:S(2)}, u32[]{:S(2)}) collective-permute-start(bf16[2320,128]{1,0:T(8,128)(2,1)S(1)} %compact.1.refs_0_), channel_id=1, source_target_pairs={{0,0},{2,4},{4,2},{6,6},{1,1},{3,5},{5,3},{7,7},{8,8},{10,12},{12,... | collective-permute-start | bytes 1781768 | tf_op jit(solution)/shard_map/ppermute | solution.py:401
  6.6 17.3 %collective-permute-start.9 = (bf16[2320,128]{1,0:T(8,128)(2,1)S(1)}, bf16[2320,128]{1,0:T(8,128)(2,1)}, u32[]{:S(2)}, u32[]{:S(2)}) collective-permute-start(bf16[2320,128]{1,0:T(8,128)(2,1)S(1)} %compact.1.refs_0_), channel_id=1, source_target_pairs={{0,16},{8,24},{16,0},{24,8},{1,17},{9,25},{17,1},{25,9},{2,18},{10... | collective-permute-start | bytes 1781768 | tf_op jit(solution)/shard_map/ppermute | solution.py:412
  8.1 15.9 %collective-permute-start.2 = (bf16[2320,128]{1,0:T(8,128)(2,1)S(1)}, bf16[2320,128]{1,0:T(8,128)(2,1)S(1)}, u32[]{:S(2)}, u32[]{:S(2)}) collective-permute-start(bf16[2320,128]{1,0:T(8,128)(2,1)S(1)} %compact.1.refs_0_), channel_id=1, source_target_pairs={{0,1},{1,0},{2,3},{3,2},{4,5},{5,4},{6,7},{7,6},{8,9},{9,8},{10,11... | collective-permute-start | bytes 1781768 | tf_op jit(solution)/shard_map/ppermute | solution.py:404
  8.1 16.4 %collective-permute-start = (bf16[2320,128]{1,0:T(8,128)(2,1)S(1)}, bf16[2320,128]{1,0:T(8,128)(2,1)}, u32[]{:S(2)}, u32[]{:S(2)}) collective-permute-start(bf16[2320,128]{1,0:T(8,128)(2,1)S(1)} %compact.1.refs_0_), channel_id=1, source_target_pairs={{0,8},{8,0},{16,24},{24,16},{1,9},{9,1},{17,25},{25,17},{2,10},{10... | collective-permute-start | bytes 1781768 | tf_op jit(solution)/shard_map/ppermute | solution.py:412
  18.6 12.1 %collective-permute-start.7 = (bf16[2320,128]{1,0:T(8,128)(2,1)S(1)}, bf16[2320,128]{1,0:T(8,128)(2,1)S(1)}, u32[]{:S(2)}, u32[]{:S(2)}) collective-permute-start(bf16[2320,128]{1,0:T(8,128)(2,1)S(1)} %collective-permute-done.4.refs_4_.refs_3_), channel_id=1, source_target_pairs={{0,0},{2,4},{4,2},{6,6},{1,1},{3,5},{5,3},{7,7},{8,8},{10,12},{12,... | collective-permute-start | bytes 1781768 | tf_op jit(solution)/shard_map/ppermute | solution.py:401
  19.3 18.1 %collective-permute-start.8 = (bf16[2320,128]{1,0:T(8,128)(2,1)}, bf16[2320,128]{1,0:T(8,128)(2,1)S(1)}, u32[]{:S(2)}, u32[]{:S(2)}) collective-permute-start(bf16[2320,128]{1,0:T(8,128)(2,1)} %collective-permute-done.3.refs_2_), channel_id=1, source_target_pairs={{0,2},{2,0},{4,6},{6,4},{1,3},{3,1},{5,7},{7,5},{8,10},{10,8},{12,... | collective-permute-start | bytes 1781768 | tf_op jit(solution)/shard_map/ppermute | solution.py:401
  24.0 13.6 %collective-permute-start.6 = (bf16[2320,128]{1,0:T(8,128)(2,1)S(1)}, bf16[2320,128]{1,0:T(8,128)(2,1)S(1)}, u32[]{:S(2)}, u32[]{:S(2)}) collective-permute-start(bf16[2320,128]{1,0:T(8,128)(2,1)S(1)} %collective-permute-done.4.refs_4_.refs_3_), channel_id=1, source_target_pairs={{0,1},{1,0},{2,3},{3,2},{4,5},{5,4},{6,7},{7,6},{8,9},{9,8},{10,11... | collective-permute-start | bytes 1781768 | tf_op jit(solution)/shard_map/ppermute | solution.py:404
  24.0 14.2 %collective-permute-start.5 = (bf16[2320,128]{1,0:T(8,128)(2,1)}, bf16[2320,128]{1,0:T(8,128)(2,1)S(1)}, u32[]{:S(2)}, u32[]{:S(2)}) collective-permute-start(bf16[2320,128]{1,0:T(8,128)(2,1)} %collective-permute-done.3.refs_2_), channel_id=1, source_target_pairs={{0,1},{1,0},{2,3},{3,2},{4,5},{5,4},{6,7},{7,6},{8,9},{9,8},{10,11... | collective-permute-start | bytes 1781768 | tf_op jit(solution)/shard_map/ppermute | solution.py:404
  24.5 15.6 %collective-permute-start.1 = (bf16[2320,128]{1,0:T(8,128)(2,1)}, bf16[2320,128]{1,0:T(8,128)(2,1)S(1)}, u32[]{:S(2)}, u32[]{:S(2)}) collective-permute-start(bf16[2320,128]{1,0:T(8,128)(2,1)} %collective-permute-done.refs_1_), channel_id=1, source_target_pairs={{0,16},{8,24},{16,0},{24,8},{1,17},{9,25},{17,1},{25,9},{2,18},{10... | collective-permute-start | bytes 1781768 | tf_op jit(solution)/shard_map/ppermute | solution.py:416
  30.7 18.6 %collective-permute-start.12 = (bf16[2320,128]{1,0:T(8,128)(2,1)S(1)}, bf16[2320,128]{1,0:T(8,128)(2,1)S(1)}, u32[]{:S(2)}, u32[]{:S(2)}) collective-permute-start(bf16[2320,128]{1,0:T(8,128)(2,1)S(1)} %collective-permute-done.7.refs_6_), channel_id=1, source_target_pairs={{0,2},{2,0},{4,6},{6,4},{1,3},{3,1},{5,7},{7,5},{8,10},{10,8},{12,... | collective-permute-start | bytes 1781768 | tf_op jit(solution)/shard_map/ppermute | solution.py:401
  37.5 2.6 %collective-permute-start.10 = (bf16[1168,128]{1,0:T(8,128)(2,1)S(1)}, bf16[1168,128]{1,0:T(8,128)(2,1)S(1)}, u32[]{:S(2)}, u32[]{:S(2)}) collective-permute-start(bf16[1168,128]{1,0:T(8,128)(2,1)S(1)} %slice.8), channel_id=1, source_target_pairs={{0,1},{1,0},{2,3},{3,2},{4,5},{5,4},{6,7},{7,6},{8,9},{9,8},{10,11... | collective-permute-start | bytes 897032 | tf_op jit(solution)/shard_map/ppermute | solution.py:404
  37.6 2.5 %collective-permute-start.11 = (bf16[1152,128]{1,0:T(8,128)(2,1)S(1)}, bf16[1152,128]{1,0:T(8,128)(2,1)S(1)}, u32[]{:S(2)}, u32[]{:S(2)}) collective-permute-start(bf16[1152,128]{1,0:T(8,128)(2,1)S(1)} %slice.9), channel_id=1, source_target_pairs={{0,1},{1,0},{2,3},{3,2},{4,5},{5,4},{6,7},{7,6},{8,9},{9,8},{10,11... | collective-permute-start | bytes 884744 | tf_op jit(solution)/shard_map/ppermute | solution.py:404
  49.3 2.0 %collective-permute-start.13 = (bf16[2320,128]{1,0:T(8,128)(2,1)S(1)}, bf16[2320,128]{1,0:T(8,128)(2,1)S(1)}, u32[]{:S(2)}, u32[]{:S(2)}) collective-permute-start(bf16[2320,128]{1,0:T(8,128)(2,1)S(1)} %collective-permute-done.12.refs_0_), channel_id=1, source_target_pairs={{0,1},{1,0},{2,3},{3,2},{4,5},{5,4},{6,7},{7,6},{8,9},{9,8},{10,11... | collective-permute-start | bytes 1781768 | tf_op jit(solution)/shard_map/ppermute | solution.py:404

commit v6 on v4

--- a/solution.py
+++ b/solution.py
@@ -398,8 +398,15 @@
     mask = block_mask.T
 
     def hop(x, tile):
-        targets = [tile(i, 1) if 0 <= tile(i, 1) < n_col else i for i in range(n_col)]
-        return lax.ppermute(x, "col", list(enumerate(targets)))
+        pairs = []
+        for i in range(n_col):
+            partner = tile(i, 1)
+            for layer in range(2):
+                if 0 <= partner < n_col:
+                    pairs.append((2 * i + layer, 2 * partner + layer))
+                else:
+                    pairs.append((2 * i + layer, 2 * i + 1 - layer))
+        return lax.ppermute(x, ("col", "layer"), pairs)
 
     def sibling(x):
         return lax.ppermute(x, "layer", [(0, 1), (1, 0)])

time: 61.8 us -> 60.2 us (0.974)
  starting transfers between devices: 25.6 us -> 21.2 us
  Pallas kernels: 16.3 us -> 18.2 us
  waiting for transfers between devices: 19 us -> 20.5 us
    ppermute x5, starting transfers between devices: 16.3 us -> 11.9 us  [hop(): return lax.ppermute(x, ('col', 'layer'), pairs)]
    ppermute x5, waiting for transfers between devices: 13.3 us -> 14.4 us  [hop(): return lax.ppermute(x, ('col', 'layer'), pairs)]
    pallas_call x1, Pallas kernels: 5.16 us -> 6.15 us  [multiply_second(): pl.pallas_call(functools.partial(second_kernel, near, n_row, n_col, nb_ro...]
    pallas_call x1, Pallas kernels: 4.33 us -> 5.23 us  [multiply_first(): pl.pallas_call(functools.partial(first_kernel, near, n_col, nb_rows, nb_c...]
    ppermute x3, waiting for transfers between devices: 2.71 us -> 3.35 us  [body(): lax.ppermute(sums, 'row', [(s, s ^ m) for s in range(n_row)])]
  transfers between devices with their start and end apart: 17 -> 17, of which waited for: 7 -> 9; matrix products, arithmetic and copies ran while one was open for 0% -> 0% of each run, Pallas kernels for 18% -> 21%
where the time goes in v6:
time: 60.2 us
  starting transfers between devices  21.2 us (35%)
  waiting for transfers between devices  20.5 us (34%)
  Pallas kernels  18.2 us (30%)
    ppermute x5, waiting for transfers between devices, hop(): return lax.ppermute(x, ('col', 'layer'), pairs)  14.4 us
    ppermute x5, starting transfers between devices, hop(): return lax.ppermute(x, ('col', 'layer'), pairs)  11.9 us
    pallas_call x1, Pallas kernels, multiply_second(): pl.pallas_call(functools.partial(second_kernel, near, n_row, n_col, nb_ro...  6.15 us
    pallas_call x1, Pallas kernels, multiply_first(): pl.pallas_call(functools.partial(first_kernel, near, n_col, nb_rows, nb_c...  5.23 us
    ppermute x3, starting transfers between devices, body(): lax.ppermute(sums, 'row', [(s, s ^ m) for s in range(n_row)])  3.55 us
    ppermute x3, waiting for transfers between devices, body(): lax.ppermute(sums, 'row', [(s, s ^ m) for s in range(n_row)])  3.35 us
    ppermute x2, starting transfers between devices, body(): ys[m] = lax.ppermute(own, 'row', [(s, s ^ m) for s in range(n_row)])  2.9 us
    pallas_call x2, Pallas kernels, multiply_late(): pl.pallas_call(functools.partial(late_kernel, n_col, nb_rows, nb_cols, x_...  2.45 us
  transfers between devices with their start and end apart: 17, of which 9 were waited for; matrix products, arithmetic and copies ran while one was open for 0% of the time, Pallas kernels for 21%

profile of v6, /device:TPU:0, one launch (start us, length us, event | category | flops | bytes accessed | tf_op | source)
XLA Modules:
  0.0 60.2 jit_solution(12680740133248043259)
XLA Ops:
  0.0 2.0 %compact.1.refs_0_ = bf16[2320,128]{1,0:T(8,128)(2,1)S(1)} custom-call(s32[6,12]{1,0:T(8,128)} %bitcast.4, bf16[1536,768]{1,0:T(8,128)(2,1)} %sim_ref.1), custom_call_target="tpu_custom_call" | custom-call | bytes 1179648 | tf_op jit(solution)/shard_map/compact/pallas_call | solution.py:65
  2.0 3.2 %collective-permute-start.4 = (bf16[2320,128]{1,0:T(8,128)(2,1)S(1)}, bf16[2320,128]{1,0:T(8,128)(2,1)S(1)}, u32[]{:S(2)}, u32[]{:S(2)}) collective-permute-start(bf16[2320,128]{1,0:T(8,128)(2,1)S(1)} %compact.1.refs_0_), channel_id=1, source_target_pairs={{0,2},{1,3},{2,0},{3,1},{4,6},{5,7},{6,4},{7,5},{8,10},{9,11},{10,... | collective-permute-start | bytes 1781768 | tf_op jit(solution)/shard_map/ppermute | solution.py:409
  5.2 0.0 collective-permute-start.3
  5.2 1.5 %collective-permute-start.9 = (bf16[2320,128]{1,0:T(8,128)(2,1)S(1)}, bf16[2320,128]{1,0:T(8,128)(2,1)}, u32[]{:S(2)}, u32[]{:S(2)}) collective-permute-start(bf16[2320,128]{1,0:T(8,128)(2,1)S(1)} %compact.1.refs_0_), channel_id=1, source_target_pairs={{0,16},{8,24},{16,0},{24,8},{1,17},{9,25},{17,1},{25,9},{2,18},{10... | collective-permute-start | bytes 1781768 | tf_op jit(solution)/shard_map/ppermute | solution.py:420
  6.7 0.2 collective-permute-start.2
  6.9 1.4 %collective-permute-start = (bf16[2320,128]{1,0:T(8,128)(2,1)S(1)}, bf16[2320,128]{1,0:T(8,128)(2,1)}, u32[]{:S(2)}, u32[]{:S(2)}) collective-permute-start(bf16[2320,128]{1,0:T(8,128)(2,1)S(1)} %compact.1.refs_0_), channel_id=1, source_target_pairs={{0,8},{8,0},{16,24},{24,16},{1,9},{9,1},{17,25},{25,17},{2,10},{10... | collective-permute-start | bytes 1781768 | tf_op jit(solution)/shard_map/ppermute | solution.py:420
  8.3 10.3 %collective-permute-done.4.refs_4_.refs_3_ = bf16[2320,128]{1,0:T(8,128)(2,1)S(1)} collective-permute-done((bf16[2320,128]{1,0:T(8,128)(2,1)S(1)}, bf16[2320,128]{1,0:T(8,128)(2,1)S(1)}, u32[]{:S(2)}, u32[]{:S(2)}) %collective-permute-start.4) | collective-permute-done | bytes 593952 | tf_op jit(solution)/shard_map/ppermute | solution.py:409
  18.6 0.0 collective-permute-start.7
  18.6 0.0 collective-permute-done.3.refs_2_
  18.6 3.3 %collective-permute-start.8 = (bf16[2320,128]{1,0:T(8,128)(2,1)}, bf16[2320,128]{1,0:T(8,128)(2,1)S(1)}, u32[]{:S(2)}, u32[]{:S(2)}) collective-permute-start(bf16[2320,128]{1,0:T(8,128)(2,1)} %collective-permute-done.3.refs_2_), channel_id=1, source_target_pairs={{0,2},{1,3},{2,0},{3,1},{4,6},{5,7},{6,4},{7,5},{8,10},{9,11},{10,... | collective-permute-start | bytes 1781768 | tf_op jit(solution)/shard_map/ppermute | solution.py:409
  22.0 0.1 pad_add_fusion.place_ref
  22.0 0.0 collective-permute-done.9.refs_2_
  22.0 0.0 collective-permute-start.6
  22.1 0.0 collective-permute-done.2.refs_3_.refs_1_
  22.1 0.5 collective-permute-start.5
  22.6 0.1 collective-permute-done.refs_1_
  22.6 1.4 %collective-permute-start.1 = (bf16[2320,128]{1,0:T(8,128)(2,1)}, bf16[2320,128]{1,0:T(8,128)(2,1)S(1)}, u32[]{:S(2)}, u32[]{:S(2)}) collective-permute-start(bf16[2320,128]{1,0:T(8,128)(2,1)} %collective-permute-done.refs_1_), channel_id=1, source_target_pairs={{0,16},{8,24},{16,0},{24,8},{1,17},{9,25},{17,1},{25,9},{2,18},{10... | collective-permute-start | bytes 1781768 | tf_op jit(solution)/shard_map/ppermute | solution.py:424
  24.1 5.2 %multiply_first.1 = (f32[73,128,128]{2,1,0:T(8,128)S(1)}, f32[7,8,128]{2,1,0:T(8,128)S(1)}, bf16[9280,128]{1,0:T(8,128)(2,1)S(1)}) custom-call(s32[3]{0:T(128)S(1)} %pad_add_fusion.place_ref, bf16[2320,128]{1,0:T(8,128)(2,1)S(1)} %compact.1.refs_0_, bf16[2320,128]{1,0:T(8,128)(2,1)} %collective-permute-done.refs_1_, ...), custom_call_target="tpu_custom_call" | custom-call | flops 100000000 | bytes 1000000 | tf_op jit(solution)/shard_map/multiply_first/pallas_call | solution.py:226
  29.3 0.0 collective-permute-done.7.refs_6_
  29.3 5.4 %collective-permute-start.12 = (bf16[2320,128]{1,0:T(8,128)(2,1)S(1)}, bf16[2320,128]{1,0:T(8,128)(2,1)S(1)}, u32[]{:S(2)}, u32[]{:S(2)}) collective-permute-start(bf16[2320,128]{1,0:T(8,128)(2,1)S(1)} %collective-permute-done.7.refs_6_), channel_id=1, source_target_pairs={{0,2},{1,3},{2,0},{3,1},{4,6},{5,7},{6,4},{7,5},{8,10},{9,11},{10,... | collective-permute-start | bytes 1781768 | tf_op jit(solution)/shard_map/ppermute | solution.py:409
  34.7 1.0 %collective-permute-done.8.refs_7_ = bf16[2320,128]{1,0:T(8,128)(2,1)S(1)} collective-permute-done((bf16[2320,128]{1,0:T(8,128)(2,1)}, bf16[2320,128]{1,0:T(8,128)(2,1)S(1)}, u32[]{:S(2)}, u32[]{:S(2)}) %collective-permute-start.8) | collective-permute-done | bytes 593952 | tf_op jit(solution)/shard_map/ppermute | solution.py:409
  35.7 0.1 broadcast_select_fusion
  35.8 0.1 collective-permute-start.10
  35.9 0.0 collective-permute-done.6.refs_5_
  35.9 0.6 collective-permute-start.11
  36.5 0.0 collective-permute-done.5.refs_4_
  36.5 1.7 %collective-permute-done.1.refs_0_ = bf16[2320,128]{1,0:T(8,128)(2,1)S(1)} collective-permute-done((bf16[2320,128]{1,0:T(8,128)(2,1)}, bf16[2320,128]{1,0:T(8,128)(2,1)S(1)}, u32[]{:S(2)}, u32[]{:S(2)}) %collective-permute-start.1) | collective-permute-done | bytes 593952 | tf_op jit(solution)/shard_map/ppermute | solution.py:424
  38.2 0.0 collective-permute-done.11.refs_9_
  38.2 0.0 collective-permute-done.10.refs_8_
  38.2 6.2 %multiply_second.1 = (f32[73,128,128]{2,1,0:T(8,128)S(1)}, f32[7,8,128]{2,1,0:T(8,128)S(1)}, bf16[9280,128]{1,0:T(8,128)(2,1)S(1)}, s32[384]{0:T(512)S(1)}, s32[48]{0:T(128)S(1)}) custom-call(s32[3]{0:T(128)S(1)} %pad_add_fusion.place_ref, ...), custom_call_target="tpu_custom_call", output_to_operand_aliasing={{0}: (11, {}), {1}: (12, {}), {2}: (13, {})} | custom-call | flops 100000000 | bytes 1000000 | tf_op jit(solution)/shard_map/multiply_second/pallas_call | solution.py:290
  44.3 3.1 %collective-permute-done.12.refs_0_ = bf16[2320,128]{1,0:T(8,128)(2,1)S(1)} collective-permute-done((bf16[2320,128]{1,0:T(8,128)(2,1)S(1)}, bf16[2320,128]{1,0:T(8,128)(2,1)S(1)}, u32[]{:S(2)}, u32[]{:S(2)}) %collective-permute-start.12) | collective-permute-done | bytes 593952 | tf_op jit(solution)/shard_map/ppermute | solution.py:409
  47.5 0.0 collective-permute-start.13
  47.5 1.0 %multiply_late.1 = (f32[73,128,128]{2,1,0:T(8,128)S(1)}, f32[7,8,128]{2,1,0:T(8,128)S(1)}) custom-call(s32[3]{0:T(128)S(1)} %pad_add_fusion.place_ref, s32[384]{0:T(512)S(1)} %get-tuple-element.28.slots_of, s32[48]{0:T(128)S(1)} %get-tuple-element.29.n_of, bf16[9280,128]{1,0:T(8,128)(2,1)S(1)} %get-tuple-element.30.y_blocks, ...), custom_call_target="tpu_custom_call", output_to_operand_aliasing={{0}: (5, {})} | custom-call | flops 100000000 | bytes 1000000 | tf_op jit(solution)/shard_map/multiply_late/pallas_call | solution.py:328
  48.5 1.0 %collective-permute-done.13.refs_0_ = bf16[2320,128]{1,0:T(8,128)(2,1)S(1)} collective-permute-done((bf16[2320,128]{1,0:T(8,128)(2,1)S(1)}, bf16[2320,128]{1,0:T(8,128)(2,1)S(1)}, u32[]{:S(2)}, u32[]{:S(2)}) %collective-permute-start.13) | collective-permute-done | bytes 593952 | tf_op jit(solution)/shard_map/ppermute | solution.py:412
  49.5 1.4 %multiply_last.1 = (f32[73,128,128]{2,1,0:T(8,128)S(1)}, f32[8,128]{1,0:T(8,128)S(1)}) custom-call(s32[3]{0:T(128)S(1)} %pad_add_fusion.place_ref, s32[384]{0:T(512)S(1)} %get-tuple-element.28.slots_of, s32[48]{0:T(128)S(1)} %get-tuple-element.29.n_of, bf16[9280,128]{1,0:T(8,128)(2,1)S(1)} %get-tuple-element.30.y_blocks, ...), custom_call_target="tpu_custom_call", output_to_operand_aliasing={{0}: (5, {})} | custom-call | flops 100000000 | bytes 1000000 | tf_op jit(solution)/shard_map/multiply_last/pallas_call | solution.py:328
  50.9 2.8 %collective-permute-start.16 = (f32[8,128]{1,0:T(8,128)S(1)}, f32[8,128]{1,0:T(8,128)S(1)}, u32[]{:S(2)}, u32[]{:S(2)}) collective-permute-start(f32[8,128]{1,0:T(8,128)S(1)} %get-tuple-element.38.refs_1_), channel_id=1, source_target_pairs={{0,24},{8,16},{16,8},{24,0},{1,25},{9,17},{17,9},{25,1},{2,26},{10... | collective-permute-start | bytes 12296 | tf_op jit(solution)/shard_map/ppermute | solution.py:451
  53.8 0.5 collective-permute-start.15
  54.2 0.3 collective-permute-start.14
  54.5 1.0 %collective-permute-done.16.refs_4_ = f32[8,128]{1,0:T(8,128)S(1)} collective-permute-done((f32[8,128]{1,0:T(8,128)S(1)}, f32[8,128]{1,0:T(8,128)S(1)}, u32[]{:S(2)}, u32[]{:S(2)}) %collective-permute-start.16) | collective-permute-done | bytes 4128 | tf_op jit(solution)/shard_map/ppermute | solution.py:451
  55.5 1.9 %collective-permute-done.15.refs_3_ = f32[8,128]{1,0:T(8,128)S(1)} collective-permute-done((f32[8,128]{1,0:T(8,128)S(1)}, f32[8,128]{1,0:T(8,128)S(1)}, u32[]{:S(2)}, u32[]{:S(2)}) %collective-permute-start.15) | collective-permute-done | bytes 4128 | tf_op jit(solution)/shard_map/ppermute | solution.py:451
  57.4 0.5 collective-permute-done.14.refs_2_
  57.8 2.3 %scale.1 = f32[1536,768]{1,0:T(8,128)} custom-call(f32[73,128,128]{2,1,0:T(8,128)S(1)} %get-tuple-element.37.refs_0_, f32[8,128]{1,0:T(8,128)S(1)} %get-tuple-element.38.refs_1_, f32[8,128]{1,0:T(8,128)S(1)} %collective-permute-done.14.refs_2_, f32[8,128]{1,0:T(8,128)S(1)} %collective-permute-done.15.refs_3_, f32[8,128]{1,0:T(8,128)S(1)} %collective-permute-done.16.refs_4_), custom_call_target="tpu_custom_call" | custom-call | flops 10000000 | bytes 10000000 | tf_op jit(solution)/shard_map/scale/pallas_call | solution.py:374
  (2 shorter events, 0.0 us)
Async XLA Ops:
  2.0 16.6 %collective-permute-start.4 = (bf16[2320,128]{1,0:T(8,128)(2,1)S(1)}, bf16[2320,128]{1,0:T(8,128)(2,1)S(1)}, u32[]{:S(2)}, u32[]{:S(2)}) collective-permute-start(bf16[2320,128]{1,0:T(8,128)(2,1)S(1)} %compact.1.refs_0_), channel_id=1, source_target_pairs={{0,2},{1,3},{2,0},{3,1},{4,6},{5,7},{6,4},{7,5},{8,10},{9,11},{10,... | collective-permute-start | bytes 1781768 | tf_op jit(solution)/shard_map/ppermute | solution.py:409
  5.2 13.4 %collective-permute-start.3 = (bf16[2320,128]{1,0:T(8,128)(2,1)S(1)}, bf16[2320,128]{1,0:T(8,128)(2,1)}, u32[]{:S(2)}, u32[]{:S(2)}) collective-permute-start(bf16[2320,128]{1,0:T(8,128)(2,1)S(1)} %compact.1.refs_0_), channel_id=1, source_target_pairs={{0,1},{1,0},{2,4},{3,5},{4,2},{5,3},{6,7},{7,6},{8,9},{9,8},{10,12... | collective-permute-start | bytes 1781768 | tf_op jit(solution)/shard_map/ppermute | solution.py:409
  5.2 16.8 %collective-permute-start.9 = (bf16[2320,128]{1,0:T(8,128)(2,1)S(1)}, bf16[2320,128]{1,0:T(8,128)(2,1)}, u32[]{:S(2)}, u32[]{:S(2)}) collective-permute-start(bf16[2320,128]{1,0:T(8,128)(2,1)S(1)} %compact.1.refs_0_), channel_id=1, source_target_pairs={{0,16},{8,24},{16,0},{24,8},{1,17},{9,25},{17,1},{25,9},{2,18},{10... | collective-permute-start | bytes 1781768 | tf_op jit(solution)/shard_map/ppermute | solution.py:420
  6.7 15.4 %collective-permute-start.2 = (bf16[2320,128]{1,0:T(8,128)(2,1)S(1)}, bf16[2320,128]{1,0:T(8,128)(2,1)S(1)}, u32[]{:S(2)}, u32[]{:S(2)}) collective-permute-start(bf16[2320,128]{1,0:T(8,128)(2,1)S(1)} %compact.1.refs_0_), channel_id=1, source_target_pairs={{0,1},{1,0},{2,3},{3,2},{4,5},{5,4},{6,7},{7,6},{8,9},{9,8},{10,11... | collective-permute-start | bytes 1781768 | tf_op jit(solution)/shard_map/ppermute | solution.py:412
  6.9 15.7 %collective-permute-start = (bf16[2320,128]{1,0:T(8,128)(2,1)S(1)}, bf16[2320,128]{1,0:T(8,128)(2,1)}, u32[]{:S(2)}, u32[]{:S(2)}) collective-permute-start(bf16[2320,128]{1,0:T(8,128)(2,1)S(1)} %compact.1.refs_0_), channel_id=1, source_target_pairs={{0,8},{8,0},{16,24},{24,16},{1,9},{9,1},{17,25},{25,17},{2,10},{10... | collective-permute-start | bytes 1781768 | tf_op jit(solution)/shard_map/ppermute | solution.py:420
  18.6 10.7 %collective-permute-start.7 = (bf16[2320,128]{1,0:T(8,128)(2,1)S(1)}, bf16[2320,128]{1,0:T(8,128)(2,1)S(1)}, u32[]{:S(2)}, u32[]{:S(2)}) collective-permute-start(bf16[2320,128]{1,0:T(8,128)(2,1)S(1)} %collective-permute-done.4.refs_4_.refs_3_), channel_id=1, source_target_pairs={{0,1},{1,0},{2,4},{3,5},{4,2},{5,3},{6,7},{7,6},{8,9},{9,8},{10,12... | collective-permute-start | bytes 1781768 | tf_op jit(solution)/shard_map/ppermute | solution.py:409
  18.6 17.1 %collective-permute-start.8 = (bf16[2320,128]{1,0:T(8,128)(2,1)}, bf16[2320,128]{1,0:T(8,128)(2,1)S(1)}, u32[]{:S(2)}, u32[]{:S(2)}) collective-permute-start(bf16[2320,128]{1,0:T(8,128)(2,1)} %collective-permute-done.3.refs_2_), channel_id=1, source_target_pairs={{0,2},{1,3},{2,0},{3,1},{4,6},{5,7},{6,4},{7,5},{8,10},{9,11},{10,... | collective-permute-start | bytes 1781768 | tf_op jit(solution)/shard_map/ppermute | solution.py:409
  22.0 13.9 %collective-permute-start.6 = (bf16[2320,128]{1,0:T(8,128)(2,1)S(1)}, bf16[2320,128]{1,0:T(8,128)(2,1)S(1)}, u32[]{:S(2)}, u32[]{:S(2)}) collective-permute-start(bf16[2320,128]{1,0:T(8,128)(2,1)S(1)} %collective-permute-done.4.refs_4_.refs_3_), channel_id=1, source_target_pairs={{0,1},{1,0},{2,3},{3,2},{4,5},{5,4},{6,7},{7,6},{8,9},{9,8},{10,11... | collective-permute-start | bytes 1781768 | tf_op jit(solution)/shard_map/ppermute | solution.py:412
  22.1 14.4 %collective-permute-start.5 = (bf16[2320,128]{1,0:T(8,128)(2,1)}, bf16[2320,128]{1,0:T(8,128)(2,1)S(1)}, u32[]{:S(2)}, u32[]{:S(2)}) collective-permute-start(bf16[2320,128]{1,0:T(8,128)(2,1)} %collective-permute-done.3.refs_2_), channel_id=1, source_target_pairs={{0,1},{1,0},{2,3},{3,2},{4,5},{5,4},{6,7},{7,6},{8,9},{9,8},{10,11... | collective-permute-start | bytes 1781768 | tf_op jit(solution)/shard_map/ppermute | solution.py:412
  22.6 15.6 %collective-permute-start.1 = (bf16[2320,128]{1,0:T(8,128)(2,1)}, bf16[2320,128]{1,0:T(8,128)(2,1)S(1)}, u32[]{:S(2)}, u32[]{:S(2)}) collective-permute-start(bf16[2320,128]{1,0:T(8,128)(2,1)} %collective-permute-done.refs_1_), channel_id=1, source_target_pairs={{0,16},{8,24},{16,0},{24,8},{1,17},{9,25},{17,1},{25,9},{2,18},{10... | collective-permute-start | bytes 1781768 | tf_op jit(solution)/shard_map/ppermute | solution.py:424
  29.3 18.2 %collective-permute-start.12 = (bf16[2320,128]{1,0:T(8,128)(2,1)S(1)}, bf16[2320,128]{1,0:T(8,128)(2,1)S(1)}, u32[]{:S(2)}, u32[]{:S(2)}) collective-permute-start(bf16[2320,128]{1,0:T(8,128)(2,1)S(1)} %collective-permute-done.7.refs_6_), channel_id=1, source_target_pairs={{0,2},{1,3},{2,0},{3,1},{4,6},{5,7},{6,4},{7,5},{8,10},{9,11},{10,... | collective-permute-start | bytes 1781768 | tf_op jit(solution)/shard_map/ppermute | solution.py:409
  35.8 2.4 %collective-permute-start.10 = (bf16[1168,128]{1,0:T(8,128)(2,1)S(1)}, bf16[1168,128]{1,0:T(8,128)(2,1)S(1)}, u32[]{:S(2)}, u32[]{:S(2)}) collective-permute-start(bf16[1168,128]{1,0:T(8,128)(2,1)S(1)} %slice.8), channel_id=1, source_target_pairs={{0,1},{1,0},{2,3},{3,2},{4,5},{5,4},{6,7},{7,6},{8,9},{9,8},{10,11... | collective-permute-start | bytes 897032 | tf_op jit(solution)/shard_map/ppermute | solution.py:412
  35.9 2.2 %collective-permute-start.11 = (bf16[1152,128]{1,0:T(8,128)(2,1)S(1)}, bf16[1152,128]{1,0:T(8,128)(2,1)S(1)}, u32[]{:S(2)}, u32[]{:S(2)}) collective-permute-start(bf16[1152,128]{1,0:T(8,128)(2,1)S(1)} %slice.9), channel_id=1, source_target_pairs={{0,1},{1,0},{2,3},{3,2},{4,5},{5,4},{6,7},{7,6},{8,9},{9,8},{10,11... | collective-permute-start | bytes 884744 | tf_op jit(solution)/shard_map/ppermute | solution.py:412
  47.5 2.0 %collective-permute-start.13 = (bf16[2320,128]{1,0:T(8,128)(2,1)S(1)}, bf16[2320,128]{1,0:T(8,128)(2,1)S(1)}, u32[]{:S(2)}, u32[]{:S(2)}) collective-permute-start(bf16[2320,128]{1,0:T(8,128)(2,1)S(1)} %collective-permute-done.12.refs_0_), channel_id=1, source_target_pairs={{0,1},{1,0},{2,3},{3,2},{4,5},{5,4},{6,7},{7,6},{8,9},{9,8},{10,11... | collective-permute-start | bytes 1781768 | tf_op jit(solution)/shard_map/ppermute | solution.py:412
  50.9 4.6 %collective-permute-start.16 = (f32[8,128]{1,0:T(8,128)S(1)}, f32[8,128]{1,0:T(8,128)S(1)}, u32[]{:S(2)}, u32[]{:S(2)}) collective-permute-start(f32[8,128]{1,0:T(8,128)S(1)} %get-tuple-element.38.refs_1_), channel_id=1, source_target_pairs={{0,24},{8,16},{16,8},{24,0},{1,25},{9,17},{17,9},{25,1},{2,26},{10... | collective-permute-start | bytes 12296 | tf_op jit(solution)/shard_map/ppermute | solution.py:451
  53.8 3.6 %collective-permute-start.15 = (f32[8,128]{1,0:T(8,128)S(1)}, f32[8,128]{1,0:T(8,128)S(1)}, u32[]{:S(2)}, u32[]{:S(2)}) collective-permute-start(f32[8,128]{1,0:T(8,128)S(1)} %get-tuple-element.38.refs_1_), channel_id=1, source_target_pairs={{0,16},{8,24},{16,0},{24,8},{1,17},{9,25},{17,1},{25,9},{2,18},{10... | collective-permute-start | bytes 12296 | tf_op jit(solution)/shard_map/ppermute | solution.py:451
  54.2 3.6 %collective-permute-start.14 = (f32[8,128]{1,0:T(8,128)S(1)}, f32[8,128]{1,0:T(8,128)S(1)}, u32[]{:S(2)}, u32[]{:S(2)}) collective-permute-start(f32[8,128]{1,0:T(8,128)S(1)} %get-tuple-element.38.refs_1_), channel_id=1, source_target_pairs={{0,8},{8,0},{16,24},{24,16},{1,9},{9,1},{17,25},{25,17},{2,10},{10... | collective-permute-start | bytes 12296 | tf_op jit(solution)/shard_map/ppermute | solution.py:451

commit v7 on v6

--- a/solution.py
+++ b/solution.py
@@ -184,7 +184,7 @@
 def first_kernel(near, n_col, nb_rows, nb_cols, place_ref, *refs):
     own_ref, refs = refs[0], refs[1:]
     y_refs, refs = refs[: len(near) - 1], refs[len(near) - 1 :]
-    x_refs, refs = refs[:2], refs[2:]
+    x_refs, refs = refs[:3], refs[3:]
     acc, sums, y_blocks, slots_of, n_of, own_head, heads, places, todo, y_sems = refs
     r, c, l = place_ref[0], place_ref[1], place_ref[2]
     head_copy = pltpu.make_async_copy(own_ref.at[pl.ds(0, HEAD), :], own_head, y_sems.at[len(near)])
@@ -202,7 +202,8 @@
     for copy in copies:
         copy.wait()
     shares = [(c, l, 0, y_blocks, r * ROWS), (c, 1 - l, len(near), x_refs[0], 0)]
-    shares.append((chain_tile(c, 1, False), l, len(near) + 1, x_refs[1], 0))
+    shares.append((chain_tile(c, 1, True), l, len(near) + 1, x_refs[1], 0))
+    shares.append((chain_tile(c, 1, False), l, len(near) + 2, x_refs[2], 0))
     for tile, layer, at, x_ref, x_base in shares:
         valid, first_inner = inner_of(n_col, nb_rows, nb_cols, tile, layer)
         n_slots = jnp.where(valid, places[at, SLOTS], 0)
@@ -230,13 +231,13 @@
             jax.ShapeDtypeStruct((nb_cols + 1, 8, BLK), jnp.float32),
             jax.ShapeDtypeStruct((n_row * ROWS, BLK), jnp.bfloat16),
         ],
-        in_specs=[SMEM, ANY] + [VMEM] * (shares - 1),
+        in_specs=[SMEM] + [VMEM] * shares,
         out_specs=[VMEM] * 3,
         scratch_shapes=lists[:2]
         + [pltpu.VMEM((HEAD, BLK), jnp.bfloat16)]
         + lists[2:]
         + [pltpu.SemaphoreType.DMA((len(near) + 1,))],
-        compiler_params=pltpu.CompilerParams(vmem_limit_bytes=24 * MIB),
+        compiler_params=pltpu.CompilerParams(vmem_limit_bytes=8 * MIB),
         cost_estimate=SMALL,
         name="multiply_first",
     )(place, *[ys[m] for m in near], *xs)
@@ -295,7 +296,7 @@
         out_specs=[VMEM] * 3 + [SMEM] * 2,
         input_output_aliases={len(operands) - 3 + at: at for at in range(3)},
         scratch_shapes=lists[2:] + [pltpu.SemaphoreType.DMA((len(distant),))],
-        compiler_params=pltpu.CompilerParams(vmem_limit_bytes=24 * MIB),
+        compiler_params=pltpu.CompilerParams(vmem_limit_bytes=8 * MIB),
         cost_estimate=SMALL,
         name="multiply_second",
     )(*operands)
@@ -333,7 +334,7 @@
         input_output_aliases={len(operands) - 2: 0},
         scratch_shapes=([pltpu.VMEM(sums.shape, jnp.float32)] if is_last else [])
         + list_scratch(0, nb_rows, nb_cols, len(xs))[2:],
-        compiler_params=pltpu.CompilerParams(vmem_limit_bytes=24 * MIB),
+        compiler_params=pltpu.CompilerParams(vmem_limit_bytes=8 * MIB),
         cost_estimate=SMALL,
         name="multiply_last" if is_last else "multiply_late",
     )(*operands)
@@ -377,7 +378,7 @@
         in_specs=[VMEM] * (1 + len(sums)),
         out_specs=ANY,
         scratch_shapes=[pltpu.VMEM(shape, jnp.float32), pltpu.SemaphoreType.DMA((nb_rows,))],
-        compiler_params=pltpu.CompilerParams(vmem_limit_bytes=16 * MIB),
+        compiler_params=pltpu.CompilerParams(vmem_limit_bytes=8 * MIB),
         cost_estimate=pl.CostEstimate(flops=10**7, bytes_accessed=10 * 10**6, transcendentals=0),
         name="scale",
     )(product, *sums)
@@ -422,9 +423,8 @@
         if ys[m] is None:
             bit = 1 << (m.bit_length() - 1)
             ys[m] = lax.ppermute(ys[m ^ bit], "row", [(s, s ^ bit) for s in range(n_row)])
-    first_xs = [sibling(own), even]
-    shares = [((0, False, True, True), first_xs[0]), ((1, True, False, False), odd), ((1, False, False, True), even)]
-    first_xs[1], _ = lax.optimization_barrier((even, odd))
+    first_xs = [sibling(own), odd, even]
+    shares = [((0, False, True, True), first_xs[0]), ((1, True, False, True), odd), ((1, False, False, True), even)]
     acc, sums, y_blocks = multiply_first(place, near, ys, first_xs, n_row, n_col, nb_rows, nb_cols)
     for step in range(1, n_col - 2):
         shares.append(((step, True, True, False), sibling(odd)))

time: 60.2 us -> 60.8 us (level)
  waiting for transfers between devices: 20.5 us -> 22.7 us
  Pallas kernels: 18.2 us -> 16.4 us
    pallas_call x1, Pallas kernels: 6.15 us -> 3.5 us  [multiply_second(): pl.pallas_call(functools.partial(second_kernel, near, n_row, n_col, nb_ro...]
    ppermute x5, waiting for transfers between devices: 14.4 us -> 16.4 us  [hop(): return lax.ppermute(x, ('col', 'layer'), pairs)]
    pallas_call x1, Pallas kernels: 2.01 us -> 2.91 us  [compact(): pl.pallas_call(compact_kernel, out_shape=pltpu.VMEM((ROWS, BLK), similari...]
  transfers between devices with their start and end apart: 17 -> 17, of which waited for: 9 -> 9; matrix products, arithmetic and copies ran while one was open for 0% -> 0% of each run, Pallas kernels for 21% -> 16%
where the time goes in v7:
time: 60.8 us; the launch traced here: 60.4 us
  waiting for transfers between devices  22.7 us (37%)
  starting transfers between devices  21 us (35%)
  Pallas kernels  16.4 us (27%)
    ppermute x5, waiting for transfers between devices, hop(): return lax.ppermute(x, ('col', 'layer'), pairs)  16.4 us
    ppermute x5, starting transfers between devices, hop(): return lax.ppermute(x, ('col', 'layer'), pairs)  11.9 us
    pallas_call x1, Pallas kernels, multiply_first(): pl.pallas_call(functools.partial(first_kernel, near, n_col, nb_rows, nb_c...  5.31 us
    ppermute x3, starting transfers between devices, body(): lax.ppermute(sums, 'row', [(s, s ^ m) for s in range(n_row)])  3.55 us
    pallas_call x1, Pallas kernels, multiply_second(): pl.pallas_call(functools.partial(second_kernel, near, n_row, n_col, nb_ro...  3.5 us
    pallas_call x1, Pallas kernels, compact(): pl.pallas_call(compact_kernel, out_shape=pltpu.VMEM((ROWS, BLK), similari...  2.91 us
    ppermute x3, waiting for transfers between devices, body(): lax.ppermute(sums, 'row', [(s, s ^ m) for s in range(n_row)])  2.9 us
    ppermute x2, starting transfers between devices, body(): ys[m] = lax.ppermute(own, 'row', [(s, s ^ m) for s in range(n_row)])  2.83 us
  transfers between devices with their start and end apart: 17, of which 9 were waited for; matrix products, arithmetic and copies ran while one was open for 0% of the time, Pallas kernels for 16%

profile of v7, /device:TPU:0, one launch (start us, length us, event | category | flops | bytes accessed | tf_op | source)
XLA Modules:
  0.0 60.4 jit_solution(8713388987538258026)
XLA Ops:
  0.0 2.9 %compact.1.refs_0_ = bf16[2320,128]{1,0:T(8,128)(2,1)} custom-call(s32[6,12]{1,0:T(8,128)} %bitcast.4, bf16[1536,768]{1,0:T(8,128)(2,1)} %sim_ref.1), custom_call_target="tpu_custom_call" | custom-call | bytes 1179648 | tf_op jit(solution)/shard_map/compact/pallas_call | solution.py:65
  2.9 3.1 %collective-permute-start.4 = (bf16[2320,128]{1,0:T(8,128)(2,1)}, bf16[2320,128]{1,0:T(8,128)(2,1)S(1)}, u32[]{:S(2)}, u32[]{:S(2)}) collective-permute-start(bf16[2320,128]{1,0:T(8,128)(2,1)} %compact.1.refs_0_), channel_id=1, source_target_pairs={{0,2},{1,3},{2,0},{3,1},{4,6},{5,7},{6,4},{7,5},{8,10},{9,11},{10,... | collective-permute-start | bytes 1781768 | tf_op jit(solution)/shard_map/ppermute | solution.py:410
  6.0 0.0 collective-permute-start.3
  6.0 1.5 %collective-permute-start.9 = (bf16[2320,128]{1,0:T(8,128)(2,1)}, bf16[2320,128]{1,0:T(8,128)(2,1)}, u32[]{:S(2)}, u32[]{:S(2)}) collective-permute-start(bf16[2320,128]{1,0:T(8,128)(2,1)} %compact.1.refs_0_), channel_id=1, source_target_pairs={{0,16},{8,24},{16,0},{24,8},{1,17},{9,25},{17,1},{25,9},{2,18},{10... | collective-permute-start | bytes 1781768 | tf_op jit(solution)/shard_map/ppermute | solution.py:421
  7.5 0.2 collective-permute-start.2
  7.8 1.3 %collective-permute-start = (bf16[2320,128]{1,0:T(8,128)(2,1)}, bf16[2320,128]{1,0:T(8,128)(2,1)}, u32[]{:S(2)}, u32[]{:S(2)}) collective-permute-start(bf16[2320,128]{1,0:T(8,128)(2,1)} %compact.1.refs_0_), channel_id=1, source_target_pairs={{0,8},{8,0},{16,24},{24,16},{1,9},{9,1},{17,25},{25,17},{2,10},{10... | collective-permute-start | bytes 1781768 | tf_op jit(solution)/shard_map/ppermute | solution.py:421
  9.1 10.5 %collective-permute-done.4.refs_5_.refs_3_ = bf16[2320,128]{1,0:T(8,128)(2,1)S(1)} collective-permute-done((bf16[2320,128]{1,0:T(8,128)(2,1)}, bf16[2320,128]{1,0:T(8,128)(2,1)S(1)}, u32[]{:S(2)}, u32[]{:S(2)}) %collective-permute-start.4) | collective-permute-done | bytes 593952 | tf_op jit(solution)/shard_map/ppermute | solution.py:410
  19.6 0.0 collective-permute-start.7
  19.6 0.0 collective-permute-done.3.refs_4_.refs_2_
  19.6 3.3 %collective-permute-start.8 = (bf16[2320,128]{1,0:T(8,128)(2,1)S(1)}, bf16[2320,128]{1,0:T(8,128)(2,1)S(1)}, u32[]{:S(2)}, u32[]{:S(2)}) collective-permute-start(bf16[2320,128]{1,0:T(8,128)(2,1)S(1)} %collective-permute-done.3.refs_4_.refs_2_), channel_id=1, source_target_pairs={{0,2},{1,3},{2,0},{3,1},{4,6},{5,7},{6,4},{7,5},{8,10},{9,11},{10,... | collective-permute-start | bytes 1781768 | tf_op jit(solution)/shard_map/ppermute | solution.py:410
  22.9 0.1 pad_add_fusion.place_ref
  23.0 0.0 collective-permute-done.9.refs_2_
  23.0 0.0 collective-permute-start.6
  23.0 0.0 collective-permute-done.2.refs_3_.refs_1_
  23.0 0.5 collective-permute-start.5
  23.5 0.2 collective-permute-done.refs_1_
  23.7 1.4 %collective-permute-start.1 = (bf16[2320,128]{1,0:T(8,128)(2,1)}, bf16[2320,128]{1,0:T(8,128)(2,1)S(1)}, u32[]{:S(2)}, u32[]{:S(2)}) collective-permute-start(bf16[2320,128]{1,0:T(8,128)(2,1)} %collective-permute-done.refs_1_), channel_id=1, source_target_pairs={{0,16},{8,24},{16,0},{24,8},{1,17},{9,25},{17,1},{25,9},{2,18},{10... | collective-permute-start | bytes 1781768 | tf_op jit(solution)/shard_map/ppermute | solution.py:425
  25.1 5.3 %multiply_first.1 = (f32[73,128,128]{2,1,0:T(8,128)S(1)}, f32[7,8,128]{2,1,0:T(8,128)S(1)}, bf16[9280,128]{1,0:T(8,128)(2,1)S(1)}) custom-call(s32[3]{0:T(128)S(1)} %pad_add_fusion.place_ref, bf16[2320,128]{1,0:T(8,128)(2,1)} %compact.1.refs_0_, bf16[2320,128]{1,0:T(8,128)(2,1)} %collective-permute-done.refs_1_, ...), custom_call_target="tpu_custom_call" | custom-call | flops 100000000 | bytes 1000000 | tf_op jit(solution)/shard_map/multiply_first/pallas_call | solution.py:227
  30.4 0.0 collective-permute-done.7.refs_6_
  30.4 5.4 %collective-permute-start.12 = (bf16[2320,128]{1,0:T(8,128)(2,1)S(1)}, bf16[2320,128]{1,0:T(8,128)(2,1)S(1)}, u32[]{:S(2)}, u32[]{:S(2)}) collective-permute-start(bf16[2320,128]{1,0:T(8,128)(2,1)S(1)} %collective-permute-done.7.refs_6_), channel_id=1, source_target_pairs={{0,2},{1,3},{2,0},{3,1},{4,6},{5,7},{6,4},{7,5},{8,10},{9,11},{10,... | collective-permute-start | bytes 1781768 | tf_op jit(solution)/shard_map/ppermute | solution.py:410
  35.9 0.2 collective-permute-done.8.refs_7_
  36.1 0.1 broadcast_select_fusion
  36.2 0.1 collective-permute-start.10
  36.3 0.0 collective-permute-done.6.refs_5_
  36.3 0.6 collective-permute-start.11
  36.8 0.0 collective-permute-done.5.refs_4_
  36.8 2.3 %collective-permute-done.1.refs_0_ = bf16[2320,128]{1,0:T(8,128)(2,1)S(1)} collective-permute-done((bf16[2320,128]{1,0:T(8,128)(2,1)}, bf16[2320,128]{1,0:T(8,128)(2,1)S(1)}, u32[]{:S(2)}, u32[]{:S(2)}) %collective-permute-start.1) | collective-permute-done | bytes 593952 | tf_op jit(solution)/shard_map/ppermute | solution.py:425
  39.1 0.0 collective-permute-done.11.refs_9_
  39.1 0.0 collective-permute-done.10.refs_8_
  39.1 3.5 %multiply_second.1 = (f32[73,128,128]{2,1,0:T(8,128)S(1)}, f32[7,8,128]{2,1,0:T(8,128)S(1)}, bf16[9280,128]{1,0:T(8,128)(2,1)S(1)}, s32[384]{0:T(512)S(1)}, s32[48]{0:T(128)S(1)}) custom-call(s32[3]{0:T(128)S(1)} %pad_add_fusion.place_ref, ...), custom_call_target="tpu_custom_call", output_to_operand_aliasing={{0}: (11, {}), {1}: (12, {}), {2}: (13, {})} | custom-call | flops 100000000 | bytes 1000000 | tf_op jit(solution)/shard_map/multiply_second/pallas_call | solution.py:291
  42.6 5.7 %collective-permute-done.12.refs_0_ = bf16[2320,128]{1,0:T(8,128)(2,1)S(1)} collective-permute-done((bf16[2320,128]{1,0:T(8,128)(2,1)S(1)}, bf16[2320,128]{1,0:T(8,128)(2,1)S(1)}, u32[]{:S(2)}, u32[]{:S(2)}) %collective-permute-start.12) | collective-permute-done | bytes 593952 | tf_op jit(solution)/shard_map/ppermute | solution.py:410
  48.3 0.0 collective-permute-start.13
  48.3 1.0 %multiply_late.1 = (f32[73,128,128]{2,1,0:T(8,128)S(1)}, f32[7,8,128]{2,1,0:T(8,128)S(1)}) custom-call(s32[3]{0:T(128)S(1)} %pad_add_fusion.place_ref, s32[384]{0:T(512)S(1)} %get-tuple-element.26.slots_of, s32[48]{0:T(128)S(1)} %get-tuple-element.27.n_of, bf16[9280,128]{1,0:T(8,128)(2,1)S(1)} %get-tuple-element.28.y_blocks, ...), custom_call_target="tpu_custom_call", output_to_operand_aliasing={{0}: (5, {})} | custom-call | flops 100000000 | bytes 1000000 | tf_op jit(solution)/shard_map/multiply_late/pallas_call | solution.py:329
  49.3 1.0 %collective-permute-done.13.refs_0_ = bf16[2320,128]{1,0:T(8,128)(2,1)S(1)} collective-permute-done((bf16[2320,128]{1,0:T(8,128)(2,1)S(1)}, bf16[2320,128]{1,0:T(8,128)(2,1)S(1)}, u32[]{:S(2)}, u32[]{:S(2)}) %collective-permute-start.13) | collective-permute-done | bytes 593952 | tf_op jit(solution)/shard_map/ppermute | solution.py:413
  50.3 1.3 %multiply_last.1 = (f32[73,128,128]{2,1,0:T(8,128)S(1)}, f32[8,128]{1,0:T(8,128)S(1)}) custom-call(s32[3]{0:T(128)S(1)} %pad_add_fusion.place_ref, s32[384]{0:T(512)S(1)} %get-tuple-element.26.slots_of, s32[48]{0:T(128)S(1)} %get-tuple-element.27.n_of, bf16[9280,128]{1,0:T(8,128)(2,1)S(1)} %get-tuple-element.28.y_blocks, ...), custom_call_target="tpu_custom_call", output_to_operand_aliasing={{0}: (5, {})} | custom-call | flops 100000000 | bytes 1000000 | tf_op jit(solution)/shard_map/multiply_last/pallas_call | solution.py:329
  51.7 2.5 %collective-permute-start.16 = (f32[8,128]{1,0:T(8,128)S(1)}, f32[8,128]{1,0:T(8,128)S(1)}, u32[]{:S(2)}, u32[]{:S(2)}) collective-permute-start(f32[8,128]{1,0:T(8,128)S(1)} %get-tuple-element.36.refs_1_), channel_id=1, source_target_pairs={{0,24},{8,16},{16,8},{24,0},{1,25},{9,17},{17,9},{25,1},{2,26},{10... | collective-permute-start | bytes 12296 | tf_op jit(solution)/shard_map/ppermute | solution.py:451
  54.1 0.4 collective-permute-start.15
  54.5 0.7 %collective-permute-start.14 = (f32[8,128]{1,0:T(8,128)S(1)}, f32[8,128]{1,0:T(8,128)S(1)}, u32[]{:S(2)}, u32[]{:S(2)}) collective-permute-start(f32[8,128]{1,0:T(8,128)S(1)} %get-tuple-element.36.refs_1_), channel_id=1, source_target_pairs={{0,8},{8,0},{16,24},{24,16},{1,9},{9,1},{17,25},{25,17},{2,10},{10... | collective-permute-start | bytes 12296 | tf_op jit(solution)/shard_map/ppermute | solution.py:451
  55.2 1.0 %collective-permute-done.16.refs_4_ = f32[8,128]{1,0:T(8,128)S(1)} collective-permute-done((f32[8,128]{1,0:T(8,128)S(1)}, f32[8,128]{1,0:T(8,128)S(1)}, u32[]{:S(2)}, u32[]{:S(2)}) %collective-permute-start.16) | collective-permute-done | bytes 4128 | tf_op jit(solution)/shard_map/ppermute | solution.py:451
  56.2 1.5 %collective-permute-done.15.refs_3_ = f32[8,128]{1,0:T(8,128)S(1)} collective-permute-done((f32[8,128]{1,0:T(8,128)S(1)}, f32[8,128]{1,0:T(8,128)S(1)}, u32[]{:S(2)}, u32[]{:S(2)}) %collective-permute-start.15) | collective-permute-done | bytes 4128 | tf_op jit(solution)/shard_map/ppermute | solution.py:451
  57.7 0.4 collective-permute-done.14.refs_2_
  58.1 2.3 %scale.1 = f32[1536,768]{1,0:T(8,128)} custom-call(f32[73,128,128]{2,1,0:T(8,128)S(1)} %get-tuple-element.35.refs_0_, f32[8,128]{1,0:T(8,128)S(1)} %get-tuple-element.36.refs_1_, f32[8,128]{1,0:T(8,128)S(1)} %collective-permute-done.14.refs_2_, f32[8,128]{1,0:T(8,128)S(1)} %collective-permute-done.15.refs_3_, f32[8,128]{1,0:T(8,128)S(1)} %collective-permute-done.16.refs_4_), custom_call_target="tpu_custom_call" | custom-call | flops 10000000 | bytes 10000000 | tf_op jit(solution)/shard_map/scale/pallas_call | solution.py:375
  (2 shorter events, 0.0 us)
Async XLA Ops:
  2.9 16.6 %collective-permute-start.4 = (bf16[2320,128]{1,0:T(8,128)(2,1)}, bf16[2320,128]{1,0:T(8,128)(2,1)S(1)}, u32[]{:S(2)}, u32[]{:S(2)}) collective-permute-start(bf16[2320,128]{1,0:T(8,128)(2,1)} %compact.1.refs_0_), channel_id=1, source_target_pairs={{0,2},{1,3},{2,0},{3,1},{4,6},{5,7},{6,4},{7,5},{8,10},{9,11},{10,... | collective-permute-start | bytes 1781768 | tf_op jit(solution)/shard_map/ppermute | solution.py:410
  6.0 13.6 %collective-permute-start.3 = (bf16[2320,128]{1,0:T(8,128)(2,1)}, bf16[2320,128]{1,0:T(8,128)(2,1)S(1)}, u32[]{:S(2)}, u32[]{:S(2)}) collective-permute-start(bf16[2320,128]{1,0:T(8,128)(2,1)} %compact.1.refs_0_), channel_id=1, source_target_pairs={{0,1},{1,0},{2,4},{3,5},{4,2},{5,3},{6,7},{7,6},{8,9},{9,8},{10,12... | collective-permute-start | bytes 1781768 | tf_op jit(solution)/shard_map/ppermute | solution.py:410
  6.0 17.0 %collective-permute-start.9 = (bf16[2320,128]{1,0:T(8,128)(2,1)}, bf16[2320,128]{1,0:T(8,128)(2,1)}, u32[]{:S(2)}, u32[]{:S(2)}) collective-permute-start(bf16[2320,128]{1,0:T(8,128)(2,1)} %compact.1.refs_0_), channel_id=1, source_target_pairs={{0,16},{8,24},{16,0},{24,8},{1,17},{9,25},{17,1},{25,9},{2,18},{10... | collective-permute-start | bytes 1781768 | tf_op jit(solution)/shard_map/ppermute | solution.py:421
  7.5 15.5 %collective-permute-start.2 = (bf16[2320,128]{1,0:T(8,128)(2,1)}, bf16[2320,128]{1,0:T(8,128)(2,1)S(1)}, u32[]{:S(2)}, u32[]{:S(2)}) collective-permute-start(bf16[2320,128]{1,0:T(8,128)(2,1)} %compact.1.refs_0_), channel_id=1, source_target_pairs={{0,1},{1,0},{2,3},{3,2},{4,5},{5,4},{6,7},{7,6},{8,9},{9,8},{10,11... | collective-permute-start | bytes 1781768 | tf_op jit(solution)/shard_map/ppermute | solution.py:413
  7.8 15.9 %collective-permute-start = (bf16[2320,128]{1,0:T(8,128)(2,1)}, bf16[2320,128]{1,0:T(8,128)(2,1)}, u32[]{:S(2)}, u32[]{:S(2)}) collective-permute-start(bf16[2320,128]{1,0:T(8,128)(2,1)} %compact.1.refs_0_), channel_id=1, source_target_pairs={{0,8},{8,0},{16,24},{24,16},{1,9},{9,1},{17,25},{25,17},{2,10},{10... | collective-permute-start | bytes 1781768 | tf_op jit(solution)/shard_map/ppermute | solution.py:421
  19.6 10.8 %collective-permute-start.7 = (bf16[2320,128]{1,0:T(8,128)(2,1)S(1)}, bf16[2320,128]{1,0:T(8,128)(2,1)S(1)}, u32[]{:S(2)}, u32[]{:S(2)}) collective-permute-start(bf16[2320,128]{1,0:T(8,128)(2,1)S(1)} %collective-permute-done.4.refs_5_.refs_3_), channel_id=1, source_target_pairs={{0,1},{1,0},{2,4},{3,5},{4,2},{5,3},{6,7},{7,6},{8,9},{9,8},{10,12... | collective-permute-start | bytes 1781768 | tf_op jit(solution)/shard_map/ppermute | solution.py:410
  19.6 16.5 %collective-permute-start.8 = (bf16[2320,128]{1,0:T(8,128)(2,1)S(1)}, bf16[2320,128]{1,0:T(8,128)(2,1)S(1)}, u32[]{:S(2)}, u32[]{:S(2)}) collective-permute-start(bf16[2320,128]{1,0:T(8,128)(2,1)S(1)} %collective-permute-done.3.refs_4_.refs_2_), channel_id=1, source_target_pairs={{0,2},{1,3},{2,0},{3,1},{4,6},{5,7},{6,4},{7,5},{8,10},{9,11},{10,... | collective-permute-start | bytes 1781768 | tf_op jit(solution)/shard_map/ppermute | solution.py:410
  23.0 13.3 %collective-permute-start.6 = (bf16[2320,128]{1,0:T(8,128)(2,1)S(1)}, bf16[2320,128]{1,0:T(8,128)(2,1)S(1)}, u32[]{:S(2)}, u32[]{:S(2)}) collective-permute-start(bf16[2320,128]{1,0:T(8,128)(2,1)S(1)} %collective-permute-done.4.refs_5_.refs_3_), channel_id=1, source_target_pairs={{0,1},{1,0},{2,3},{3,2},{4,5},{5,4},{6,7},{7,6},{8,9},{9,8},{10,11... | collective-permute-start | bytes 1781768 | tf_op jit(solution)/shard_map/ppermute | solution.py:413
  23.0 13.8 %collective-permute-start.5 = (bf16[2320,128]{1,0:T(8,128)(2,1)S(1)}, bf16[2320,128]{1,0:T(8,128)(2,1)S(1)}, u32[]{:S(2)}, u32[]{:S(2)}) collective-permute-start(bf16[2320,128]{1,0:T(8,128)(2,1)S(1)} %collective-permute-done.3.refs_4_.refs_2_), channel_id=1, source_target_pairs={{0,1},{1,0},{2,3},{3,2},{4,5},{5,4},{6,7},{7,6},{8,9},{9,8},{10,11... | collective-permute-start | bytes 1781768 | tf_op jit(solution)/shard_map/ppermute | solution.py:413
  23.7 15.4 %collective-permute-start.1 = (bf16[2320,128]{1,0:T(8,128)(2,1)}, bf16[2320,128]{1,0:T(8,128)(2,1)S(1)}, u32[]{:S(2)}, u32[]{:S(2)}) collective-permute-start(bf16[2320,128]{1,0:T(8,128)(2,1)} %collective-permute-done.refs_1_), channel_id=1, source_target_pairs={{0,16},{8,24},{16,0},{24,8},{1,17},{9,25},{17,1},{25,9},{2,18},{10... | collective-permute-start | bytes 1781768 | tf_op jit(solution)/shard_map/ppermute | solution.py:425
  30.4 17.9 %collective-permute-start.12 = (bf16[2320,128]{1,0:T(8,128)(2,1)S(1)}, bf16[2320,128]{1,0:T(8,128)(2,1)S(1)}, u32[]{:S(2)}, u32[]{:S(2)}) collective-permute-start(bf16[2320,128]{1,0:T(8,128)(2,1)S(1)} %collective-permute-done.7.refs_6_), channel_id=1, source_target_pairs={{0,2},{1,3},{2,0},{3,1},{4,6},{5,7},{6,4},{7,5},{8,10},{9,11},{10,... | collective-permute-start | bytes 1781768 | tf_op jit(solution)/shard_map/ppermute | solution.py:410
  36.2 2.9 %collective-permute-start.10 = (bf16[1168,128]{1,0:T(8,128)(2,1)S(1)}, bf16[1168,128]{1,0:T(8,128)(2,1)S(1)}, u32[]{:S(2)}, u32[]{:S(2)}) collective-permute-start(bf16[1168,128]{1,0:T(8,128)(2,1)S(1)} %slice.8), channel_id=1, source_target_pairs={{0,1},{1,0},{2,3},{3,2},{4,5},{5,4},{6,7},{7,6},{8,9},{9,8},{10,11... | collective-permute-start | bytes 897032 | tf_op jit(solution)/shard_map/ppermute | solution.py:413
  36.3 2.8 %collective-permute-start.11 = (bf16[1152,128]{1,0:T(8,128)(2,1)S(1)}, bf16[1152,128]{1,0:T(8,128)(2,1)S(1)}, u32[]{:S(2)}, u32[]{:S(2)}) collective-permute-start(bf16[1152,128]{1,0:T(8,128)(2,1)S(1)} %slice.9), channel_id=1, source_target_pairs={{0,1},{1,0},{2,3},{3,2},{4,5},{5,4},{6,7},{7,6},{8,9},{9,8},{10,11... | collective-permute-start | bytes 884744 | tf_op jit(solution)/shard_map/ppermute | solution.py:413
  48.3 2.0 %collective-permute-start.13 = (bf16[2320,128]{1,0:T(8,128)(2,1)S(1)}, bf16[2320,128]{1,0:T(8,128)(2,1)S(1)}, u32[]{:S(2)}, u32[]{:S(2)}) collective-permute-start(bf16[2320,128]{1,0:T(8,128)(2,1)S(1)} %collective-permute-done.12.refs_0_), channel_id=1, source_target_pairs={{0,1},{1,0},{2,3},{3,2},{4,5},{5,4},{6,7},{7,6},{8,9},{9,8},{10,11... | collective-permute-start | bytes 1781768 | tf_op jit(solution)/shard_map/ppermute | solution.py:413
  51.7 4.6 %collective-permute-start.16 = (f32[8,128]{1,0:T(8,128)S(1)}, f32[8,128]{1,0:T(8,128)S(1)}, u32[]{:S(2)}, u32[]{:S(2)}) collective-permute-start(f32[8,128]{1,0:T(8,128)S(1)} %get-tuple-element.36.refs_1_), channel_id=1, source_target_pairs={{0,24},{8,16},{16,8},{24,0},{1,25},{9,17},{17,9},{25,1},{2,26},{10... | collective-permute-start | bytes 12296 | tf_op jit(solution)/shard_map/ppermute | solution.py:451
  54.1 3.6 %collective-permute-start.15 = (f32[8,128]{1,0:T(8,128)S(1)}, f32[8,128]{1,0:T(8,128)S(1)}, u32[]{:S(2)}, u32[]{:S(2)}) collective-permute-start(f32[8,128]{1,0:T(8,128)S(1)} %get-tuple-element.36.refs_1_), channel_id=1, source_target_pairs={{0,16},{8,24},{16,0},{24,8},{1,17},{9,25},{17,1},{25,9},{2,18},{10... | collective-permute-start | bytes 12296 | tf_op jit(solution)/shard_map/ppermute | solution.py:451
  54.5 3.6 %collective-permute-start.14 = (f32[8,128]{1,0:T(8,128)S(1)}, f32[8,128]{1,0:T(8,128)S(1)}, u32[]{:S(2)}, u32[]{:S(2)}) collective-permute-start(f32[8,128]{1,0:T(8,128)S(1)} %get-tuple-element.36.refs_1_), channel_id=1, source_target_pairs={{0,8},{8,0},{16,24},{24,16},{1,9},{9,1},{17,25},{25,17},{2,10},{10... | collective-permute-start | bytes 12296 | tf_op jit(solution)/shard_map/ppermute | solution.py:451

commit v8 on v6

--- a/solution.py
+++ b/solution.py
@@ -12,6 +12,7 @@
 SHARE = SLOTS * BLK
 HEAD = 16
 HALF = 9
+PIECE = 64
 ROWS = HEAD + SHARE
 FIRST_ROWS = HEAD + HALF * BLK
 UNROLL = 8
@@ -348,16 +349,16 @@
     factor = scaling / total[0:nb_cols, :]
 
     def out_copy(i):
-        rows = pl.ds(pl.multiple_of(i * BLK, BLK), BLK)
+        rows = pl.ds(pl.multiple_of(i * PIECE, PIECE), PIECE)
         return pltpu.make_async_copy(scaled.at[rows, :], out.at[rows, :], sems.at[i])
 
     def square(i, carry):
-        for j in range(nb_cols):
-            value = product[i * nb_cols + j]
-            scaled[pl.ds(pl.multiple_of(i * BLK, BLK), BLK), j * BLK : (j + 1) * BLK] = (
-                value * value * factor[j : j + 1, :]
-            )
-        out_copy(i).start()
+        for part in range(BLK // PIECE):
+            for j in range(nb_cols):
+                value = product[i * nb_cols + j, part * PIECE : (part + 1) * PIECE, :]
+                rows = pl.ds(pl.multiple_of(i * BLK + part * PIECE, PIECE), PIECE)
+                scaled[rows, j * BLK : (j + 1) * BLK] = value * value * factor[j : j + 1, :]
+            out_copy(i * (BLK // PIECE) + part).start()
         return carry
 
     lax.fori_loop(0, nb_rows, square, 0)
@@ -366,7 +367,7 @@
         out_copy(i).wait()
         return carry
 
-    lax.fori_loop(0, nb_rows, wait, 0)
+    lax.fori_loop(0, nb_rows * (BLK // PIECE), wait, 0)
 
 
 def scale(product, sums, scaling, nb_rows, nb_cols):
@@ -376,7 +377,7 @@
         out_shape=jax.ShapeDtypeStruct(shape, jnp.float32),
         in_specs=[VMEM] * (1 + len(sums)),
         out_specs=ANY,
-        scratch_shapes=[pltpu.VMEM(shape, jnp.float32), pltpu.SemaphoreType.DMA((nb_rows,))],
+        scratch_shapes=[pltpu.VMEM(shape, jnp.float32), pltpu.SemaphoreType.DMA((nb_rows * (BLK // PIECE),))],
         compiler_params=pltpu.CompilerParams(vmem_limit_bytes=16 * MIB),
         cost_estimate=pl.CostEstimate(flops=10**7, bytes_accessed=10 * 10**6, transcendentals=0),
         name="scale",

time: 60.2 us -> 59.9 us (level)
  Pallas kernels: 18.2 us -> 17.2 us
    pallas_call x1, Pallas kernels: 6.15 us -> 5.33 us  [multiply_second(): pl.pallas_call(functools.partial(second_kernel, near, n_row, n_col, nb_ro...]
  transfers between devices with their start and end apart: 17 -> 17, of which waited for: 9 -> 9; matrix products, arithmetic and copies ran while one was open for 0% -> 0% of each run, Pallas kernels for 21% -> 20%
where the time goes in v8:
time: 59.9 us; the launch traced here: 59.7 us
  starting transfers between devices  21.4 us (36%)
  waiting for transfers between devices  20.7 us (35%)
  Pallas kernels  17.2 us (29%)
    ppermute x5, waiting for transfers between devices, hop(): return lax.ppermute(x, ('col', 'layer'), pairs)  14.9 us
    ppermute x5, starting transfers between devices, hop(): return lax.ppermute(x, ('col', 'layer'), pairs)  12.2 us
    pallas_call x1, Pallas kernels, multiply_second(): pl.pallas_call(functools.partial(second_kernel, near, n_row, n_col, nb_ro...  5.33 us
    pallas_call x1, Pallas kernels, multiply_first(): pl.pallas_call(functools.partial(first_kernel, near, n_col, nb_rows, nb_c...  4.98 us
    ppermute x3, starting transfers between devices, body(): lax.ppermute(sums, 'row', [(s, s ^ m) for s in range(n_row)])  3.56 us
    ppermute x3, waiting for transfers between devices, body(): lax.ppermute(sums, 'row', [(s, s ^ m) for s in range(n_row)])  3.43 us
    ppermute x2, starting transfers between devices, body(): ys[m] = lax.ppermute(own, 'row', [(s, s ^ m) for s in range(n_row)])  2.98 us
    pallas_call x2, Pallas kernels, multiply_late(): pl.pallas_call(functools.partial(late_kernel, n_col, nb_rows, nb_cols, x_...  2.47 us
  transfers between devices with their start and end apart: 17, of which 9 were waited for; matrix products, arithmetic and copies ran while one was open for 0% of the time, Pallas kernels for 20%

profile of v8, /device:TPU:0, one launch (start us, length us, event | category | flops | bytes accessed | tf_op | source)
XLA Modules:
  0.0 59.7 jit_solution(9770969186366183072)
XLA Ops:
  0.0 2.1 %compact.1.refs_0_ = bf16[2320,128]{1,0:T(8,128)(2,1)S(1)} custom-call(s32[6,12]{1,0:T(8,128)} %bitcast.4, bf16[1536,768]{1,0:T(8,128)(2,1)} %sim_ref.1), custom_call_target="tpu_custom_call" | custom-call | bytes 1179648 | tf_op jit(solution)/shard_map/compact/pallas_call | solution.py:66
  2.1 3.1 %collective-permute-start.4 = (bf16[2320,128]{1,0:T(8,128)(2,1)S(1)}, bf16[2320,128]{1,0:T(8,128)(2,1)S(1)}, u32[]{:S(2)}, u32[]{:S(2)}) collective-permute-start(bf16[2320,128]{1,0:T(8,128)(2,1)S(1)} %compact.1.refs_0_), channel_id=1, source_target_pairs={{0,2},{1,3},{2,0},{3,1},{4,6},{5,7},{6,4},{7,5},{8,10},{9,11},{10,... | collective-permute-start | bytes 1781768 | tf_op jit(solution)/shard_map/ppermute | solution.py:410
  5.2 0.0 collective-permute-start.3
  5.2 1.5 %collective-permute-start.9 = (bf16[2320,128]{1,0:T(8,128)(2,1)S(1)}, bf16[2320,128]{1,0:T(8,128)(2,1)}, u32[]{:S(2)}, u32[]{:S(2)}) collective-permute-start(bf16[2320,128]{1,0:T(8,128)(2,1)S(1)} %compact.1.refs_0_), channel_id=1, source_target_pairs={{0,16},{8,24},{16,0},{24,8},{1,17},{9,25},{17,1},{25,9},{2,18},{10... | collective-permute-start | bytes 1781768 | tf_op jit(solution)/shard_map/ppermute | solution.py:421
  6.7 0.2 collective-permute-start.2
  7.0 1.5 %collective-permute-start = (bf16[2320,128]{1,0:T(8,128)(2,1)S(1)}, bf16[2320,128]{1,0:T(8,128)(2,1)}, u32[]{:S(2)}, u32[]{:S(2)}) collective-permute-start(bf16[2320,128]{1,0:T(8,128)(2,1)S(1)} %compact.1.refs_0_), channel_id=1, source_target_pairs={{0,8},{8,0},{16,24},{24,16},{1,9},{9,1},{17,25},{25,17},{2,10},{10... | collective-permute-start | bytes 1781768 | tf_op jit(solution)/shard_map/ppermute | solution.py:421
  8.4 10.2 %collective-permute-done.4.refs_4_.refs_3_ = bf16[2320,128]{1,0:T(8,128)(2,1)S(1)} collective-permute-done((bf16[2320,128]{1,0:T(8,128)(2,1)S(1)}, bf16[2320,128]{1,0:T(8,128)(2,1)S(1)}, u32[]{:S(2)}, u32[]{:S(2)}) %collective-permute-start.4) | collective-permute-done | bytes 593952 | tf_op jit(solution)/shard_map/ppermute | solution.py:410
  18.6 0.0 collective-permute-start.7
  18.6 0.0 collective-permute-done.3.refs_2_
  18.6 3.3 %collective-permute-start.8 = (bf16[2320,128]{1,0:T(8,128)(2,1)}, bf16[2320,128]{1,0:T(8,128)(2,1)S(1)}, u32[]{:S(2)}, u32[]{:S(2)}) collective-permute-start(bf16[2320,128]{1,0:T(8,128)(2,1)} %collective-permute-done.3.refs_2_), channel_id=1, source_target_pairs={{0,2},{1,3},{2,0},{3,1},{4,6},{5,7},{6,4},{7,5},{8,10},{9,11},{10,... | collective-permute-start | bytes 1781768 | tf_op jit(solution)/shard_map/ppermute | solution.py:410
  21.9 0.1 pad_add_fusion.place_ref
  22.0 0.0 collective-permute-done.9.refs_2_
  22.0 0.0 collective-permute-start.6
  22.0 0.0 collective-permute-done.2.refs_3_.refs_1_
  22.0 0.5 collective-permute-start.5
  22.5 0.2 collective-permute-done.refs_1_
  22.7 1.4 %collective-permute-start.1 = (bf16[2320,128]{1,0:T(8,128)(2,1)}, bf16[2320,128]{1,0:T(8,128)(2,1)S(1)}, u32[]{:S(2)}, u32[]{:S(2)}) collective-permute-start(bf16[2320,128]{1,0:T(8,128)(2,1)} %collective-permute-done.refs_1_), channel_id=1, source_target_pairs={{0,16},{8,24},{16,0},{24,8},{1,17},{9,25},{17,1},{25,9},{2,18},{10... | collective-permute-start | bytes 1781768 | tf_op jit(solution)/shard_map/ppermute | solution.py:425
  24.0 5.0 %multiply_first.1 = (f32[73,128,128]{2,1,0:T(8,128)S(1)}, f32[7,8,128]{2,1,0:T(8,128)S(1)}, bf16[9280,128]{1,0:T(8,128)(2,1)S(1)}) custom-call(s32[3]{0:T(128)S(1)} %pad_add_fusion.place_ref, bf16[2320,128]{1,0:T(8,128)(2,1)S(1)} %compact.1.refs_0_, bf16[2320,128]{1,0:T(8,128)(2,1)} %collective-permute-done.refs_1_, ...), custom_call_target="tpu_custom_call" | custom-call | flops 100000000 | bytes 1000000 | tf_op jit(solution)/shard_map/multiply_first/pallas_call | solution.py:227
  29.0 0.0 collective-permute-done.7.refs_6_
  29.0 5.7 %collective-permute-start.12 = (bf16[2320,128]{1,0:T(8,128)(2,1)S(1)}, bf16[2320,128]{1,0:T(8,128)(2,1)S(1)}, u32[]{:S(2)}, u32[]{:S(2)}) collective-permute-start(bf16[2320,128]{1,0:T(8,128)(2,1)S(1)} %collective-permute-done.7.refs_6_), channel_id=1, source_target_pairs={{0,2},{1,3},{2,0},{3,1},{4,6},{5,7},{6,4},{7,5},{8,10},{9,11},{10,... | collective-permute-start | bytes 1781768 | tf_op jit(solution)/shard_map/ppermute | solution.py:410
  34.8 0.7 %collective-permute-done.8.refs_7_ = bf16[2320,128]{1,0:T(8,128)(2,1)S(1)} collective-permute-done((bf16[2320,128]{1,0:T(8,128)(2,1)}, bf16[2320,128]{1,0:T(8,128)(2,1)S(1)}, u32[]{:S(2)}, u32[]{:S(2)}) %collective-permute-start.8) | collective-permute-done | bytes 593952 | tf_op jit(solution)/shard_map/ppermute | solution.py:410
  35.5 0.1 broadcast_select_fusion
  35.6 0.1 collective-permute-start.10
  35.7 0.0 collective-permute-done.6.refs_5_
  35.7 0.6 collective-permute-start.11
  36.3 0.0 collective-permute-done.5.refs_4_
  36.3 1.8 %collective-permute-done.1.refs_0_ = bf16[2320,128]{1,0:T(8,128)(2,1)S(1)} collective-permute-done((bf16[2320,128]{1,0:T(8,128)(2,1)}, bf16[2320,128]{1,0:T(8,128)(2,1)S(1)}, u32[]{:S(2)}, u32[]{:S(2)}) %collective-permute-start.1) | collective-permute-done | bytes 593952 | tf_op jit(solution)/shard_map/ppermute | solution.py:425
  38.1 0.0 collective-permute-done.11.refs_9_
  38.1 0.0 collective-permute-done.10.refs_8_
  38.1 5.3 %multiply_second.1 = (f32[73,128,128]{2,1,0:T(8,128)S(1)}, f32[7,8,128]{2,1,0:T(8,128)S(1)}, bf16[9280,128]{1,0:T(8,128)(2,1)S(1)}, s32[384]{0:T(512)S(1)}, s32[48]{0:T(128)S(1)}) custom-call(s32[3]{0:T(128)S(1)} %pad_add_fusion.place_ref, ...), custom_call_target="tpu_custom_call", output_to_operand_aliasing={{0}: (11, {}), {1}: (12, {}), {2}: (13, {})} | custom-call | flops 100000000 | bytes 1000000 | tf_op jit(solution)/shard_map/multiply_second/pallas_call | solution.py:291
  43.5 3.9 %collective-permute-done.12.refs_0_ = bf16[2320,128]{1,0:T(8,128)(2,1)S(1)} collective-permute-done((bf16[2320,128]{1,0:T(8,128)(2,1)S(1)}, bf16[2320,128]{1,0:T(8,128)(2,1)S(1)}, u32[]{:S(2)}, u32[]{:S(2)}) %collective-permute-start.12) | collective-permute-done | bytes 593952 | tf_op jit(solution)/shard_map/ppermute | solution.py:410
  47.4 0.0 collective-permute-start.13
  47.4 1.6 %multiply_late.1 = (f32[73,128,128]{2,1,0:T(8,128)S(1)}, f32[7,8,128]{2,1,0:T(8,128)S(1)}) custom-call(s32[3]{0:T(128)S(1)} %pad_add_fusion.place_ref, s32[384]{0:T(512)S(1)} %get-tuple-element.28.slots_of, s32[48]{0:T(128)S(1)} %get-tuple-element.29.n_of, bf16[9280,128]{1,0:T(8,128)(2,1)S(1)} %get-tuple-element.30.y_blocks, ...), custom_call_target="tpu_custom_call", output_to_operand_aliasing={{0}: (5, {})} | custom-call | flops 100000000 | bytes 1000000 | tf_op jit(solution)/shard_map/multiply_late/pallas_call | solution.py:329
  49.0 0.4 collective-permute-done.13.refs_0_
  49.4 0.9 %multiply_last.1 = (f32[73,128,128]{2,1,0:T(8,128)S(1)}, f32[8,128]{1,0:T(8,128)S(1)}) custom-call(s32[3]{0:T(128)S(1)} %pad_add_fusion.place_ref, s32[384]{0:T(512)S(1)} %get-tuple-element.28.slots_of, s32[48]{0:T(128)S(1)} %get-tuple-element.29.n_of, bf16[9280,128]{1,0:T(8,128)(2,1)S(1)} %get-tuple-element.30.y_blocks, ...), custom_call_target="tpu_custom_call", output_to_operand_aliasing={{0}: (5, {})} | custom-call | flops 100000000 | bytes 1000000 | tf_op jit(solution)/shard_map/multiply_last/pallas_call | solution.py:329
  50.3 2.9 %collective-permute-start.16 = (f32[8,128]{1,0:T(8,128)S(1)}, f32[8,128]{1,0:T(8,128)S(1)}, u32[]{:S(2)}, u32[]{:S(2)}) collective-permute-start(f32[8,128]{1,0:T(8,128)S(1)} %get-tuple-element.38.refs_1_), channel_id=1, source_target_pairs={{0,24},{8,16},{16,8},{24,0},{1,25},{9,17},{17,9},{25,1},{2,26},{10... | collective-permute-start | bytes 12296 | tf_op jit(solution)/shard_map/ppermute | solution.py:452
  53.2 0.5 collective-permute-start.15
  53.7 0.2 collective-permute-start.14
  53.9 1.0 %collective-permute-done.16.refs_4_ = f32[8,128]{1,0:T(8,128)S(1)} collective-permute-done((f32[8,128]{1,0:T(8,128)S(1)}, f32[8,128]{1,0:T(8,128)S(1)}, u32[]{:S(2)}, u32[]{:S(2)}) %collective-permute-start.16) | collective-permute-done | bytes 4128 | tf_op jit(solution)/shard_map/ppermute | solution.py:452
  54.9 2.0 %collective-permute-done.15.refs_3_ = f32[8,128]{1,0:T(8,128)S(1)} collective-permute-done((f32[8,128]{1,0:T(8,128)S(1)}, f32[8,128]{1,0:T(8,128)S(1)}, u32[]{:S(2)}, u32[]{:S(2)}) %collective-permute-start.15) | collective-permute-done | bytes 4128 | tf_op jit(solution)/shard_map/ppermute | solution.py:452
  56.8 0.5 collective-permute-done.14.refs_2_
  57.3 2.4 %scale.1 = f32[1536,768]{1,0:T(8,128)} custom-call(f32[73,128,128]{2,1,0:T(8,128)S(1)} %get-tuple-element.37.refs_0_, f32[8,128]{1,0:T(8,128)S(1)} %get-tuple-element.38.refs_1_, f32[8,128]{1,0:T(8,128)S(1)} %collective-permute-done.14.refs_2_, f32[8,128]{1,0:T(8,128)S(1)} %collective-permute-done.15.refs_3_, f32[8,128]{1,0:T(8,128)S(1)} %collective-permute-done.16.refs_4_), custom_call_target="tpu_custom_call" | custom-call | flops 10000000 | bytes 10000000 | tf_op jit(solution)/shard_map/scale/pallas_call | solution.py:375
  (2 shorter events, 0.0 us)
Async XLA Ops:
  2.1 16.6 %collective-permute-start.4 = (bf16[2320,128]{1,0:T(8,128)(2,1)S(1)}, bf16[2320,128]{1,0:T(8,128)(2,1)S(1)}, u32[]{:S(2)}, u32[]{:S(2)}) collective-permute-start(bf16[2320,128]{1,0:T(8,128)(2,1)S(1)} %compact.1.refs_0_), channel_id=1, source_target_pairs={{0,2},{1,3},{2,0},{3,1},{4,6},{5,7},{6,4},{7,5},{8,10},{9,11},{10,... | collective-permute-start | bytes 1781768 | tf_op jit(solution)/shard_map/ppermute | solution.py:410
  5.2 13.4 %collective-permute-start.3 = (bf16[2320,128]{1,0:T(8,128)(2,1)S(1)}, bf16[2320,128]{1,0:T(8,128)(2,1)}, u32[]{:S(2)}, u32[]{:S(2)}) collective-permute-start(bf16[2320,128]{1,0:T(8,128)(2,1)S(1)} %compact.1.refs_0_), channel_id=1, source_target_pairs={{0,1},{1,0},{2,4},{3,5},{4,2},{5,3},{6,7},{7,6},{8,9},{9,8},{10,12... | collective-permute-start | bytes 1781768 | tf_op jit(solution)/shard_map/ppermute | solution.py:410
  5.2 16.8 %collective-permute-start.9 = (bf16[2320,128]{1,0:T(8,128)(2,1)S(1)}, bf16[2320,128]{1,0:T(8,128)(2,1)}, u32[]{:S(2)}, u32[]{:S(2)}) collective-permute-start(bf16[2320,128]{1,0:T(8,128)(2,1)S(1)} %compact.1.refs_0_), channel_id=1, source_target_pairs={{0,16},{8,24},{16,0},{24,8},{1,17},{9,25},{17,1},{25,9},{2,18},{10... | collective-permute-start | bytes 1781768 | tf_op jit(solution)/shard_map/ppermute | solution.py:421
  6.7 15.3 %collective-permute-start.2 = (bf16[2320,128]{1,0:T(8,128)(2,1)S(1)}, bf16[2320,128]{1,0:T(8,128)(2,1)S(1)}, u32[]{:S(2)}, u32[]{:S(2)}) collective-permute-start(bf16[2320,128]{1,0:T(8,128)(2,1)S(1)} %compact.1.refs_0_), channel_id=1, source_target_pairs={{0,1},{1,0},{2,3},{3,2},{4,5},{5,4},{6,7},{7,6},{8,9},{9,8},{10,11... | collective-permute-start | bytes 1781768 | tf_op jit(solution)/shard_map/ppermute | solution.py:413
  7.0 15.7 %collective-permute-start = (bf16[2320,128]{1,0:T(8,128)(2,1)S(1)}, bf16[2320,128]{1,0:T(8,128)(2,1)}, u32[]{:S(2)}, u32[]{:S(2)}) collective-permute-start(bf16[2320,128]{1,0:T(8,128)(2,1)S(1)} %compact.1.refs_0_), channel_id=1, source_target_pairs={{0,8},{8,0},{16,24},{24,16},{1,9},{9,1},{17,25},{25,17},{2,10},{10... | collective-permute-start | bytes 1781768 | tf_op jit(solution)/shard_map/ppermute | solution.py:421
  18.6 10.4 %collective-permute-start.7 = (bf16[2320,128]{1,0:T(8,128)(2,1)S(1)}, bf16[2320,128]{1,0:T(8,128)(2,1)S(1)}, u32[]{:S(2)}, u32[]{:S(2)}) collective-permute-start(bf16[2320,128]{1,0:T(8,128)(2,1)S(1)} %collective-permute-done.4.refs_4_.refs_3_), channel_id=1, source_target_pairs={{0,1},{1,0},{2,4},{3,5},{4,2},{5,3},{6,7},{7,6},{8,9},{9,8},{10,12... | collective-permute-start | bytes 1781768 | tf_op jit(solution)/shard_map/ppermute | solution.py:410
  18.6 16.9 %collective-permute-start.8 = (bf16[2320,128]{1,0:T(8,128)(2,1)}, bf16[2320,128]{1,0:T(8,128)(2,1)S(1)}, u32[]{:S(2)}, u32[]{:S(2)}) collective-permute-start(bf16[2320,128]{1,0:T(8,128)(2,1)} %collective-permute-done.3.refs_2_), channel_id=1, source_target_pairs={{0,2},{1,3},{2,0},{3,1},{4,6},{5,7},{6,4},{7,5},{8,10},{9,11},{10,... | collective-permute-start | bytes 1781768 | tf_op jit(solution)/shard_map/ppermute | solution.py:410
  22.0 13.7 %collective-permute-start.6 = (bf16[2320,128]{1,0:T(8,128)(2,1)S(1)}, bf16[2320,128]{1,0:T(8,128)(2,1)S(1)}, u32[]{:S(2)}, u32[]{:S(2)}) collective-permute-start(bf16[2320,128]{1,0:T(8,128)(2,1)S(1)} %collective-permute-done.4.refs_4_.refs_3_), channel_id=1, source_target_pairs={{0,1},{1,0},{2,3},{3,2},{4,5},{5,4},{6,7},{7,6},{8,9},{9,8},{10,11... | collective-permute-start | bytes 1781768 | tf_op jit(solution)/shard_map/ppermute | solution.py:413
  22.0 14.3 %collective-permute-start.5 = (bf16[2320,128]{1,0:T(8,128)(2,1)}, bf16[2320,128]{1,0:T(8,128)(2,1)S(1)}, u32[]{:S(2)}, u32[]{:S(2)}) collective-permute-start(bf16[2320,128]{1,0:T(8,128)(2,1)} %collective-permute-done.3.refs_2_), channel_id=1, source_target_pairs={{0,1},{1,0},{2,3},{3,2},{4,5},{5,4},{6,7},{7,6},{8,9},{9,8},{10,11... | collective-permute-start | bytes 1781768 | tf_op jit(solution)/shard_map/ppermute | solution.py:413
  22.7 15.5 %collective-permute-start.1 = (bf16[2320,128]{1,0:T(8,128)(2,1)}, bf16[2320,128]{1,0:T(8,128)(2,1)S(1)}, u32[]{:S(2)}, u32[]{:S(2)}) collective-permute-start(bf16[2320,128]{1,0:T(8,128)(2,1)} %collective-permute-done.refs_1_), channel_id=1, source_target_pairs={{0,16},{8,24},{16,0},{24,8},{1,17},{9,25},{17,1},{25,9},{2,18},{10... | collective-permute-start | bytes 1781768 | tf_op jit(solution)/shard_map/ppermute | solution.py:425
  29.0 18.4 %collective-permute-start.12 = (bf16[2320,128]{1,0:T(8,128)(2,1)S(1)}, bf16[2320,128]{1,0:T(8,128)(2,1)S(1)}, u32[]{:S(2)}, u32[]{:S(2)}) collective-permute-start(bf16[2320,128]{1,0:T(8,128)(2,1)S(1)} %collective-permute-done.7.refs_6_), channel_id=1, source_target_pairs={{0,2},{1,3},{2,0},{3,1},{4,6},{5,7},{6,4},{7,5},{8,10},{9,11},{10,... | collective-permute-start | bytes 1781768 | tf_op jit(solution)/shard_map/ppermute | solution.py:410
  35.6 2.5 %collective-permute-start.10 = (bf16[1168,128]{1,0:T(8,128)(2,1)S(1)}, bf16[1168,128]{1,0:T(8,128)(2,1)S(1)}, u32[]{:S(2)}, u32[]{:S(2)}) collective-permute-start(bf16[1168,128]{1,0:T(8,128)(2,1)S(1)} %slice.8), channel_id=1, source_target_pairs={{0,1},{1,0},{2,3},{3,2},{4,5},{5,4},{6,7},{7,6},{8,9},{9,8},{10,11... | collective-permute-start | bytes 897032 | tf_op jit(solution)/shard_map/ppermute | solution.py:413
  35.7 2.4 %collective-permute-start.11 = (bf16[1152,128]{1,0:T(8,128)(2,1)S(1)}, bf16[1152,128]{1,0:T(8,128)(2,1)S(1)}, u32[]{:S(2)}, u32[]{:S(2)}) collective-permute-start(bf16[1152,128]{1,0:T(8,128)(2,1)S(1)} %slice.9), channel_id=1, source_target_pairs={{0,1},{1,0},{2,3},{3,2},{4,5},{5,4},{6,7},{7,6},{8,9},{9,8},{10,11... | collective-permute-start | bytes 884744 | tf_op jit(solution)/shard_map/ppermute | solution.py:413
  47.4 2.0 %collective-permute-start.13 = (bf16[2320,128]{1,0:T(8,128)(2,1)S(1)}, bf16[2320,128]{1,0:T(8,128)(2,1)S(1)}, u32[]{:S(2)}, u32[]{:S(2)}) collective-permute-start(bf16[2320,128]{1,0:T(8,128)(2,1)S(1)} %collective-permute-done.12.refs_0_), channel_id=1, source_target_pairs={{0,1},{1,0},{2,3},{3,2},{4,5},{5,4},{6,7},{7,6},{8,9},{9,8},{10,11... | collective-permute-start | bytes 1781768 | tf_op jit(solution)/shard_map/ppermute | solution.py:413
  50.3 4.6 %collective-permute-start.16 = (f32[8,128]{1,0:T(8,128)S(1)}, f32[8,128]{1,0:T(8,128)S(1)}, u32[]{:S(2)}, u32[]{:S(2)}) collective-permute-start(f32[8,128]{1,0:T(8,128)S(1)} %get-tuple-element.38.refs_1_), channel_id=1, source_target_pairs={{0,24},{8,16},{16,8},{24,0},{1,25},{9,17},{17,9},{25,1},{2,26},{10... | collective-permute-start | bytes 12296 | tf_op jit(solution)/shard_map/ppermute | solution.py:452
  53.2 3.6 %collective-permute-start.15 = (f32[8,128]{1,0:T(8,128)S(1)}, f32[8,128]{1,0:T(8,128)S(1)}, u32[]{:S(2)}, u32[]{:S(2)}) collective-permute-start(f32[8,128]{1,0:T(8,128)S(1)} %get-tuple-element.38.refs_1_), channel_id=1, source_target_pairs={{0,16},{8,24},{16,0},{24,8},{1,17},{9,25},{17,1},{25,9},{2,18},{10... | collective-permute-start | bytes 12296 | tf_op jit(solution)/shard_map/ppermute | solution.py:452
  53.7 3.6 %collective-permute-start.14 = (f32[8,128]{1,0:T(8,128)S(1)}, f32[8,128]{1,0:T(8,128)S(1)}, u32[]{:S(2)}, u32[]{:S(2)}) collective-permute-start(f32[8,128]{1,0:T(8,128)S(1)} %get-tuple-element.38.refs_1_), channel_id=1, source_target_pairs={{0,8},{8,0},{16,24},{24,16},{1,9},{9,1},{17,25},{25,17},{2,10},{10... | collective-permute-start | bytes 12296 | tf_op jit(solution)/shard_map/ppermute | solution.py:452
